TPU v7x, 32 devices: a whole 2x2x4 slice. The times are simulated.
32 devices in a mesh: row: 4 (over x, core), real: 8 (over z, y).
Axes of the slice: x: 2, y: 2, z: 4, core: 2. Of those that a mesh axis runs over, the one named last changes fastest.
Arguments:
- right_sides: float32 [10, 4, 256, 4096], P(None, 'row', None, 'real'), may hold values from -8 to 8
- factor: float32 [10, 4, 256, 1024], P(None, 'row', None, 'real'), may hold values from -1 to 2, as said below
Outputs:
- updated: float32 [10, 4, 256, 4096], P(None, 'row', None, 'real')
Inputs may be any that keep to these rules, and one draw needn't show every extreme that they name: factor is lower triangular in global row and column order (entries with column above the global row are 0), with diagonal entries from 1 to 2.
All inputs are finite; a program needn't handle non-finite values.
Results may differ from a plain program's by a relative error of at most 0.0001.
Values sent between devices are 32-bit elements; how exact they have to be, the bound alone decides.
No kernel may reach another device: no remote copies, remote signals or barrier semaphores. Data moves between devices by JAX's collectives and lax.ppermute only.
A program may use at most 128 MiB of HBM per device.

v0:
```python
import jax
import jax.numpy as jnp
from jax import lax
from jax.sharding import PartitionSpec as P


def broadcast(value, axis, source):
    kept = jnp.where(lax.axis_index(axis) == source, value, 0).astype(value.dtype)
    return lax.psum(kept, axis)


def forward_chain(head_rows, current, position, row_count):
    span_cols = current.shape[0]
    solved = []
    for panel_index in range(row_count):
        columns = head_rows[:, panel_index * span_cols : (panel_index + 1) * span_cols]
        candidate = lax.linalg.triangular_solve(columns, current, left_side=True, lower=True)
        answer = broadcast(candidate, "row", panel_index)
        update = jnp.dot(columns, answer, precision=lax.Precision.HIGHEST)
        current = jnp.where(
            position > panel_index,
            current - update,
            jnp.where(position == panel_index, answer, current),
        )
        solved.append(answer)
    return (current, jnp.concatenate(solved, axis=0))


def body(right_sides, factor):
    position = lax.axis_index("row")
    row_count = lax.axis_size("row")
    working = right_sides[:, 0]
    gathered = lax.all_gather(factor, "real", axis=3, tiled=True)[:, 0]
    head_rows = gathered[0]
    first, window_solved = forward_chain(head_rows, working[0], position, row_count)
    trailing = working[1:] - jnp.einsum(
        "bpw,wc->bpc", gathered[1:], window_solved, precision=lax.Precision.HIGHEST
    )
    return jnp.concatenate([first[None], trailing], axis=0)[:, None]


def solution(mesh):
    placed = (P(None, "row", None, "real"), P(None, "row", None, "real"))
    return jax.shard_map(
        body, mesh=mesh, in_specs=placed, out_specs=P(None, "row", None, "real"), check_vma=False
    )
```

profile of v0, /device:TPU:0, one launch (start us, length us, event | category | flops | bytes accessed | tf_op | source)
XLA Modules:
  0.0 386.2 jit_solution(13455126686229483599)
XLA Ops:
  8.4 154.7 %all-gather.2.cloned.1.call-done = f32[10,1,256,1024]{3,2,0,1:T(8,128)} async-done(((f32[10,1,256,128]{3,2,0,1:T(8,128)}), f32[10,1,256,1024]{3,2,0,1:T(8,128)}) %all-gather.2.cloned.1.call-update) | async-done | bytes 10485776 | tf_op jit(solution)/shard_map/all_gather | solution.py:33
  164.6 3.9 %while.8 = (s32[]{:T(128)}, f32[256,256]{1,0:T(8,128)S(1)}, s32[2,2]{1,0:T(2,128)S(1)}, f32[2,128,128]{2,1,0:T(8,128)S(1)}, s32[]{:T(128)}) while((s32[]{:T(128)}, f32[256,256]{1,0:T(8,128)S(1)}, s32[2,2]{1,0:T(2,128)S(1)}, f32[2,128,128]{2,1,0:T(8,128)S(1)}, s32[]{:T(128)}) %tuple.66), condition=%wide.while_cond, body=%wide.while_body.sunk | while | flops 2 | bytes 131189 | solution.py:17
  168.5 19.7 %custom-call.6 = f32[2,128,128]{1,2,0:T(8,128)S(1)} custom-call(f32[2,128,128]{2,1,0:T(8,128)S(1)} %get-tuple-element.32), custom_call_target="InvertDiagBlocksLowerTriangular" | custom-call | tf_op jit(solution)/shard_map/triangular_solve/custom-call.1 | solution.py:17
  190.3 3.9 %while.9 = (s32[]{:T(128)}, f32[256,256]{1,0:T(8,128)S(1)}, s32[2,2]{1,0:T(2,128)S(1)}, f32[2,128,128]{2,1,0:T(8,128)S(1)}, s32[]{:T(128)}) while((s32[]{:T(128)}, f32[256,256]{1,0:T(8,128)S(1)}, s32[2,2]{1,0:T(2,128)S(1)}, f32[2,128,128]{2,1,0:T(8,128)S(1)}, s32[]{:T(128)}) %tuple.88), condition=%wide.while_cond.clone, body=%wide.while_body.clone.sunk | while | flops 2 | bytes 131189 | solution.py:17
  194.2 19.7 %custom-call.7 = f32[2,128,128]{1,2,0:T(8,128)S(1)} custom-call(f32[2,128,128]{2,1,0:T(8,128)S(1)} %get-tuple-element.33), custom_call_target="InvertDiagBlocksLowerTriangular" | custom-call | tf_op jit(solution)/shard_map/triangular_solve/custom-call.1 | solution.py:17
  213.9 8.1 %all-reduce.5.cloned.1.call-done = f32[256,512]{1,0:T(8,128)} async-done(((f32[256,512]{1,0:T(8,128)}), f32[256,512]{1,0:T(8,128)}) %all-reduce.5.cloned.1.call-update) | async-done | bytes 524304 | tf_op jit(solution)/shard_map/psum | solution.py:9
  221.9 2.0 fusion.8
  226.1 4.0 %while.10 = (s32[]{:T(128)}, f32[256,256]{1,0:T(8,128)S(1)}, s32[2,2]{1,0:T(2,128)S(1)}, f32[2,128,128]{2,1,0:T(8,128)S(1)}, s32[]{:T(128)}) while((s32[]{:T(128)}, f32[256,256]{1,0:T(8,128)S(1)}, s32[2,2]{1,0:T(2,128)S(1)}, f32[2,128,128]{2,1,0:T(8,128)S(1)}, s32[]{:T(128)}) %tuple.89), condition=%wide.while_cond.clone.1, body=%wide.while_body.clone.1.sunk | while | flops 2 | bytes 131189 | solution.py:17
  230.1 19.7 %custom-call.8 = f32[2,128,128]{1,2,0:T(8,128)S(1)} custom-call(f32[2,128,128]{2,1,0:T(8,128)S(1)} %get-tuple-element.34), custom_call_target="InvertDiagBlocksLowerTriangular" | custom-call | tf_op jit(solution)/shard_map/triangular_solve/custom-call.1 | solution.py:17
  249.8 9.7 %all-reduce.7.cloned.1.call-done = f32[256,512]{1,0:T(8,128)} async-done(((f32[256,512]{1,0:T(8,128)}), f32[256,512]{1,0:T(8,128)}) %all-reduce.7.cloned.1.call-update) | async-done | bytes 524304 | tf_op jit(solution)/shard_map/psum | solution.py:9
  259.5 1.9 fusion.10
  263.7 4.2 %while.11 = (s32[]{:T(128)}, f32[256,256]{1,0:T(8,128)S(1)}, s32[2,2]{1,0:T(2,128)S(1)}, f32[2,128,128]{2,1,0:T(8,128)S(1)}, s32[]{:T(128)}) while((s32[]{:T(128)}, f32[256,256]{1,0:T(8,128)S(1)}, s32[2,2]{1,0:T(2,128)S(1)}, f32[2,128,128]{2,1,0:T(8,128)S(1)}, s32[]{:T(128)}) %tuple.90), condition=%wide.while_cond.clone.2, body=%wide.while_body.clone.2.sunk | while | flops 2 | bytes 131189 | solution.py:17
  264.4 1.4 bitcast_dynamic-update-slice_fusion.11
  266.5 1.4 bitcast_dynamic-update-slice_fusion.11
  267.9 19.7 %custom-call.9 = f32[2,128,128]{1,2,0:T(8,128)S(1)} custom-call(f32[2,128,128]{2,1,0:T(8,128)S(1)} %get-tuple-element.35), custom_call_target="InvertDiagBlocksLowerTriangular" | custom-call | tf_op jit(solution)/shard_map/triangular_solve/custom-call.1 | solution.py:17
  287.6 9.6 %all-reduce.9.cloned.1.call-done = f32[256,512]{1,0:T(8,128)} async-done(((f32[256,512]{1,0:T(8,128)}), f32[256,512]{1,0:T(8,128)}) %all-reduce.9.cloned.1.call-update) | async-done | bytes 524304 | tf_op jit(solution)/shard_map/psum | solution.py:9
  297.2 1.9 fusion.12
  301.2 5.0 %slice.53 = f32[9,1,256,512]{3,2,1,0:T(8,128)} slice(f32[10,1,256,512]{3,2,1,0:T(8,128)} %param.4), slice={[1:10], [0:1], [0:256], [0:512]} | slice | bytes 9437184 | tf_op jit(solution)/shard_map/slice | solution.py:36
  306.3 6.2 %copy.18 = f32[9,1,256,512]{2,3,0,1:T(8,128)} copy(f32[9,1,256,512]{3,2,1,0:T(8,128)} %slice.53) | data formatting | bytes 9437184
  312.4 22.1 %all-reduce.11.cloned.1.call-done = f32[256,512]{1,0:T(8,128)} async-done(((f32[256,512]{1,0:T(8,128)}), f32[256,512]{1,0:T(8,128)}) %all-reduce.11.cloned.1.call-update) | async-done | bytes 524304 | tf_op jit(solution)/shard_map/psum | solution.py:9
  334.5 2.7 fusion.15
  338.5 32.4 %bitcast_subtract_fusion = f32[9,256,512]{1,2,0:T(8,128)S(1)} fusion(f32[9,1,256,512]{2,3,0,1:T(8,128)} %copy.18, f32[10,1,256,1024]{3,2,0,1:T(8,128)} %all-gather.2.cloned.1.call-done, f32[256,512]{1,0:T(8,128)} %all-reduce.11.cloned.1.call-done, f32[256,512]{1,0:T(8,128)S(1)} %copy-done.2, f32[256,512]{1,0:T(8,128)S(1)} %copy-done.1, ...), kind=kOutput, calls=%fused_computation.11 | convolution fusion | flops 14498267136 | bytes 20971520 | tf_op jit(solution)/shard_map/bpw,wc->bpc/dot_general | solution.py:36
  370.9 2.9 maximum_bitcast_fusion
  373.8 5.9 %copy.11 = f32[10,1,256,512]{3,2,1,0:T(8,128)} copy(f32[10,1,256,512]{2,3,0,1:T(8,128)} %maximum_bitcast_fusion) | data formatting | bytes 10485760 | tf_op jit(solution)/shard_map/broadcast_in_dim | solution.py:39
  (64 shorter events, 26.0 us)
Async XLA Ops:
  6.5 156.6 %all-gather.2.cloned.1.call-start = ((), (), s32[]{:S(2)}) async-start(), calls=%async_computation | async-start | bytes 11796480 | tf_op jit(solution)/shard_map/all_gather | solution.py:33
  7.3 214.7 %all-reduce.5.cloned.1.call-start = ((), (), s32[]{:S(2)}) async-start(), calls=%async_computation.1 | async-start | bytes 1048576 | tf_op jit(solution)/shard_map/psum | solution.py:9
  190.2 69.3 %all-reduce.7.cloned.1.call-start = ((), (), s32[]{:S(2)}) async-start(), calls=%async_computation.2 | async-start | bytes 1048576 | tf_op jit(solution)/shard_map/psum | solution.py:9
  226.1 71.2 %all-reduce.9.cloned.1.call-start = ((), (), s32[]{:S(2)}) async-start(), calls=%async_computation.3 | async-start | bytes 1048576 | tf_op jit(solution)/shard_map/psum | solution.py:9
  263.5 71.0 %all-reduce.11.cloned.1.call-start = ((), (), s32[]{:S(2)}) async-start(), calls=%async_computation.4 | async-start | bytes 1048576 | tf_op jit(solution)/shard_map/psum | solution.py:9
  306.3 32.2 %copy-start = (f32[256,512]{1,0:T(8,128)S(1)}, f32[256,512]{1,0:T(8,128)}, u32[]{:S(2)}) copy-start(f32[256,512]{1,0:T(8,128)} %all-reduce.5.cloned.1.call-done) | copy-start | bytes 1572868
  306.3 32.2 %copy-start.1 = (f32[256,512]{1,0:T(8,128)S(1)}, f32[256,512]{1,0:T(8,128)}, u32[]{:S(2)}) copy-start(f32[256,512]{1,0:T(8,128)} %all-reduce.7.cloned.1.call-done) | copy-start | bytes 1572868
  306.3 32.2 %copy-start.2 = (f32[256,512]{1,0:T(8,128)S(1)}, f32[256,512]{1,0:T(8,128)}, u32[]{:S(2)}) copy-start(f32[256,512]{1,0:T(8,128)} %all-reduce.9.cloned.1.call-done) | copy-start | bytes 1572868
Sparse Core Ops, SparseCore 0:
  9.4 153.6 all-gather.1
  190.4 31.5 all-reduce.4
  226.2 33.2 all-reduce.6
  263.6 33.5 all-reduce.8
  301.3 33.1 all-reduce.10
where the time goes:
time: 387 us; the launch traced here: 386 us
  waiting for transfers between devices  205 us (53%)
  other arithmetic  85 us (22%)
  matrix products  45.7 us (12%)
  local copies, waits for them, and re-layouts  36.5 us (9%)
  between operations  13.4 us (3%)
    all_gather x1, waiting for transfers between devices, body(): gathered = lax.all_gather(factor, 'real', axis=3, tiled=True)[:, 0]  155 us
    another operation x6, other arithmetic, forward_chain(): lax.linalg.triangular_solve(columns, current, left_side=True, lower=True)  78.8 us
    psum x4, waiting for transfers between devices, broadcast(): return lax.psum(kept, axis)  49.5 us
    dot_general x1, matrix products, body(): jnp.einsum('bpw,wc->bpc', gathered[1:], window_solved, precision=lax.Prec...  32.4 us
    another operation x28, local copies, waits for them, and re-layouts, forward_chain(): lax.linalg.triangular_solve(columns, current, left_side=True, lower=True)  15.7 us
    dot_general x4, matrix products, forward_chain(): update = jnp.dot(columns, answer, precision=lax.Precision.HIGHEST)  8.47 us
  transfers between devices with their start and end apart: 5, of which 5 were waited for; matrix products, arithmetic and copies ran while one was open for 22% of the time, Pallas kernels for 0%

commit v1 on v0

v1 whole, which is shorter than its diff:
```python
import functools

import jax
import jax.numpy as jnp
from jax import lax
from jax.experimental import pallas as pl
from jax.experimental.pallas import tpu as pltpu
from jax.sharding import PartitionSpec as P

F32, BF16 = jnp.float32, jnp.bfloat16
TILE, HALF, BASE = 128, 64, 16


def split(value):
    high = value.astype(BF16)
    return high, (value - high.astype(F32)).astype(BF16)


def product(a_high, a_low, b_high, b_low):
    dot = functools.partial(jnp.dot, preferred_element_type=F32)
    return dot(a_high, b_high) + (dot(a_high, b_low) + dot(a_low, b_high))


def exact(a, b):
    return jnp.dot(a, b, precision=lax.Precision.HIGHEST, preferred_element_type=F32)


def half_inverses(tiles):
    count = len(tiles)
    lane = lax.broadcasted_iota(jnp.int32, (BASE, TILE), 1)
    row = lax.broadcasted_iota(jnp.int32, (BASE, TILE), 0)
    packed = []
    for tile in tiles:
        kept = jnp.zeros((BASE, TILE), F32)
        for g in range(TILE // BASE):
            kept = jnp.where(lane // BASE == g, tile[g * BASE : (g + 1) * BASE], kept)
        packed.append(kept)
    packed = jnp.concatenate(packed, axis=0)
    k = lax.broadcasted_iota(jnp.int32, (TILE, TILE), 0)
    m = lax.broadcasted_iota(jnp.int32, (TILE, TILE), 1)
    x = jnp.broadcast_to((row == lane % BASE).astype(F32)[None], (count, BASE, TILE))
    for j in range(BASE):
        spread = (k == (m // BASE) * BASE + j).astype(F32)
        column = exact(packed, spread).reshape(count, BASE, TILE)
        solved = x[:, j : j + 1] / column[:, j : j + 1]
        x = jnp.where(row[None] == j, solved, x - column * solved)
    inverses = []
    for t, tile in enumerate(tiles):
        w = jnp.where(k // BASE == m // BASE, jnp.concatenate([x[t]] * (TILE // BASE), axis=0), 0.0)
        size = BASE
        while size < HALF:
            joined = (k // (2 * size) == m // (2 * size)) & (k // size != m // size)
            w = w - exact(exact(w, jnp.where(joined, tile, 0.0)), w)
            size *= 2
        inverses.append(w)
    return inverses


def solve_kernel(codes, place, head_refs, side_refs, y_ref, l_high, l_low, y_high, y_low):
    rows = head_refs[0].shape[-2]
    window = l_high.shape[0]
    position = place[0]
    diagonals = pl.ds(0, 1)
    for code, head, side in zip(codes, head_refs, side_refs):
        at = pl.ds(pl.multiple_of((position ^ code) * rows, rows), rows)
        high, low = split(head[...])
        l_high[at] = high
        l_low[at] = low
        y_ref[at] = side[...]
    tiles = []
    for t in range(window // TILE):
        at = slice(t * TILE, (t + 1) * TILE)
        tiles.append(l_high[at, at].astype(F32) + l_low[at, at].astype(F32))
    inverses = half_inverses(tiles)
    for t in range(window // TILE):
        begin = t * TILE
        value = y_ref[begin : begin + TILE]
        if t:
            value = value - product(
                l_high[begin : begin + TILE, :begin],
                l_low[begin : begin + TILE, :begin],
                y_high[:begin],
                y_low[:begin],
            )
        w = inverses[t]
        for h in range(TILE // HALF):
            part = value[h * HALF : (h + 1) * HALF]
            at = slice(begin + h * HALF, begin + (h + 1) * HALF)
            if h:
                inside = slice(begin, begin + h * HALF)
                part = part - product(
                    l_high[at, inside], l_low[at, inside], y_high[inside], y_low[inside]
                )
            inv = w[h * HALF : (h + 1) * HALF, h * HALF : (h + 1) * HALF]
            answer = product(*split(inv), *split(part))
            y_ref[at] = answer
            high, low = split(answer)
            y_high[at] = high
            y_low[at] = low


def solve(position, codes, heads, sides):
    window = heads[0].shape[-1]
    columns = sides[0].shape[-1]
    count = len(codes)

    def kernel(place, *refs):
        solve_kernel(codes, place, refs[:count], refs[count : 2 * count], *refs[2 * count :])

    whole = pl.BlockSpec(memory_space=pltpu.VMEM)
    return pl.pallas_call(
        kernel,
        out_shape=jax.ShapeDtypeStruct((window, columns), F32),
        in_specs=[pl.BlockSpec(memory_space=pltpu.SMEM)] + [whole] * (2 * count),
        out_specs=whole,
        scratch_shapes=[
            pltpu.VMEM((window, window), BF16),
            pltpu.VMEM((window, window), BF16),
            pltpu.VMEM((window, columns), BF16),
            pltpu.VMEM((window, columns), BF16),
        ],
        compiler_params=pltpu.CompilerParams(vmem_limit_bytes=40 << 20),
        cost_estimate=pl.CostEstimate(
            flops=6 * window * window * columns, bytes_accessed=4 * window * (window + 2 * columns), transcendentals=0
        ),
        name="solve",
    )(position, *heads, *sides)


def update(y, places, pieces, base, first, target=None, solved=None):
    blocks, rows, _ = pieces[0].shape
    columns = y.shape[1]
    widths = [piece.shape[-1] for piece in pieces]
    count = len(pieces)
    depth = sum(widths)
    in_place = target is base

    def kernel(place, *refs):
        y_ref, base_ref = refs[0], refs[1]
        piece_refs = refs[2 : 2 + count]
        out_ref, y_high, y_low = refs[-3:]

        @pl.when(pl.program_id(0) == 0)
        def _():
            begin = 0
            for n, width in enumerate(widths):
                high, low = split(y_ref[pl.ds(pl.multiple_of(place[n] * width, width), width)])
                y_high[begin : begin + width] = high
                y_low[begin : begin + width] = low
                begin += width

        wide = jnp.concatenate([ref[0] for ref in piece_refs], axis=1)
        out_ref[0, 0] = base_ref[0, 0] - product(*split(wide), y_high[...], y_low[...])

    block = pl.BlockSpec((1, 1, rows, columns), lambda i, *_: (i + first, 0, 0, 0))
    specs = [pl.BlockSpec((y.shape[0], columns), lambda i, *_: (0, 0)), block]
    specs += [pl.BlockSpec((1, rows, width), lambda i, *_: (i, 0, 0)) for width in widths]
    operands = [y, base, *pieces]
    aliases = {}
    if in_place:
        aliases = {2: 0}
    elif target is not None:
        specs.append(pl.BlockSpec(memory_space=pl.ANY))
        operands.append(target)
        aliases = {len(operands): 0}
    return pl.pallas_call(
        kernel,
        out_shape=jax.ShapeDtypeStruct(base.shape, F32),
        grid_spec=pltpu.PrefetchScalarGridSpec(
            num_scalar_prefetch=1,
            grid=(blocks,),
            in_specs=specs,
            out_specs=block,
            scratch_shapes=[pltpu.VMEM((depth, columns), BF16), pltpu.VMEM((depth, columns), BF16)],
        ),
        input_output_aliases=aliases,
        compiler_params=pltpu.CompilerParams(vmem_limit_bytes=40 << 20),
        cost_estimate=pl.CostEstimate(
            flops=6 * blocks * rows * depth * columns,
            bytes_accessed=4 * blocks * rows * (depth + 2 * columns),
            transcendentals=0,
        ),
        name="update",
    )(places, *operands)


def place_head(y, position, target):
    _, _, rows, columns = target.shape

    def kernel(place, y_ref, target_ref, out_ref):
        out_ref[0, 0] = y_ref[...]

    return pl.pallas_call(
        kernel,
        out_shape=jax.ShapeDtypeStruct(target.shape, F32),
        grid_spec=pltpu.PrefetchScalarGridSpec(
            num_scalar_prefetch=1,
            grid=(1,),
            in_specs=[
                pl.BlockSpec((rows, columns), lambda i, place: (place[0], 0)),
                pl.BlockSpec(memory_space=pl.ANY),
            ],
            out_specs=pl.BlockSpec((1, 1, rows, columns), lambda i, place: (0, 0, 0, 0)),
        ),
        input_output_aliases={2: 0},
        name="place_head",
    )(position, y, target)


def over_row(block, size):
    codes, held = [0], [block]
    bit = size // 2
    while bit:
        pairs = [(n, n ^ bit) for n in range(size)]
        held = held + [lax.ppermute(value, "row", pairs) for value in held]
        codes = codes + [code ^ bit for code in codes]
        bit //= 2
    return codes, held


def ring_of_pairs():
    lanes = 2
    at = lambda z, lane: z * lanes + lane
    each = lambda pairs: [(at(a, lane), at(b, lane)) for a, b in pairs for lane in range(lanes)]
    across = lambda zs: [(at(z, lane), at(z, 1 - lane)) for z in zs for lane in range(lanes)]
    return {
        "ends": each([(0, 1), (1, 0), (2, 3), (3, 2)]),
        "out": each([(1, 0), (2, 3)]),
        "middle": each([(1, 2), (2, 1)]),
        "across": across(range(4)),
        "across_outer": across((0, 3)),
    }


def body(right_sides, factor):
    row_count, real_count = lax.axis_size("row"), lax.axis_size("real")
    position = lax.axis_index("row")[None]
    mine = factor[:, 0]
    head = lax.all_gather(mine[0], "real", axis=1, tiled=True)
    codes, sides = over_row(right_sides[0, 0], row_count)
    codes, heads = over_row(head, row_count)
    y = solve(position, codes, heads, sides)
    if real_count != 8:
        rest = lax.all_gather(mine[1:], "real", axis=2, tiled=True)
        out = update(y, jnp.zeros((1,), jnp.int32), [rest], right_sides, 1)
        return place_head(y, position, out)

    ways = ring_of_pairs()
    move = lambda value, way: lax.ppermute(value, "real", ways[way])
    here = lax.axis_index("real")
    z, lane = here // 2, here % 2
    outer = (z == 0) | (z == 3)
    pick = lambda a, b: jnp.where(outer, a, b)
    trailing = mine.shape[0] - 1
    cut = 1 + (trailing + 1) // 2
    own = [mine[1:cut], mine[cut:]]
    ends, mid, side, ends2, mid2, side2, ends3, side3 = ([None, None] for _ in range(8))
    for k in range(2):
        ends[k] = move(own[k], "ends")
        mid[k] = move(own[k], "middle")
        side[k] = move(own[k], "across")
    for k in range(2):
        ends2[k] = move(pick(side[k], mid[k]), "ends")
        mid2[k] = move(ends[k], "middle")
        side2[k] = move(pick(ends[k], mid[k]), "across")
    for k in (1, 0):
        side3[k] = move(pick(ends2[k], mid2[k]), "across")
    for k in range(2):
        ends3[k] = move(mid2[k], "out")
    last = [move(ends3[0], "across_outer"), move(side3[1], "out")]

    mirror = 3 - z
    partner = jnp.where(z < 2, 1 - z, 5 - z)
    other = 3 - partner
    spot = lambda at, which: at * 2 + which
    places = jnp.stack(
        [
            here,
            spot(partner, lane),
            spot(z, 1 - lane),
            jnp.where(outer, spot(other, lane), spot(partner, 1 - lane)),
            jnp.where(outer, spot(partner, 1 - lane), spot(mirror, 1 - lane)),
            jnp.where(outer, here, spot(mirror, lane)),
            jnp.where(outer, spot(mirror, lane), here),
            jnp.where(outer, here, spot(other, lane)),
            jnp.where(outer, spot(other, 1 - lane), spot(other, 1 - lane)),
        ]
    ).astype(jnp.int32)
    out = None
    for k, first in ((0, 1), (1, cut)):
        pieces = [own[k], ends[k], side[k], ends2[k], side2[k], mid[k], ends3[k], mid2[k], side3[k]]
        out = update(y, places, pieces, right_sides, first, target=out)
    out = place_head(y, position, out)
    final = jnp.where(outer, spot(mirror, 1 - lane), here)[None].astype(jnp.int32)
    for k, first in ((1, cut), (0, 1)):
        out = update(y, final, [last[k]], out, first, target=out)
    return out


def solution(mesh):
    placed = (P(None, "row", None, "real"), P(None, "row", None, "real"))
    return jax.shard_map(
        body, mesh=mesh, in_specs=placed, out_specs=P(None, "row", None, "real"), check_vma=False
    )
```

time: 387 us -> 173 us (0.45)
  waiting for transfers between devices: 205 us -> 70.6 us
  other arithmetic: 85 us -> 3.98 us
  matrix products: 45.7 us -> 0 us
  Pallas kernels: 0 us -> 44 us
  starting transfers between devices: 0.34 us -> 27 us
  local copies, waits for them, and re-layouts: 36.5 us -> 10.5 us
    all_gather x1, waiting for transfers between devices: 155 us -> 37 us  [body(): head = lax.all_gather(mine[0], 'real', axis=1, tiled=True)]
    another operation x6 -> x0, other arithmetic: 78.8 us -> none  [forward_chain(): lax.linalg.triangular_solve(columns, current, left_side=True, lower=True)]
    psum x4 -> x0, waiting for transfers between devices: 49.5 us -> none  [broadcast(): return lax.psum(kept, axis)]
    pallas_call x0 -> x6, Pallas kernels: none -> 44 us  [the longest x4 26.4 us: update(): pl.pallas_call(kernel, out_shape=jax.ShapeDtypeStruct(base.shape, F32), g...]
    dot_general x5 -> x0, matrix products: 40.9 us -> none  [the longest x1 32.4 us: body(): jnp.einsum('bpw,wc->bpc', gathered[1:], window_solved, precision=lax.Prec...]
    ppermute x0 -> x24, waiting for transfers between devices: none -> 33.5 us  [the longest x18 27.8 us: body(): move = lambda value, way: lax.ppermute(value, 'real', ways[way])]
    ppermute x0 -> x24, starting transfers between devices: none -> 27 us  [the longest x18 22.3 us: body(): move = lambda value, way: lax.ppermute(value, 'real', ways[way])]
    another operation x28 -> x1, local copies, waits for them, and re-layouts: 15.7 us -> 0.08 us  [body(): jnp.stack([here, spot(partner, lane), spot(z, 1 - lane), jnp.where(outer,...]
  transfers between devices with their start and end apart: 5 -> 25, of which waited for: 5 -> 8; matrix products, arithmetic and copies ran while one was open for 22% -> 5% of each run, Pallas kernels for 0% -> 23%
where the time goes in v1:
time: 173 us; the launch traced here: 170 us
  waiting for transfers between devices  70.6 us (41%)
  Pallas kernels  44 us (25%)
  starting transfers between devices  27 us (16%)
  between operations  13.7 us (8%)
  local copies, waits for them, and re-layouts  10.5 us (6%)
  other arithmetic  3.98 us (2%)
    all_gather x1, waiting for transfers between devices, body(): head = lax.all_gather(mine[0], 'real', axis=1, tiled=True)  37 us
    ppermute x18, waiting for transfers between devices, body(): move = lambda value, way: lax.ppermute(value, 'real', ways[way])  27.8 us
    pallas_call x4, Pallas kernels, update(): pl.pallas_call(kernel, out_shape=jax.ShapeDtypeStruct(base.shape, F32), g...  26.4 us
    ppermute x18, starting transfers between devices, body(): move = lambda value, way: lax.ppermute(value, 'real', ways[way])  22.3 us
    pallas_call x1, Pallas kernels, solve(): pl.pallas_call(kernel, out_shape=jax.ShapeDtypeStruct((window, columns),...  15.5 us
    ppermute x6, waiting for transfers between devices, over_row(): held = held + [lax.ppermute(value, 'row', pairs) for value in held]  5.75 us
    unnamed x42, local copies, waits for them, and re-layouts  4.8 us
    ppermute x6, starting transfers between devices, over_row(): held = held + [lax.ppermute(value, 'row', pairs) for value in held]  4.75 us
  transfers between devices with their start and end apart: 25, of which 8 were waited for; matrix products, arithmetic and copies ran while one was open for 5% of the time, Pallas kernels for 23%

profile of v1, /device:TPU:0, one launch (start us, length us, event | category | flops | bytes accessed | tf_op | source)
XLA Modules:
  0.0 169.8 jit_solution(17714738911255529769)
XLA Ops:
  6.5 1.6 slice.19
  8.1 1.9 %slice_bitcast_fusion.2.refs_4_ = f32[256,512]{1,0:T(8,128)} fusion(f32[10,1,256,512]{3,2,1,0:T(8,128)} %refs_1_.3), kind=kLoop, calls=%fused_computation.2 | loop fusion | bytes 1048576 | tf_op jit(solution)/shard_map/squeeze | solution.py:240
  10.0 2.9 %collective-permute-start.3 = (f32[256,512]{1,0:T(8,128)}, f32[256,512]{1,0:T(8,128)}, u32[]{:S(2)}, u32[]{:S(2)}) collective-permute-start(f32[256,512]{1,0:T(8,128)} %slice_bitcast_fusion.2.refs_4_), channel_id=1, source_target_pairs={{0,16},{8,24},{16,0},{24,8},{1,17},{9,25},{17,1},{25,9},{2,18},{10... | collective-permute-start | bytes 1572872 | tf_op jit(solution)/shard_map/ppermute | solution.py:215
  14.1 1.6 collective-permute-start.14
  15.7 1.5 collective-permute-start.15
  17.9 37.0 %all-gather.3.cloned.1.call-done = f32[1,1,256,1024]{3,2,1,0:T(8,128)} async-done(((f32[1,1,256,128]{3,2,1,0:T(8,128)}), f32[1,1,256,1024]{3,2,1,0:T(8,128)}) %all-gather.3.cloned.1.call-update) | async-done | bytes 1048592 | tf_op jit(solution)/shard_map/all_gather | solution.py:239
  55.0 1.5 collective-permute-start
  58.6 1.5 collective-permute-start.7
  61.0 2.6 %collective-permute-start.17 = (f32[5,256,128]{2,1,0:T(8,128)S(1)}, f32[5,256,128]{2,1,0:T(8,128)S(1)}, u32[]{:S(2)}, u32[]{:S(2)}) collective-permute-start(f32[5,256,128]{2,1,0:T(8,128)S(1)} %get-tuple-element.6), channel_id=1, source_target_pairs={{0,2},{1,3},{2,0},{3,1},{4,6},{5,7},{6,4},{7,5},{8,10},{9,11},{10,... | collective-permute-start | bytes 1966088 | tf_op jit(solution)/shard_map/ppermute | solution.py:249
  63.6 8.9 %collective-permute-done.6.refs_3_ = f32[4,256,128]{2,1,0:T(8,128)} collective-permute-done((f32[4,256,128]{2,1,0:T(8,128)S(1)}, f32[4,256,128]{2,1,0:T(8,128)}, u32[]{:S(2)}, u32[]{:S(2)}) %collective-permute-start.6) | collective-permute-done | bytes 524320 | tf_op jit(solution)/shard_map/ppermute | solution.py:249
  73.8 5.7 %collective-permute-done.refs_1_ = f32[256,1024]{1,0:T(8,128)} collective-permute-done((f32[256,1024]{1,0:T(8,128)}, f32[256,1024]{1,0:T(8,128)}, u32[]{:S(2)}, u32[]{:S(2)}) %collective-permute-start) | collective-permute-done | bytes 1048608 | tf_op jit(solution)/shard_map/ppermute | solution.py:215
  79.5 2.1 %broadcast_select_fusion.4 = (f32[4,256,128]{2,1,0:T(8,128)}, f32[4,256,128]{2,1,0:T(8,128)S(1)}) fusion(f32[4,256,128]{2,1,0:T(8,128)} %collective-permute-done.6.refs_3_, f32[4,256,128]{2,1,0:T(8,128)S(1)} %collective-permute-done.8.refs_7_, pred[]{:T(512)S(6)} %or.3, f32[4,256,128]{2,1,0:T(8,128)} %collective-permute-done.7.refs_4_), kind=kLoop, calls=%fused_computation.7 | loop fusion | flops 262144 | bytes 2621441 | tf_op jit(solution)/shard_map/jit(_where)/select_n | solution.py:253
  82.5 4.0 %collective-permute-done.17.refs_5_ = f32[5,256,128]{2,1,0:T(8,128)S(1)} collective-permute-done((f32[5,256,128]{2,1,0:T(8,128)S(1)}, f32[5,256,128]{2,1,0:T(8,128)S(1)}, u32[]{:S(2)}, u32[]{:S(2)}) %collective-permute-start.17) | collective-permute-done | bytes 655392 | tf_op jit(solution)/shard_map/ppermute | solution.py:249
  88.9 8.4 %collective-permute-done.9.refs_5_ = f32[4,256,128]{2,1,0:T(8,128)S(1)} collective-permute-done((f32[4,256,128]{2,1,0:T(8,128)S(1)}, f32[4,256,128]{2,1,0:T(8,128)S(1)}, u32[]{:S(2)}, u32[]{:S(2)}) %collective-permute-start.9) | collective-permute-done | bytes 524320 | tf_op jit(solution)/shard_map/ppermute | solution.py:249
  97.3 1.6 collective-permute-start.21
  101.8 3.1 %collective-permute-done.18.refs_6_ = f32[5,256,128]{2,1,0:T(8,128)S(1)} collective-permute-done((f32[5,256,128]{2,1,0:T(8,128)S(1)}, f32[5,256,128]{2,1,0:T(8,128)S(1)}, u32[]{:S(2)}, u32[]{:S(2)}) %collective-permute-start.18) | collective-permute-done | bytes 655392 | tf_op jit(solution)/shard_map/ppermute | solution.py:249
  111.5 15.5 %solve.1.refs_0_.y_ref = f32[1024,512]{1,0:T(8,128)S(1)} custom-call(s32[1]{0:T(128)} %bitcast.1.place, f32[256,1024]{1,0:T(8,128)S(1)} %bitcast.23, f32[256,1024]{1,0:T(8,128)} %collective-permute-done.refs_1_, f32[256,1024]{1,0:T(8,128)} %collective-permute-done.1.refs_2_, f32[256,1024]{1,0:T(8,128)} %collective-permute-done.2.refs_3_, ...), custom_call_target="tpu_custom_call" | custom-call | flops 3221225472 | bytes 8388608 | tf_op jit(solution)/shard_map/solve/pallas_call | solution.py:111
  127.1 3.2 %collective-permute-done.13.refs_10_ = f32[4,256,128]{2,1,0:T(8,128)} collective-permute-done((f32[4,256,128]{2,1,0:T(8,128)}, f32[4,256,128]{2,1,0:T(8,128)}, u32[]{:S(2)}, u32[]{:S(2)}) %collective-permute-start.13) | collective-permute-done | bytes 524320 | tf_op jit(solution)/shard_map/ppermute | solution.py:249
  131.6 2.8 %collective-permute-start.23 = (f32[5,256,128]{2,1,0:T(8,128)}, f32[5,256,128]{2,1,0:T(8,128)}, u32[]{:S(2)}, u32[]{:S(2)}) collective-permute-start(f32[5,256,128]{2,1,0:T(8,128)} %collective-permute-done.20.refs_8_), channel_id=1, source_target_pairs={{0,1},{1,0},{6,7},{7,6},{8,9},{9,8},{14,15},{15,14},{16,17},{17,16... | collective-permute-start | bytes 1966088 | tf_op jit(solution)/shard_map/ppermute | solution.py:249
  134.5 8.8 %update.4.refs_11_ = f32[10,1,256,512]{3,2,1,0:T(8,128)} custom-call(s32[9]{0:T(128)S(1)} %stack.39.place, f32[1024,512]{1,0:T(8,128)S(1)} %solve.1.refs_0_.y_ref, f32[10,1,256,512]{3,2,1,0:T(8,128)S(1)} %bitcast.20, f32[5,256,128]{2,1,0:T(8,128)S(1)} %slice_bitcast_fusion.refs_2_, f32[5,256,128]{2,1,0:T(8,128)S(1)} %copy-done.3, ...), custom_call_target="tpu_custom_call" | custom-call | flops 4529848320 | bytes 11141120 | tf_op jit(solution)/shard_map/update/pallas_call | solution.py:166
  143.3 7.6 %update.5.target_ref = f32[10,1,256,512]{3,2,1,0:T(8,128)} custom-call(s32[9]{0:T(128)S(1)} %stack.39.place, f32[1024,512]{1,0:T(8,128)S(1)} %solve.1.refs_0_.y_ref, f32[10,1,256,512]{3,2,1,0:T(8,128)S(1)} %bitcast.20, f32[4,256,128]{2,1,0:T(8,128)S(1)} %slice_bitcast_fusion.1.refs_2_, ...), custom_call_target="tpu_custom_call", output_to_operand_aliasing={{}: (12, {})} | custom-call | flops 3623878656 | bytes 8912896 | tf_op jit(solution)/shard_map/update/pallas_call | solution.py:166
  150.9 2.0 %place_head.1.refs_1_ = f32[10,1,256,512]{3,2,1,0:T(8,128)} custom-call(s32[1]{0:T(128)} %bitcast.1.place, f32[1024,512]{1,0:T(8,128)} %copy-done, f32[10,1,256,512]{3,2,1,0:T(8,128)} %update.5.target_ref), custom_call_target="tpu_custom_call", output_to_operand_aliasing={{}: (2, {})} | custom-call | tf_op jit(solution)/shard_map/place_head/pallas_call | solution.py:193
  153.0 4.5 %update.6.refs_1_ = f32[10,1,256,512]{3,2,1,0:T(8,128)} custom-call(s32[1]{0:T(128)} %bitcast.place, f32[1024,512]{1,0:T(8,128)S(1)} %copy-done.1, f32[10,1,256,512]{3,2,1,0:T(8,128)} %place_head.1.refs_1_, f32[4,256,128]{2,1,0:T(8,128)} %collective-permute-done.22.refs_2_), custom_call_target="tpu_custom_call", output_to_operand_aliasing={{}: (2, {})} | custom-call | flops 402653184 | bytes 4718592 | tf_op jit(solution)/shard_map/update/pallas_call | solution.py:166
  157.5 5.5 %update.7 = f32[10,1,256,512]{3,2,1,0:T(8,128)} custom-call(s32[1]{0:T(128)} %bitcast.place, f32[1024,512]{1,0:T(8,128)S(1)} %copy-done.1, f32[10,1,256,512]{3,2,1,0:T(8,128)} %update.6.refs_1_, f32[5,256,128]{2,1,0:T(8,128)} %collective-permute-done.23.refs_2_), custom_call_target="tpu_custom_call", output_to_operand_aliasing={{}: (2, {})} | custom-call | flops 503316480 | bytes 5898240 | tf_op jit(solution)/shard_map/update/pallas_call | solution.py:166
  (85 shorter events, 20.1 us)
Async XLA Ops:
  6.5 48.4 %all-gather.3.cloned.1.call-start = ((), (), s32[]{:S(2)}) async-start(), calls=%async_computation | async-start | bytes 1179648 | tf_op jit(solution)/shard_map/all_gather | solution.py:239
  10.0 46.5 %collective-permute-start.3 = (f32[256,512]{1,0:T(8,128)}, f32[256,512]{1,0:T(8,128)}, u32[]{:S(2)}, u32[]{:S(2)}) collective-permute-start(f32[256,512]{1,0:T(8,128)} %slice_bitcast_fusion.2.refs_4_), channel_id=1, source_target_pairs={{0,16},{8,24},{16,0},{24,8},{1,17},{9,25},{17,1},{25,9},{2,18},{10... | collective-permute-start | bytes 1572872 | tf_op jit(solution)/shard_map/ppermute | solution.py:215
  14.1 43.5 %collective-permute-start.14 = (f32[5,256,128]{2,1,0:T(8,128)S(1)}, f32[5,256,128]{2,1,0:T(8,128)S(1)}, u32[]{:S(2)}, u32[]{:S(2)}) collective-permute-start(f32[5,256,128]{2,1,0:T(8,128)S(1)} %slice_bitcast_fusion.refs_2_), channel_id=1, source_target_pairs={{0,2},{1,3},{2,0},{3,1},{4,6},{5,7},{6,4},{7,5},{8,10},{9,11},{10,... | collective-permute-start | bytes 1966088 | tf_op jit(solution)/shard_map/ppermute | solution.py:249
  15.7 42.9 %collective-permute-start.15 = (f32[5,256,128]{2,1,0:T(8,128)S(1)}, f32[5,256,128]{2,1,0:T(8,128)S(1)}, u32[]{:S(2)}, u32[]{:S(2)}) collective-permute-start(f32[5,256,128]{2,1,0:T(8,128)S(1)} %slice_bitcast_fusion.refs_2_), channel_id=1, source_target_pairs={{0,1},{1,0},{2,3},{3,2},{4,5},{5,4},{6,7},{7,6},{8,9},{9,8},{10,11... | collective-permute-start | bytes 1966088 | tf_op jit(solution)/shard_map/ppermute | solution.py:249
  17.2 42.9 %collective-permute-start.16 = (f32[5,256,128]{2,1,0:T(8,128)S(1)}, f32[5,256,128]{2,1,0:T(8,128)S(1)}, u32[]{:S(2)}, u32[]{:S(2)}) collective-permute-start(f32[5,256,128]{2,1,0:T(8,128)S(1)} %slice_bitcast_fusion.refs_2_), channel_id=1, source_target_pairs={{2,4},{3,5},{4,2},{5,3},{10,12},{11,13},{12,10},{13,11},{18,20},{1... | collective-permute-start | bytes 1966088 | tf_op jit(solution)/shard_map/ppermute | solution.py:249
  55.0 24.6 %collective-permute-start = (f32[256,1024]{1,0:T(8,128)}, f32[256,1024]{1,0:T(8,128)}, u32[]{:S(2)}, u32[]{:S(2)}) collective-permute-start(f32[256,1024]{1,0:T(8,128)} %bitcast.21), channel_id=1, source_target_pairs={{0,16},{8,24},{16,0},{24,8},{1,17},{9,25},{17,1},{25,9},{2,18},{10... | collective-permute-start | bytes 3145736 | tf_op jit(solution)/shard_map/ppermute | solution.py:215
  57.6 14.9 %collective-permute-start.6 = (f32[4,256,128]{2,1,0:T(8,128)S(1)}, f32[4,256,128]{2,1,0:T(8,128)}, u32[]{:S(2)}, u32[]{:S(2)}) collective-permute-start(f32[4,256,128]{2,1,0:T(8,128)S(1)} %slice_bitcast_fusion.1.refs_2_), channel_id=1, source_target_pairs={{0,2},{1,3},{2,0},{3,1},{4,6},{5,7},{6,4},{7,5},{8,10},{9,11},{10,... | collective-permute-start | bytes 1572872 | tf_op jit(solution)/shard_map/ppermute | solution.py:249
  58.6 14.2 %collective-permute-start.7 = (f32[4,256,128]{2,1,0:T(8,128)S(1)}, f32[4,256,128]{2,1,0:T(8,128)}, u32[]{:S(2)}, u32[]{:S(2)}) collective-permute-start(f32[4,256,128]{2,1,0:T(8,128)S(1)} %slice_bitcast_fusion.1.refs_2_), channel_id=1, source_target_pairs={{0,1},{1,0},{2,3},{3,2},{4,5},{5,4},{6,7},{7,6},{8,9},{9,8},{10,11... | collective-permute-start | bytes 1572872 | tf_op jit(solution)/shard_map/ppermute | solution.py:249
  60.2 13.3 %collective-permute-start.8 = (f32[4,256,128]{2,1,0:T(8,128)S(1)}, f32[4,256,128]{2,1,0:T(8,128)S(1)}, u32[]{:S(2)}, u32[]{:S(2)}) collective-permute-start(f32[4,256,128]{2,1,0:T(8,128)S(1)} %slice_bitcast_fusion.1.refs_2_), channel_id=1, source_target_pairs={{2,4},{3,5},{4,2},{5,3},{10,12},{11,13},{12,10},{13,11},{18,20},{1... | collective-permute-start | bytes 1572872 | tf_op jit(solution)/shard_map/ppermute | solution.py:249
  61.0 25.4 %collective-permute-start.17 = (f32[5,256,128]{2,1,0:T(8,128)S(1)}, f32[5,256,128]{2,1,0:T(8,128)S(1)}, u32[]{:S(2)}, u32[]{:S(2)}) collective-permute-start(f32[5,256,128]{2,1,0:T(8,128)S(1)} %get-tuple-element.6), channel_id=1, source_target_pairs={{0,2},{1,3},{2,0},{3,1},{4,6},{5,7},{6,4},{7,5},{8,10},{9,11},{10,... | collective-permute-start | bytes 1966088 | tf_op jit(solution)/shard_map/ppermute | solution.py:249
  72.5 9.2 %collective-permute-start.5 = (f32[256,512]{1,0:T(8,128)}, f32[256,512]{1,0:T(8,128)S(1)}, u32[]{:S(2)}, u32[]{:S(2)}) collective-permute-start(f32[256,512]{1,0:T(8,128)} %collective-permute-done.3.refs_5_), channel_id=1, source_target_pairs={{0,8},{8,0},{16,24},{24,16},{1,9},{9,1},{17,25},{25,17},{2,10},{10... | collective-permute-start | bytes 1572872 | tf_op jit(solution)/shard_map/ppermute | solution.py:215
  72.8 14.3 %collective-permute-start.19 = (f32[5,256,128]{2,1,0:T(8,128)S(1)}, f32[5,256,128]{2,1,0:T(8,128)S(1)}, u32[]{:S(2)}, u32[]{:S(2)}) collective-permute-start(f32[5,256,128]{2,1,0:T(8,128)S(1)} %collective-permute-done.14.refs_3_), channel_id=1, source_target_pairs={{2,4},{3,5},{4,2},{5,3},{10,12},{11,13},{12,10},{13,11},{18,20},{1... | collective-permute-start | bytes 1966088 | tf_op jit(solution)/shard_map/ppermute | solution.py:249
  73.5 33.1 %collective-permute-start.1 = (f32[256,1024]{1,0:T(8,128)}, f32[256,1024]{1,0:T(8,128)}, u32[]{:S(2)}, u32[]{:S(2)}) collective-permute-start(f32[256,1024]{1,0:T(8,128)} %bitcast.22), channel_id=1, source_target_pairs={{0,8},{8,0},{16,24},{24,16},{1,9},{9,1},{17,25},{25,17},{2,10},{10... | collective-permute-start | bytes 3145736 | tf_op jit(solution)/shard_map/ppermute | solution.py:215
  79.5 28.4 %collective-permute-start.2 = (f32[256,1024]{1,0:T(8,128)}, f32[256,1024]{1,0:T(8,128)}, u32[]{:S(2)}, u32[]{:S(2)}) collective-permute-start(f32[256,1024]{1,0:T(8,128)} %collective-permute-done.refs_1_), channel_id=1, source_target_pairs={{0,8},{8,0},{16,24},{24,16},{1,9},{9,1},{17,25},{25,17},{2,10},{10... | collective-permute-start | bytes 3145736 | tf_op jit(solution)/shard_map/ppermute | solution.py:215
  82.5 14.8 %collective-permute-start.9 = (f32[4,256,128]{2,1,0:T(8,128)S(1)}, f32[4,256,128]{2,1,0:T(8,128)S(1)}, u32[]{:S(2)}, u32[]{:S(2)}) collective-permute-start(f32[4,256,128]{2,1,0:T(8,128)S(1)} %get-tuple-element.8), channel_id=1, source_target_pairs={{0,2},{1,3},{2,0},{3,1},{4,6},{5,7},{6,4},{7,5},{8,10},{9,11},{10,... | collective-permute-start | bytes 1572872 | tf_op jit(solution)/shard_map/ppermute | solution.py:249
  86.4 12.4 %collective-permute-start.11 = (f32[4,256,128]{2,1,0:T(8,128)}, f32[4,256,128]{2,1,0:T(8,128)S(1)}, u32[]{:S(2)}, u32[]{:S(2)}) collective-permute-start(f32[4,256,128]{2,1,0:T(8,128)} %collective-permute-done.6.refs_3_), channel_id=1, source_target_pairs={{2,4},{3,5},{4,2},{5,3},{10,12},{11,13},{12,10},{13,11},{18,20},{1... | collective-permute-start | bytes 1572872 | tf_op jit(solution)/shard_map/ppermute | solution.py:249
  87.1 17.7 %collective-permute-start.18 = (f32[5,256,128]{2,1,0:T(8,128)S(1)}, f32[5,256,128]{2,1,0:T(8,128)S(1)}, u32[]{:S(2)}, u32[]{:S(2)}) collective-permute-start(f32[5,256,128]{2,1,0:T(8,128)S(1)} %get-tuple-element.5), channel_id=1, source_target_pairs={{0,1},{1,0},{2,3},{3,2},{4,5},{5,4},{6,7},{7,6},{8,9},{9,8},{10,11... | collective-permute-start | bytes 1966088 | tf_op jit(solution)/shard_map/ppermute | solution.py:249
  97.3 37.1 %collective-permute-start.21 = (f32[5,256,128]{2,1,0:T(8,128)}, f32[5,256,128]{2,1,0:T(8,128)}, u32[]{:S(2)}, u32[]{:S(2)}) collective-permute-start(f32[5,256,128]{2,1,0:T(8,128)} %broadcast_select_fusion), channel_id=1, source_target_pairs={{0,1},{1,0},{2,3},{3,2},{4,5},{5,4},{6,7},{7,6},{8,9},{9,8},{10,11... | collective-permute-start | bytes 1966088 | tf_op jit(solution)/shard_map/ppermute | solution.py:249
  98.9 32.7 %collective-permute-start.20 = (f32[5,256,128]{2,1,0:T(8,128)S(1)}, f32[5,256,128]{2,1,0:T(8,128)}, u32[]{:S(2)}, u32[]{:S(2)}) collective-permute-start(f32[5,256,128]{2,1,0:T(8,128)S(1)} %collective-permute-done.19.refs_9_), channel_id=1, source_target_pairs={{2,0},{3,1},{4,6},{5,7},{10,8},{11,9},{12,14},{13,15},{18,16},{19,... | collective-permute-start | bytes 1966088 | tf_op jit(solution)/shard_map/ppermute | solution.py:249
  105.8 24.5 %collective-permute-start.13 = (f32[4,256,128]{2,1,0:T(8,128)}, f32[4,256,128]{2,1,0:T(8,128)}, u32[]{:S(2)}, u32[]{:S(2)}) collective-permute-start(f32[4,256,128]{2,1,0:T(8,128)} %broadcast_select_fusion.3), channel_id=1, source_target_pairs={{0,1},{1,0},{2,3},{3,2},{4,5},{5,4},{6,7},{7,6},{8,9},{9,8},{10,11... | collective-permute-start | bytes 1572872 | tf_op jit(solution)/shard_map/ppermute | solution.py:249
  106.6 36.7 %collective-permute-start.10 = (f32[4,256,128]{2,1,0:T(8,128)}, f32[4,256,128]{2,1,0:T(8,128)S(1)}, u32[]{:S(2)}, u32[]{:S(2)}) collective-permute-start(f32[4,256,128]{2,1,0:T(8,128)} %get-tuple-element.7), channel_id=1, source_target_pairs={{0,1},{1,0},{2,3},{3,2},{4,5},{5,4},{6,7},{7,6},{8,9},{9,8},{10,11... | collective-permute-start | bytes 1572872 | tf_op jit(solution)/shard_map/ppermute | solution.py:249
  107.9 35.3 %collective-permute-start.12 = (f32[4,256,128]{2,1,0:T(8,128)}, f32[4,256,128]{2,1,0:T(8,128)S(1)}, u32[]{:S(2)}, u32[]{:S(2)}) collective-permute-start(f32[4,256,128]{2,1,0:T(8,128)} %copy-done.10), channel_id=1, source_target_pairs={{2,0},{3,1},{4,6},{5,7},{10,8},{11,9},{12,14},{13,15},{18,16},{19,... | collective-permute-start | bytes 1572872 | tf_op jit(solution)/shard_map/ppermute | solution.py:249
  130.3 22.7 %collective-permute-start.22 = (f32[4,256,128]{2,1,0:T(8,128)}, f32[4,256,128]{2,1,0:T(8,128)}, u32[]{:S(2)}, u32[]{:S(2)}) collective-permute-start(f32[4,256,128]{2,1,0:T(8,128)} %collective-permute-done.13.refs_10_), channel_id=1, source_target_pairs={{2,0},{3,1},{4,6},{5,7},{10,8},{11,9},{12,14},{13,15},{18,16},{19,... | collective-permute-start | bytes 1572872 | tf_op jit(solution)/shard_map/ppermute | solution.py:249
  131.6 25.9 %collective-permute-start.23 = (f32[5,256,128]{2,1,0:T(8,128)}, f32[5,256,128]{2,1,0:T(8,128)}, u32[]{:S(2)}, u32[]{:S(2)}) collective-permute-start(f32[5,256,128]{2,1,0:T(8,128)} %collective-permute-done.20.refs_8_), channel_id=1, source_target_pairs={{0,1},{1,0},{6,7},{7,6},{8,9},{9,8},{14,15},{15,14},{16,17},{17,16... | collective-permute-start | bytes 1966088 | tf_op jit(solution)/shard_map/ppermute | solution.py:249
  (22 other events, 314.4 us)
Sparse Core Ops, SparseCore 0:
  9.4 45.5 all-gather.2

commit v2 on v1

v2 whole, which is shorter than its diff:
```python
import functools

import jax
import jax.numpy as jnp
from jax import lax
from jax.experimental import pallas as pl
from jax.experimental.pallas import tpu as pltpu
from jax.sharding import PartitionSpec as P

F32, BF16 = jnp.float32, jnp.bfloat16
TILE, HALF, BASE = 128, 64, 16


def split(value):
    high = value.astype(BF16)
    return high, (value - high.astype(F32)).astype(BF16)


def product(a_high, a_low, b_high, b_low):
    dot = functools.partial(jnp.dot, preferred_element_type=F32)
    return dot(a_high, b_high) + (dot(a_high, b_low) + dot(a_low, b_high))


def exact(a, b):
    return jnp.dot(a, b, precision=lax.Precision.HIGHEST, preferred_element_type=F32)


def half_inverses(tiles):
    count = len(tiles)
    lane = lax.broadcasted_iota(jnp.int32, (BASE, TILE), 1)
    row = lax.broadcasted_iota(jnp.int32, (BASE, TILE), 0)
    packed = []
    for tile in tiles:
        kept = jnp.zeros((BASE, TILE), F32)
        for g in range(TILE // BASE):
            kept = jnp.where(lane // BASE == g, tile[g * BASE : (g + 1) * BASE], kept)
        packed.append(kept)
    packed = jnp.concatenate(packed, axis=0)
    k = lax.broadcasted_iota(jnp.int32, (TILE, TILE), 0)
    m = lax.broadcasted_iota(jnp.int32, (TILE, TILE), 1)
    x = jnp.broadcast_to((row == lane % BASE).astype(F32)[None], (count, BASE, TILE))
    for j in range(BASE):
        spread = (k == (m // BASE) * BASE + j).astype(F32)
        column = exact(packed, spread).reshape(count, BASE, TILE)
        solved = x[:, j : j + 1] / column[:, j : j + 1]
        x = jnp.where(row[None] == j, solved, x - column * solved)
    inverses = []
    for t, tile in enumerate(tiles):
        w = jnp.where(k // BASE == m // BASE, jnp.concatenate([x[t]] * (TILE // BASE), axis=0), 0.0)
        size = BASE
        while size < HALF:
            joined = (k // (2 * size) == m // (2 * size)) & (k // size != m // size)
            w = w - exact(exact(w, jnp.where(joined, tile, 0.0)), w)
            size *= 2
        inverses.append(w)
    return inverses


def solve_kernel(codes, counts, place, head_refs, side_refs, y_ref, l_high, l_low, y_high, y_low, landing, head_sems, side_sems):
    rows, width = head_refs[0].shape[-2:]
    window = l_high.shape[0]
    per_row = len(head_refs) // len(codes)
    head_copies, side_copies = [], []
    for c, code in enumerate(codes):
        at = pl.ds(pl.multiple_of((place[0] ^ code) * rows, rows), rows)
        begin = c * sum(counts)
        for p in range(per_row):
            n = c * per_row + p
            into = landing.at[begin : begin + counts[p]]
            head_copies.append(pltpu.make_async_copy(head_refs[n], into, head_sems.at[n]))
            begin += counts[p]
        side_copies.append(pltpu.make_async_copy(side_refs[c], y_ref.at[at], side_sems.at[c]))
    for copy in head_copies + side_copies:
        copy.start()
    for c, code in enumerate(codes):
        at = pl.ds(pl.multiple_of((place[0] ^ code) * rows, rows), rows)
        n = c * sum(counts)
        for p in range(per_row):
            head_copies[c * per_row + p].wait()
            for k in range(counts[p]):
                across = pl.ds(pl.multiple_of(place[1 + n] * width, width), width)
                high, low = split(landing[n])
                l_high[at, across] = high
                l_low[at, across] = low
                n += 1
    for copy in side_copies:
        copy.wait()
    tiles = []
    for t in range(window // TILE):
        at = slice(t * TILE, (t + 1) * TILE)
        tiles.append(l_high[at, at].astype(F32) + l_low[at, at].astype(F32))
    inverses = half_inverses(tiles)
    for t in range(window // TILE):
        begin = t * TILE
        value = y_ref[begin : begin + TILE]
        if t:
            value = value - product(
                l_high[begin : begin + TILE, :begin],
                l_low[begin : begin + TILE, :begin],
                y_high[:begin],
                y_low[:begin],
            )
        w = inverses[t]
        for h in range(TILE // HALF):
            part = value[h * HALF : (h + 1) * HALF]
            at = slice(begin + h * HALF, begin + (h + 1) * HALF)
            if h:
                inside = slice(begin, begin + h * HALF)
                part = part - product(
                    l_high[at, inside], l_low[at, inside], y_high[inside], y_low[inside]
                )
            inv = w[h * HALF : (h + 1) * HALF, h * HALF : (h + 1) * HALF]
            answer = product(*split(inv), *split(part))
            y_ref[at] = answer
            high, low = split(answer)
            y_high[at] = high
            y_low[at] = low


def solve(position, codes, heads, owners, sides):
    counts = [part.shape[0] for part in heads[0]]
    window = sum(counts) * heads[0][0].shape[-1]
    columns = sides[0].shape[-1]
    flat = [part for parts in heads for part in parts]
    total = len(flat)
    place = jnp.concatenate([position] + [owners] * len(codes))

    def kernel(place, *refs):
        head_refs, side_refs = refs[:total], refs[total : total + len(codes)]
        solve_kernel(codes, counts, place, head_refs, side_refs, *refs[total + len(codes) :])

    return pl.pallas_call(
        kernel,
        out_shape=jax.ShapeDtypeStruct((window, columns), F32),
        in_specs=[pl.BlockSpec(memory_space=pltpu.SMEM)] + [pl.BlockSpec(memory_space=pl.ANY)] * (total + len(codes)),
        out_specs=pl.BlockSpec(memory_space=pltpu.VMEM),
        scratch_shapes=[
            pltpu.VMEM((window, window), BF16),
            pltpu.VMEM((window, window), BF16),
            pltpu.VMEM((window, columns), BF16),
            pltpu.VMEM((window, columns), BF16),
            pltpu.VMEM((len(codes) * sum(counts), *flat[0].shape[1:]), F32),
            pltpu.SemaphoreType.DMA((total,)),
            pltpu.SemaphoreType.DMA((len(codes),)),
        ],
        compiler_params=pltpu.CompilerParams(vmem_limit_bytes=48 << 20),
        cost_estimate=pl.CostEstimate(
            flops=30 * window * window * columns, bytes_accessed=4 * window * (window + 2 * columns), transcendentals=0
        ),
        name="solve",
    )(place, *flat, *sides)


def update(y, position, places, pieces, base, first, target=None, with_head=False):
    flat = [part for piece in pieces for part in piece]
    blocks, rows, _ = flat[0].shape
    columns = y.shape[1]
    widths = [piece[0].shape[-1] for piece in pieces]
    count = len(flat)
    depth = sum(widths)
    skip = int(with_head)

    def kernel(place, *refs):
        y_ref, base_ref = refs[0], refs[1]
        piece_refs = list(refs[2 : 2 + count])
        out_ref, y_high, y_low = refs[-3:]

        @pl.when(pl.program_id(0) == 0)
        def _():
            begin = 0
            for n, width in enumerate(widths):
                high, low = split(y_ref[pl.ds(pl.multiple_of(place[n + 1] * width, width), width)])
                y_high[begin : begin + width] = high
                y_low[begin : begin + width] = low
                begin += width

        def below():
            columns_of = iter(piece_refs)
            wide = [sum(next(columns_of)[0] for _ in piece) for piece in pieces]
            high, low = split(jnp.concatenate(wide, axis=1))
            out_ref[0, 0] = base_ref[0, 0] - product(high, low, y_high[...], y_low[...])

        if skip:

            @pl.when(pl.program_id(0) == 0)
            def _():
                out_ref[0, 0] = y_ref[pl.ds(pl.multiple_of(place[0] * rows, rows), rows)]

            pl.when(pl.program_id(0) > 0)(below)
        else:
            below()

    block = pl.BlockSpec((1, 1, rows, columns), lambda i, *_: (i + first - skip, 0, 0, 0))
    specs = [pl.BlockSpec((y.shape[0], columns), lambda i, *_: (0, 0)), block]
    specs += [pl.BlockSpec((1, rows, part.shape[-1]), lambda i, *_: (jnp.maximum(i - skip, 0), 0, 0)) for part in flat]
    operands = [y, base, *flat]
    aliases = {}
    if target is not None:
        specs.append(pl.BlockSpec(memory_space=pl.ANY))
        operands.append(target)
        aliases = {len(operands): 0}
    return pl.pallas_call(
        kernel,
        out_shape=jax.ShapeDtypeStruct(base.shape, F32),
        grid_spec=pltpu.PrefetchScalarGridSpec(
            num_scalar_prefetch=1,
            grid=(blocks + skip,),
            in_specs=specs,
            out_specs=block,
            scratch_shapes=[pltpu.VMEM((depth, columns), BF16), pltpu.VMEM((depth, columns), BF16)],
        ),
        input_output_aliases=aliases,
        compiler_params=pltpu.CompilerParams(vmem_limit_bytes=48 << 20),
        cost_estimate=pl.CostEstimate(
            flops=6 * blocks * rows * depth * columns,
            bytes_accessed=4 * blocks * rows * (depth + 2 * columns),
            transcendentals=0,
        ),
        name="update",
    )(jnp.concatenate([position, places]), *operands)


def finish(y, place, piece, out, first):
    offsets = [offset for _, offset in piece]
    piece = [part for part, _ in piece]
    blocks = min(part.shape[0] for part in piece)
    _, rows, width = piece[0].shape
    columns = y.shape[1]
    count = len(piece)

    def kernel(place, y_ref, *refs):
        y_high, y_low = split(y_ref[...])
        high, low = split(sum(ref[0] for ref in refs[:count]))
        wide = jnp.concatenate([high, low, high], axis=1)
        stack = jnp.concatenate([y_high, y_high, y_low], axis=0)
        refs[-1][0, 0] = refs[count][0, 0] - jnp.dot(wide, stack, preferred_element_type=F32)

    block = pl.BlockSpec((1, 1, rows, columns), lambda i, *_: (i + first, 0, 0, 0))
    return pl.pallas_call(
        kernel,
        out_shape=jax.ShapeDtypeStruct(out.shape, F32),
        grid_spec=pltpu.PrefetchScalarGridSpec(
            num_scalar_prefetch=1,
            grid=(blocks,),
            in_specs=[pl.BlockSpec((width, columns), lambda i, place: (place[0], 0))]
            + [pl.BlockSpec((1, rows, width), lambda i, *_, offset=offset: (i + offset, 0, 0)) for offset in offsets]
            + [block],
            out_specs=block,
        ),
        input_output_aliases={2 + count: 0},
        compiler_params=pltpu.CompilerParams(vmem_limit_bytes=48 << 20),
        cost_estimate=pl.CostEstimate(
            flops=6 * blocks * rows * width * columns,
            bytes_accessed=4 * blocks * rows * (width + 2 * columns),
            transcendentals=0,
        ),
        name="finish",
    )(place, y, *piece, out)


def over_row(block, size):
    codes, held = [0], [block]
    bit = size // 2
    while bit:
        pairs = [(n, n ^ bit) for n in range(size)]
        held = held + [lax.ppermute(value, "row", pairs) for value in held]
        codes = codes + [code ^ bit for code in codes]
        bit //= 2
    return codes, held


def after(value, *others):
    return lax.optimization_barrier((value, *others))[0]


def body(right_sides, factor):
    row_count, real_count = lax.axis_size("row"), lax.axis_size("real")
    position = lax.axis_index("row")[None]
    mine = factor[:, 0]
    if real_count != 8:
        codes, sides = over_row(right_sides[0, 0], row_count)
        head = lax.all_gather(mine[0], "real", axis=1, tiled=True)
        codes, heads = over_row(head[None], row_count)
        y = solve(position, codes, [[part] for part in heads], jnp.zeros((1,), jnp.int32), sides)
        rest = lax.all_gather(mine[1:], "real", axis=2, tiled=True)
        return update(y, position, jnp.zeros((1,), jnp.int32), [[rest]], right_sides, 1, with_head=True)

    lanes = 2
    here = lax.axis_index("real")
    z, side = here // lanes, here % lanes
    outer = (z == 0) | (z == 3)
    pick = lambda a, b: jnp.where(outer, a, b)
    mirror = 3 - z
    partner = z ^ 1
    other = mirror ^ 1
    spot = lambda at, which: at * lanes + which

    def hop(value, bits):
        return lax.ppermute(value, "real", [(n, n ^ bits) for n in range(real_count)])

    def move(value, pairs):
        return lax.ppermute(value, "real", [(a * lanes + n, b * lanes + n) for a, b in pairs for n in range(lanes)])

    ends = lambda value: hop(value, 2)
    lane = lambda value: hop(value, 1)
    middle = lambda value: move(value, [(1, 2), (2, 1)])
    out = lambda value: move(value, [(1, 0), (2, 3)])
    outer_lane = lambda value: lax.ppermute(value, "real", [(n, n ^ 1) for n in (0, 1, 6, 7)])

    trailing = mine.shape[0] - 1
    cut = 1 + (trailing + 1) // 2
    own = mine[1:]
    halves = [slice(0, cut - 1), slice(cut - 1, trailing)]

    h_own = mine[0:1]
    h_line = [h_own] + [hop(h_own, bits) for bits in (2, 4, 6)]
    s1 = [lane(own[halves[0]]), None]
    h_line = jnp.concatenate(h_line)
    start = after(own, h_line)
    e1, m1 = ends(start), middle(start)
    h_all = jnp.concatenate([h_line, lane(h_line)])
    s1[1] = lane(after(own[halves[1]], s1[0]))
    s1 = jnp.concatenate(s1)
    owners = jnp.stack([here ^ bits for bits in (0, 2, 4, 6, 1, 3, 5, 7)]).astype(jnp.int32)
    codes, sides = over_row(after(right_sides, h_line)[0, 0], row_count)
    codes, heads = over_row(h_all, row_count)

    held = (e1, m1, s1)
    o2, m2, s2 = out(after(m1, *held)), middle(after(e1, *held)), lane(after(e1, *held))
    held = (o2, m2, s2)
    o3, m3, s3 = out(after(m2, *held)), middle(after(s1, *held)), lane(after(pick(o2, m2), *held))
    heads[0] = after(heads[0], *held)
    y = solve(position, codes, [[part] for part in heads], owners, sides)
    last = [outer_lane(after(o3[halves[0]], y)), out(after(s3[halves[1]], y))]

    places = [
        here,
        spot(partner, side),
        spot(z, 1 - side),
        pick(spot(other, side), spot(mirror, side)),
        spot(partner, 1 - side),
        pick(spot(mirror, side), spot(other, side)),
        spot(other, 1 - side),
    ]
    places = jnp.stack(places).astype(jnp.int32)
    pieces = [[own], [e1], [s1], [m1, o2], [s2], [m2, o3], [s3]]
    result = update(y, position, places, pieces, right_sides, 1, with_head=True)
    place = spot(mirror, 1 - side)[None].astype(jnp.int32)
    for k, first in ((1, cut), (0, 1)):
        result = finish(y, place, [(m3, first - 1), (last[k], 0)], result, first)
    return result


def solution(mesh):
    placed = (P(None, "row", None, "real"), P(None, "row", None, "real"))
    return jax.shard_map(
        body, mesh=mesh, in_specs=placed, out_specs=P(None, "row", None, "real"), check_vma=False
    )
```

time: 173 us -> 144 us (0.83); the launches traced: 170 us -> 143 us
  waiting for transfers between devices: 70.6 us -> 54.6 us
  between operations: 13.7 us -> 0.25 us
  local copies, waits for them, and re-layouts: 10.5 us -> 16.2 us
  Pallas kernels: 44 us -> 41.1 us
  starting transfers between devices: 27 us -> 29.8 us
  other arithmetic: 3.98 us -> 1.18 us
    all_gather x1 -> x0, waiting for transfers between devices: 37 us -> none  [body(): head = lax.all_gather(mine[0], 'real', axis=1, tiled=True)]
    pallas_call x4 -> x1, Pallas kernels: 26.4 us -> 15 us  [update(): pl.pallas_call(kernel, out_shape=jax.ShapeDtypeStruct(base.shape, F32), g...]
    ppermute x18 -> x16, waiting for transfers between devices: 27.8 us -> 39.1 us  [the longest x9 24.1 us: hop(): lax.ppermute(value, 'real', [(n, n ^ bits) for n in range(real_count)])]
    ppermute x6, waiting for transfers between devices: 5.75 us -> 15.4 us  [over_row(): held = held + [lax.ppermute(value, 'row', pairs) for value in held]]
    pallas_call x1 -> x2, Pallas kernels: 2.02 us -> 9.97 us  [finish(): pl.pallas_call(kernel, out_shape=jax.ShapeDtypeStruct(out.shape, F32), gr...]
    unnamed x42 -> x27, local copies, waits for them, and re-layouts: 4.8 us -> 9 us
    ppermute x18 -> x16, starting transfers between devices: 22.3 us -> 26.1 us  [the longest x9 17.5 us: hop(): lax.ppermute(value, 'real', [(n, n ^ bits) for n in range(real_count)])]
    select_n x4 -> x1, other arithmetic: 3.98 us -> 1.15 us  [body(): pick = lambda a, b: jnp.where(outer, a, b)]
  transfers between devices with their start and end apart: 25 -> 22, of which waited for: 8 -> 8; matrix products, arithmetic and copies ran while one was open for 5% -> 8% of each run, Pallas kernels for 23% -> 25%
where the time goes in v2:
time: 144 us; the launch traced here: 143 us
  waiting for transfers between devices  54.6 us (38%)
  Pallas kernels  41.1 us (29%)
  starting transfers between devices  29.8 us (21%)
  local copies, waits for them, and re-layouts  16.2 us (11%)
    ppermute x9, waiting for transfers between devices, hop(): lax.ppermute(value, 'real', [(n, n ^ bits) for n in range(real_count)])  24.1 us
    ppermute x9, starting transfers between devices, hop(): lax.ppermute(value, 'real', [(n, n ^ bits) for n in range(real_count)])  17.5 us
    pallas_call x1, Pallas kernels, solve(): pl.pallas_call(kernel, out_shape=jax.ShapeDtypeStruct((window, columns),...  16.1 us
    ppermute x6, waiting for transfers between devices, over_row(): held = held + [lax.ppermute(value, 'row', pairs) for value in held]  15.4 us
    ppermute x6, waiting for transfers between devices, move(): lax.ppermute(value, 'real', [(a * lanes + n, b * lanes + n) for a, b in p...  15.1 us
    pallas_call x1, Pallas kernels, update(): pl.pallas_call(kernel, out_shape=jax.ShapeDtypeStruct(base.shape, F32), g...  15 us
    pallas_call x2, Pallas kernels, finish(): pl.pallas_call(kernel, out_shape=jax.ShapeDtypeStruct(out.shape, F32), gr...  9.97 us
    unnamed x27, local copies, waits for them, and re-layouts  9 us
  transfers between devices with their start and end apart: 22, of which 8 were waited for; matrix products, arithmetic and copies ran while one was open for 8% of the time, Pallas kernels for 25%

profile of v2, /device:TPU:0, one launch (start us, length us, event | category | flops | bytes accessed | tf_op | source)
XLA Modules:
  0.0 143.1 jit_solution(15680082553118150566)
XLA Ops:
  1.0 3.1 %collective-permute-start = (f32[1,256,128]{2,1,0:T(8,128)S(1)}, f32[1,256,128]{2,1,0:T(8,128)S(1)}, u32[]{:S(2)}, u32[]{:S(2)}) collective-permute-start(f32[1,256,128]{2,1,0:T(8,128)S(1)} %slice_bitcast_fusion.4), channel_id=1, source_target_pairs={{0,2},{1,3},{2,0},{3,1},{4,6},{5,7},{6,4},{7,5},{8,10},{9,11},{10,... | collective-permute-start | bytes 393224 | tf_op jit(solution)/shard_map/ppermute | solution.py:299
  4.1 2.6 %collective-permute-start.1 = (f32[1,256,128]{2,1,0:T(8,128)S(1)}, f32[1,256,128]{2,1,0:T(8,128)S(1)}, u32[]{:S(2)}, u32[]{:S(2)}) collective-permute-start(f32[1,256,128]{2,1,0:T(8,128)S(1)} %slice_bitcast_fusion.4), channel_id=1, source_target_pairs={{0,4},{1,5},{2,6},{3,7},{4,0},{5,1},{6,2},{7,3},{8,12},{9,13},{10,... | collective-permute-start | bytes 393224 | tf_op jit(solution)/shard_map/ppermute | solution.py:299
  7.8 1.8 %collective-permute-start.6 = (f32[5,256,128]{2,1,0:T(8,128)S(1)}, f32[5,256,128]{2,1,0:T(8,128)S(1)}, u32[]{:S(2)}, u32[]{:S(2)}) collective-permute-start(f32[5,256,128]{2,1,0:T(8,128)S(1)} %slice_bitcast_fusion.1), channel_id=1, source_target_pairs={{0,1},{1,0},{2,3},{3,2},{4,5},{5,4},{6,7},{7,6},{8,9},{9,8},{10,11... | collective-permute-start | bytes 1966088 | tf_op jit(solution)/shard_map/ppermute | solution.py:299
  9.7 7.3 %collective-permute-done.1 = f32[1,256,128]{2,1,0:T(8,128)S(1)} collective-permute-done((f32[1,256,128]{2,1,0:T(8,128)S(1)}, f32[1,256,128]{2,1,0:T(8,128)S(1)}, u32[]{:S(2)}, u32[]{:S(2)}) %collective-permute-start.1) | collective-permute-done | bytes 131104 | tf_op jit(solution)/shard_map/ppermute | solution.py:299
  17.8 4.8 %collective-permute-start.5 = (f32[9,256,128]{2,1,0:T(8,128)S(1)}, f32[9,256,128]{2,1,0:T(8,128)}, u32[]{:S(2)}, u32[]{:S(2)}) collective-permute-start(f32[9,256,128]{2,1,0:T(8,128)S(1)} %slice_bitcast_fusion.refs_2_), channel_id=1, source_target_pairs={{0,2},{1,3},{2,0},{3,1},{4,6},{5,7},{6,4},{7,5},{8,10},{9,11},{10,... | collective-permute-start | bytes 3538952 | tf_op jit(solution)/shard_map/ppermute | solution.py:299
  22.6 1.6 %collective-permute-start.3 = (f32[4,256,128]{2,1,0:T(8,128)S(1)}, f32[4,256,128]{2,1,0:T(8,128)S(1)}, u32[]{:S(2)}, u32[]{:S(2)}) collective-permute-start(f32[4,256,128]{2,1,0:T(8,128)S(1)} %pad_maximum_fusion), channel_id=1, source_target_pairs={{0,1},{1,0},{2,3},{3,2},{4,5},{5,4},{6,7},{7,6},{8,9},{9,8},{10,11... | collective-permute-start | bytes 1572872 | tf_op jit(solution)/shard_map/ppermute | solution.py:299
  27.5 10.1 %collective-permute-done.3 = f32[4,256,128]{2,1,0:T(8,128)S(1)} collective-permute-done((f32[4,256,128]{2,1,0:T(8,128)S(1)}, f32[4,256,128]{2,1,0:T(8,128)S(1)}, u32[]{:S(2)}, u32[]{:S(2)}) %collective-permute-start.3) | collective-permute-done | bytes 524320 | tf_op jit(solution)/shard_map/ppermute | solution.py:299
  38.4 1.5 %collective-permute-start.11 = (f32[8,256,128]{2,1,0:T(8,128)}, f32[8,256,128]{2,1,0:T(8,128)}, u32[]{:S(2)}, u32[]{:S(2)}) collective-permute-start(f32[8,256,128]{2,1,0:T(8,128)} %constant_dynamic-update-slice_fusion.refs_0_), channel_id=1, source_target_pairs={{0,16},{8,24},{16,0},{24,8},{1,17},{9,25},{17,1},{25,9},{2,18},{10... | collective-permute-start | bytes 3145736 | tf_op jit(solution)/shard_map/ppermute | solution.py:266
  40.8 5.5 %collective-permute-done.7 = f32[4,256,128]{2,1,0:T(8,128)S(1)} collective-permute-done((f32[4,256,128]{2,1,0:T(8,128)S(1)}, f32[4,256,128]{2,1,0:T(8,128)S(1)}, u32[]{:S(2)}, u32[]{:S(2)}) %collective-permute-start.7) | collective-permute-done | bytes 524320 | tf_op jit(solution)/shard_map/ppermute | solution.py:299
  48.2 1.3 collective-permute-start.8
  51.6 1.6 %collective-permute-start.14 = (f32[256,512]{1,0:T(8,128)S(1)}, f32[256,512]{1,0:T(8,128)S(1)}, u32[]{:S(2)}, u32[]{:S(2)}) collective-permute-start(f32[256,512]{1,0:T(8,128)S(1)} %slice_bitcast_fusion.3.refs_4_), channel_id=1, source_target_pairs={{0,16},{8,24},{16,0},{24,8},{1,17},{9,25},{17,1},{25,9},{2,18},{10... | collective-permute-start | bytes 1572872 | tf_op jit(solution)/shard_map/ppermute | solution.py:266
  53.1 1.5 %collective-permute-start.10 = (f32[9,256,128]{2,1,0:T(8,128)}, f32[9,256,128]{2,1,0:T(8,128)}, u32[]{:S(2)}, u32[]{:S(2)}) collective-permute-start(f32[9,256,128]{2,1,0:T(8,128)} %collective-permute-done.5.refs_3_), channel_id=1, source_target_pairs={{0,1},{1,0},{2,3},{3,2},{4,5},{5,4},{6,7},{7,6},{8,9},{9,8},{10,11... | collective-permute-start | bytes 3538952 | tf_op jit(solution)/shard_map/ppermute | solution.py:299
  54.7 15.4 %collective-permute-done.14.refs_5_ = f32[256,512]{1,0:T(8,128)S(1)} collective-permute-done((f32[256,512]{1,0:T(8,128)S(1)}, f32[256,512]{1,0:T(8,128)S(1)}, u32[]{:S(2)}, u32[]{:S(2)}) %collective-permute-start.14) | collective-permute-done | bytes 524320 | tf_op jit(solution)/shard_map/ppermute | solution.py:266
  70.7 6.1 %collective-permute-done.8.refs_6_ = f32[9,256,128]{2,1,0:T(8,128)S(1)} collective-permute-done((f32[9,256,128]{2,1,0:T(8,128)S(1)}, f32[9,256,128]{2,1,0:T(8,128)S(1)}, u32[]{:S(2)}, u32[]{:S(2)}) %collective-permute-start.8) | collective-permute-done | bytes 1179680 | tf_op jit(solution)/shard_map/ppermute | solution.py:302
  79.0 1.5 %collective-permute-start.20 = (f32[9,256,128]{2,1,0:T(8,128)}, f32[9,256,128]{2,1,0:T(8,128)}, u32[]{:S(2)}, u32[]{:S(2)}) collective-permute-start(f32[9,256,128]{2,1,0:T(8,128)} %broadcast_select_fusion), channel_id=1, source_target_pairs={{0,1},{1,0},{2,3},{3,2},{4,5},{5,4},{6,7},{7,6},{8,9},{9,8},{10,11... | collective-permute-start | bytes 3538952 | tf_op jit(solution)/shard_map/ppermute | solution.py:299
  80.5 1.3 collective-permute-start.18
  84.7 16.1 %solve.1.refs_0_.y_ref = f32[1024,512]{1,0:T(8,128)} custom-call(s32[33]{0:T(128)S(1)} %concatenate.17.place, f32[8,256,128]{2,1,0:T(8,128)} %constant_dynamic-update-slice_fusion.refs_0_, f32[8,256,128]{2,1,0:T(8,128)} %collective-permute-done.11.refs_1_, f32[8,256,128]{2,1,0:T(8,128)} %collective-permute-done.12.refs_2_, ...), custom_call_target="tpu_custom_call" | custom-call | flops 16106127360 | bytes 8388608 | tf_op jit(solution)/shard_map/solve/pallas_call | solution.py:132
  100.8 8.9 %collective-permute-done.18.refs_9_ = f32[9,256,128]{2,1,0:T(8,128)S(1)} collective-permute-done((f32[9,256,128]{2,1,0:T(8,128)S(1)}, f32[9,256,128]{2,1,0:T(8,128)S(1)}, u32[]{:S(2)}, u32[]{:S(2)}) %collective-permute-start.18) | collective-permute-done | bytes 1179680 | tf_op jit(solution)/shard_map/ppermute | solution.py:302
  111.7 2.6 %collective-permute-start.19 = (f32[5,256,128]{2,1,0:T(8,128)}, f32[5,256,128]{2,1,0:T(8,128)}, u32[]{:S(2)}, u32[]{:S(2)}) collective-permute-start(f32[5,256,128]{2,1,0:T(8,128)} %slice.49), channel_id=1, source_target_pairs={{0,1},{1,0},{6,7},{7,6},{8,9},{9,8},{14,15},{15,14},{16,17},{17,16... | collective-permute-start | bytes 1966088 | tf_op jit(solution)/shard_map/ppermute | solution.py:308
  115.5 1.3 collective-permute-start.21
  116.8 1.3 copy-done.4
  118.1 15.0 %update.1.refs_2_ = f32[10,1,256,512]{3,2,1,0:T(8,128)} custom-call(s32[8]{0:T(128)S(1)} %concatenate.21.place, f32[1024,512]{1,0:T(8,128)} %solve.1.refs_0_.y_ref, f32[10,1,256,512]{3,2,1,0:T(8,128)} %refs_1_.1, f32[9,256,128]{2,1,0:T(8,128)S(1)} %slice_bitcast_fusion.refs_2_, f32[9,256,128]{2,1,0:T(8,128)} %collective-permute-done.5.refs_3_, ...), custom_call_target="tpu_custom_call" | custom-call | flops 6341787648 | bytes 17694720 | tf_op jit(solution)/shard_map/update/pallas_call | solution.py:202
  133.1 4.3 %finish.2.refs_2_ = f32[10,1,256,512]{3,2,1,0:T(8,128)} custom-call(s32[1]{0:T(128)} %bitcast.place, f32[1024,512]{1,0:T(8,128)S(1)} %copy-done, f32[9,256,128]{2,1,0:T(8,128)S(1)} %collective-permute-done.17.refs_0_, f32[4,256,128]{2,1,0:T(8,128)S(1)} %collective-permute-done.21.refs_1_, ...), custom_call_target="tpu_custom_call", output_to_operand_aliasing={{}: (4, {})} | custom-call | flops 402653184 | bytes 4718592 | tf_op jit(solution)/shard_map/finish/pallas_call | solution.py:239
  137.5 5.6 %finish.3 = f32[10,1,256,512]{3,2,1,0:T(8,128)} custom-call(s32[1]{0:T(128)} %bitcast.place, f32[1024,512]{1,0:T(8,128)S(1)} %copy-done, f32[9,256,128]{2,1,0:T(8,128)S(1)} %collective-permute-done.17.refs_0_, f32[5,256,128]{2,1,0:T(8,128)} %collective-permute-done.19.refs_1_, f32[10,1,256,512]{3,2,1,0:T(8,128)} %finish.2.refs_2_), custom_call_target="tpu_custom_call", output_to_operand_aliasing={{}: (4, {})} | custom-call | flops 503316480 | bytes 5898240 | tf_op jit(solution)/shard_map/finish/pallas_call | solution.py:239
  (64 shorter events, 20.7 us)
Async XLA Ops:
  1.0 8.7 %collective-permute-start = (f32[1,256,128]{2,1,0:T(8,128)S(1)}, f32[1,256,128]{2,1,0:T(8,128)S(1)}, u32[]{:S(2)}, u32[]{:S(2)}) collective-permute-start(f32[1,256,128]{2,1,0:T(8,128)S(1)} %slice_bitcast_fusion.4), channel_id=1, source_target_pairs={{0,2},{1,3},{2,0},{3,1},{4,6},{5,7},{6,4},{7,5},{8,10},{9,11},{10,... | collective-permute-start | bytes 393224 | tf_op jit(solution)/shard_map/ppermute | solution.py:299
  4.1 12.9 %collective-permute-start.1 = (f32[1,256,128]{2,1,0:T(8,128)S(1)}, f32[1,256,128]{2,1,0:T(8,128)S(1)}, u32[]{:S(2)}, u32[]{:S(2)}) collective-permute-start(f32[1,256,128]{2,1,0:T(8,128)S(1)} %slice_bitcast_fusion.4), channel_id=1, source_target_pairs={{0,4},{1,5},{2,6},{3,7},{4,0},{5,1},{6,2},{7,3},{8,12},{9,13},{10,... | collective-permute-start | bytes 393224 | tf_op jit(solution)/shard_map/ppermute | solution.py:299
  6.7 10.3 %collective-permute-start.2 = (f32[1,256,128]{2,1,0:T(8,128)S(1)}, f32[1,256,128]{2,1,0:T(8,128)S(1)}, u32[]{:S(2)}, u32[]{:S(2)}) collective-permute-start(f32[1,256,128]{2,1,0:T(8,128)S(1)} %slice_bitcast_fusion.4), channel_id=1, source_target_pairs={{0,6},{1,7},{2,4},{3,5},{4,2},{5,3},{6,0},{7,1},{8,14},{9,15},{10,... | collective-permute-start | bytes 393224 | tf_op jit(solution)/shard_map/ppermute | solution.py:299
  7.8 17.1 %collective-permute-start.6 = (f32[5,256,128]{2,1,0:T(8,128)S(1)}, f32[5,256,128]{2,1,0:T(8,128)S(1)}, u32[]{:S(2)}, u32[]{:S(2)}) collective-permute-start(f32[5,256,128]{2,1,0:T(8,128)S(1)} %slice_bitcast_fusion.1), channel_id=1, source_target_pairs={{0,1},{1,0},{2,3},{3,2},{4,5},{5,4},{6,7},{7,6},{8,9},{9,8},{10,11... | collective-permute-start | bytes 1966088 | tf_op jit(solution)/shard_map/ppermute | solution.py:299
  17.1 30.1 %collective-permute-start.4 = (f32[9,256,128]{2,1,0:T(8,128)S(1)}, f32[9,256,128]{2,1,0:T(8,128)S(1)}, u32[]{:S(2)}, u32[]{:S(2)}) collective-permute-start(f32[9,256,128]{2,1,0:T(8,128)S(1)} %slice_bitcast_fusion.refs_2_), channel_id=1, source_target_pairs={{2,4},{3,5},{4,2},{5,3},{10,12},{11,13},{12,10},{13,11},{18,20},{1... | collective-permute-start | bytes 3538952 | tf_op jit(solution)/shard_map/ppermute | solution.py:302
  17.8 29.6 %collective-permute-start.5 = (f32[9,256,128]{2,1,0:T(8,128)S(1)}, f32[9,256,128]{2,1,0:T(8,128)}, u32[]{:S(2)}, u32[]{:S(2)}) collective-permute-start(f32[9,256,128]{2,1,0:T(8,128)S(1)} %slice_bitcast_fusion.refs_2_), channel_id=1, source_target_pairs={{0,2},{1,3},{2,0},{3,1},{4,6},{5,7},{6,4},{7,5},{8,10},{9,11},{10,... | collective-permute-start | bytes 3538952 | tf_op jit(solution)/shard_map/ppermute | solution.py:299
  22.6 14.9 %collective-permute-start.3 = (f32[4,256,128]{2,1,0:T(8,128)S(1)}, f32[4,256,128]{2,1,0:T(8,128)S(1)}, u32[]{:S(2)}, u32[]{:S(2)}) collective-permute-start(f32[4,256,128]{2,1,0:T(8,128)S(1)} %pad_maximum_fusion), channel_id=1, source_target_pairs={{0,1},{1,0},{2,3},{3,2},{4,5},{5,4},{6,7},{7,6},{8,9},{9,8},{10,11... | collective-permute-start | bytes 1572872 | tf_op jit(solution)/shard_map/ppermute | solution.py:299
  24.9 21.4 %collective-permute-start.7 = (f32[4,256,128]{2,1,0:T(8,128)S(1)}, f32[4,256,128]{2,1,0:T(8,128)S(1)}, u32[]{:S(2)}, u32[]{:S(2)}) collective-permute-start(f32[4,256,128]{2,1,0:T(8,128)S(1)} %slice_bitcast_fusion.2), channel_id=1, source_target_pairs={{0,1},{1,0},{2,3},{3,2},{4,5},{5,4},{6,7},{7,6},{8,9},{9,8},{10,11... | collective-permute-start | bytes 1572872 | tf_op jit(solution)/shard_map/ppermute | solution.py:299
  38.4 31.7 %collective-permute-start.11 = (f32[8,256,128]{2,1,0:T(8,128)}, f32[8,256,128]{2,1,0:T(8,128)}, u32[]{:S(2)}, u32[]{:S(2)}) collective-permute-start(f32[8,256,128]{2,1,0:T(8,128)} %constant_dynamic-update-slice_fusion.refs_0_), channel_id=1, source_target_pairs={{0,16},{8,24},{16,0},{24,8},{1,17},{9,25},{17,1},{25,9},{2,18},{10... | collective-permute-start | bytes 3145736 | tf_op jit(solution)/shard_map/ppermute | solution.py:266
  47.4 23.2 %collective-permute-start.9 = (f32[9,256,128]{2,1,0:T(8,128)}, f32[9,256,128]{2,1,0:T(8,128)S(1)}, u32[]{:S(2)}, u32[]{:S(2)}) collective-permute-start(f32[9,256,128]{2,1,0:T(8,128)} %collective-permute-done.5.refs_3_), channel_id=1, source_target_pairs={{2,4},{3,5},{4,2},{5,3},{10,12},{11,13},{12,10},{13,11},{18,20},{1... | collective-permute-start | bytes 3538952 | tf_op jit(solution)/shard_map/ppermute | solution.py:302
  48.2 28.7 %collective-permute-start.8 = (f32[9,256,128]{2,1,0:T(8,128)S(1)}, f32[9,256,128]{2,1,0:T(8,128)S(1)}, u32[]{:S(2)}, u32[]{:S(2)}) collective-permute-start(f32[9,256,128]{2,1,0:T(8,128)S(1)} %collective-permute-done.4.refs_5_), channel_id=1, source_target_pairs={{2,0},{3,1},{4,6},{5,7},{10,8},{11,9},{12,14},{13,15},{18,16},{19,... | collective-permute-start | bytes 3538952 | tf_op jit(solution)/shard_map/ppermute | solution.py:302
  51.6 26.6 %copy-start.1 = (f32[256,512]{1,0:T(8,128)}, f32[256,512]{1,0:T(8,128)S(1)}, u32[]{:S(2)}) copy-start(f32[256,512]{1,0:T(8,128)S(1)} %slice_bitcast_fusion.3.refs_4_) | copy-start | bytes 1572868
  51.6 18.5 %collective-permute-start.14 = (f32[256,512]{1,0:T(8,128)S(1)}, f32[256,512]{1,0:T(8,128)S(1)}, u32[]{:S(2)}, u32[]{:S(2)}) collective-permute-start(f32[256,512]{1,0:T(8,128)S(1)} %slice_bitcast_fusion.3.refs_4_), channel_id=1, source_target_pairs={{0,16},{8,24},{16,0},{24,8},{1,17},{9,25},{17,1},{25,9},{2,18},{10... | collective-permute-start | bytes 1572872 | tf_op jit(solution)/shard_map/ppermute | solution.py:266
  53.1 25.9 %collective-permute-start.10 = (f32[9,256,128]{2,1,0:T(8,128)}, f32[9,256,128]{2,1,0:T(8,128)}, u32[]{:S(2)}, u32[]{:S(2)}) collective-permute-start(f32[9,256,128]{2,1,0:T(8,128)} %collective-permute-done.5.refs_3_), channel_id=1, source_target_pairs={{0,1},{1,0},{2,3},{3,2},{4,5},{5,4},{6,7},{7,6},{8,9},{9,8},{10,11... | collective-permute-start | bytes 3538952 | tf_op jit(solution)/shard_map/ppermute | solution.py:299
  70.1 12.5 %collective-permute-start.12 = (f32[8,256,128]{2,1,0:T(8,128)}, f32[8,256,128]{2,1,0:T(8,128)}, u32[]{:S(2)}, u32[]{:S(2)}) collective-permute-start(f32[8,256,128]{2,1,0:T(8,128)} %constant_dynamic-update-slice_fusion.refs_0_), channel_id=1, source_target_pairs={{0,8},{8,0},{16,24},{24,16},{1,9},{9,1},{17,25},{25,17},{2,10},{10... | collective-permute-start | bytes 3145736 | tf_op jit(solution)/shard_map/ppermute | solution.py:266
  70.1 12.5 %collective-permute-start.13 = (f32[8,256,128]{2,1,0:T(8,128)}, f32[8,256,128]{2,1,0:T(8,128)}, u32[]{:S(2)}, u32[]{:S(2)}) collective-permute-start(f32[8,256,128]{2,1,0:T(8,128)} %collective-permute-done.11.refs_1_), channel_id=1, source_target_pairs={{0,8},{8,0},{16,24},{24,16},{1,9},{9,1},{17,25},{25,17},{2,10},{10... | collective-permute-start | bytes 3145736 | tf_op jit(solution)/shard_map/ppermute | solution.py:266
  70.6 9.9 %collective-permute-start.15 = (f32[256,512]{1,0:T(8,128)S(1)}, f32[256,512]{1,0:T(8,128)}, u32[]{:S(2)}, u32[]{:S(2)}) collective-permute-start(f32[256,512]{1,0:T(8,128)S(1)} %slice_bitcast_fusion.3.refs_4_), channel_id=1, source_target_pairs={{0,8},{8,0},{16,24},{24,16},{1,9},{9,1},{17,25},{25,17},{2,10},{10... | collective-permute-start | bytes 1572872 | tf_op jit(solution)/shard_map/ppermute | solution.py:266
  76.9 5.0 %collective-permute-start.16 = (f32[256,512]{1,0:T(8,128)S(1)}, f32[256,512]{1,0:T(8,128)}, u32[]{:S(2)}, u32[]{:S(2)}) collective-permute-start(f32[256,512]{1,0:T(8,128)S(1)} %collective-permute-done.14.refs_5_), channel_id=1, source_target_pairs={{0,8},{8,0},{16,24},{24,16},{1,9},{9,1},{17,25},{25,17},{2,10},{10... | collective-permute-start | bytes 1572872 | tf_op jit(solution)/shard_map/ppermute | solution.py:266
  79.0 35.4 %collective-permute-start.20 = (f32[9,256,128]{2,1,0:T(8,128)}, f32[9,256,128]{2,1,0:T(8,128)}, u32[]{:S(2)}, u32[]{:S(2)}) collective-permute-start(f32[9,256,128]{2,1,0:T(8,128)} %broadcast_select_fusion), channel_id=1, source_target_pairs={{0,1},{1,0},{2,3},{3,2},{4,5},{5,4},{6,7},{7,6},{8,9},{9,8},{10,11... | collective-permute-start | bytes 3538952 | tf_op jit(solution)/shard_map/ppermute | solution.py:299
  80.5 29.2 %collective-permute-start.18 = (f32[9,256,128]{2,1,0:T(8,128)S(1)}, f32[9,256,128]{2,1,0:T(8,128)S(1)}, u32[]{:S(2)}, u32[]{:S(2)}) collective-permute-start(f32[9,256,128]{2,1,0:T(8,128)S(1)} %copy-done.9), channel_id=1, source_target_pairs={{2,0},{3,1},{4,6},{5,7},{10,8},{11,9},{12,14},{13,15},{18,16},{19,... | collective-permute-start | bytes 3538952 | tf_op jit(solution)/shard_map/ppermute | solution.py:302
  81.8 51.3 %collective-permute-start.17 = (f32[9,256,128]{2,1,0:T(8,128)}, f32[9,256,128]{2,1,0:T(8,128)S(1)}, u32[]{:S(2)}, u32[]{:S(2)}) collective-permute-start(f32[9,256,128]{2,1,0:T(8,128)} %constant_dynamic-update-slice_fusion.5.refs_4_), channel_id=1, source_target_pairs={{2,4},{3,5},{4,2},{5,3},{10,12},{11,13},{12,10},{13,11},{18,20},{1... | collective-permute-start | bytes 3538952 | tf_op jit(solution)/shard_map/ppermute | solution.py:302
  111.7 25.8 %collective-permute-start.19 = (f32[5,256,128]{2,1,0:T(8,128)}, f32[5,256,128]{2,1,0:T(8,128)}, u32[]{:S(2)}, u32[]{:S(2)}) collective-permute-start(f32[5,256,128]{2,1,0:T(8,128)} %slice.49), channel_id=1, source_target_pairs={{0,1},{1,0},{6,7},{7,6},{8,9},{9,8},{14,15},{15,14},{16,17},{17,16... | collective-permute-start | bytes 1966088 | tf_op jit(solution)/shard_map/ppermute | solution.py:308
  115.5 17.6 %collective-permute-start.21 = (f32[4,256,128]{2,1,0:T(8,128)S(1)}, f32[4,256,128]{2,1,0:T(8,128)S(1)}, u32[]{:S(2)}, u32[]{:S(2)}) collective-permute-start(f32[4,256,128]{2,1,0:T(8,128)S(1)} %slice.50), channel_id=1, source_target_pairs={{2,0},{3,1},{4,6},{5,7},{10,8},{11,9},{12,14},{13,15},{18,16},{19,... | collective-permute-start | bytes 1572872 | tf_op jit(solution)/shard_map/ppermute | solution.py:302
  118.1 15.1 %copy-start = (f32[1024,512]{1,0:T(8,128)S(1)}, f32[1024,512]{1,0:T(8,128)}, u32[]{:S(2)}) copy-start(f32[1024,512]{1,0:T(8,128)} %solve.1.refs_0_.y_ref) | copy-start | bytes 6291460
  (9 other events, 32.9 us)

commit v3 on v2

--- a/solution.py
+++ b/solution.py
@@ -1,4 +1,5 @@
 import functools
+import math
 
 import jax
 import jax.numpy as jnp
@@ -56,7 +57,7 @@
     return inverses
 
 
-def solve_kernel(codes, counts, place, head_refs, side_refs, y_ref, l_high, l_low, y_high, y_low, landing, head_sems, side_sems):
+def solve_kernel(codes, counts, place, head_refs, side_refs, y_ref, out_ref, l_high, l_low, y_high, y_low, landing, head_sems, side_sems):
     rows, width = head_refs[0].shape[-2:]
     window = l_high.shape[0]
     per_row = len(head_refs) // len(codes)
@@ -115,9 +116,13 @@
             high, low = split(answer)
             y_high[at] = high
             y_low[at] = low
-
-
-def solve(position, codes, heads, owners, sides):
+    at = pl.ds(pl.multiple_of(place[0] * rows, rows), rows)
+    copy = pltpu.make_async_copy(y_ref.at[at], out_ref.at[0, 0], side_sems.at[0])
+    copy.start()
+    copy.wait()
+
+
+def solve(position, codes, heads, owners, sides, out_shape):
     counts = [part.shape[0] for part in heads[0]]
     window = sum(counts) * heads[0][0].shape[-1]
     columns = sides[0].shape[-1]
@@ -131,9 +136,9 @@
 
     return pl.pallas_call(
         kernel,
-        out_shape=jax.ShapeDtypeStruct((window, columns), F32),
+        out_shape=[jax.ShapeDtypeStruct((window, columns), F32), jax.ShapeDtypeStruct(out_shape, F32)],
         in_specs=[pl.BlockSpec(memory_space=pltpu.SMEM)] + [pl.BlockSpec(memory_space=pl.ANY)] * (total + len(codes)),
-        out_specs=pl.BlockSpec(memory_space=pltpu.VMEM),
+        out_specs=[pl.BlockSpec(memory_space=pltpu.VMEM), pl.BlockSpec(memory_space=pl.ANY)],
         scratch_shapes=[
             pltpu.VMEM((window, window), BF16),
             pltpu.VMEM((window, window), BF16),
@@ -151,65 +156,77 @@
     )(place, *flat, *sides)
 
 
-def update(y, position, places, pieces, base, first, target=None, with_head=False):
-    flat = [part for piece in pieces for part in piece]
-    blocks, rows, _ = flat[0].shape
+def row_blocks(count):
+    return next(n for n in (3, 2, 1) if count % n == 0)
+
+
+def laid(parts, step, width):
+    begins = [sum(part.shape[0] for part in parts[:n]) // step for n in range(len(parts))]
+    ends = [begin + part.shape[0] // step for begin, part in zip(begins, parts)]
+
+    def spec(part, begin, end):
+        return pl.BlockSpec((step, part.shape[1], width), lambda i, *_: (jnp.clip(i - begin, 0, end - begin - 1), 0, 0))
+
+    def read(refs, n):
+        value = refs[0][n]
+        for ref, begin in zip(refs[1:], begins[1:]):
+            value = jnp.where(pl.program_id(0) >= begin, ref[n], value)
+        return value
+
+    return [spec(*given) for given in zip(parts, begins, ends)], read
+
+
+def update(y, places, pieces, base, target=None):
+    flat = [part if isinstance(part, tuple) else (part,) for piece in pieces for part in piece]
+    blocks = sum(part.shape[0] for part in flat[0])
+    rows = flat[0][0].shape[1]
     columns = y.shape[1]
-    widths = [piece[0].shape[-1] for piece in pieces]
-    count = len(flat)
+    widths = [(piece[0][0] if isinstance(piece[0], tuple) else piece[0]).shape[-1] for piece in pieces]
+    owner = [n for n, piece in enumerate(pieces) for _ in piece]
     depth = sum(widths)
-    skip = int(with_head)
+    step = row_blocks(math.gcd(*(part.shape[0] for parts in flat for part in parts)))
+    specs, reads = zip(*(laid(parts, step, widths[n]) for parts, n in zip(flat, owner)))
+    lengths = [len(parts) for parts in flat]
+    count = sum(lengths)
 
     def kernel(place, *refs):
         y_ref, base_ref = refs[0], refs[1]
-        piece_refs = list(refs[2 : 2 + count])
         out_ref, y_high, y_low = refs[-3:]
 
         @pl.when(pl.program_id(0) == 0)
         def _():
-            begin = 0
+            at = 0
             for n, width in enumerate(widths):
-                high, low = split(y_ref[pl.ds(pl.multiple_of(place[n + 1] * width, width), width)])
-                y_high[begin : begin + width] = high
-                y_low[begin : begin + width] = low
-                begin += width
-
-        def below():
-            columns_of = iter(piece_refs)
-            wide = [sum(next(columns_of)[0] for _ in piece) for piece in pieces]
+                high, low = split(y_ref[pl.ds(pl.multiple_of(place[n] * width, width), width)])
+                y_high[at : at + width] = high
+                y_low[at : at + width] = low
+                at += width
+
+        for n in range(step):
+            wide = [0] * len(pieces)
+            at = 2
+            for read, length, piece in zip(reads, lengths, owner):
+                wide[piece] = wide[piece] + read(refs[at : at + length], n)
+                at += length
             high, low = split(jnp.concatenate(wide, axis=1))
-            out_ref[0, 0] = base_ref[0, 0] - product(high, low, y_high[...], y_low[...])
-
-        if skip:
-
-            @pl.when(pl.program_id(0) == 0)
-            def _():
-                out_ref[0, 0] = y_ref[pl.ds(pl.multiple_of(place[0] * rows, rows), rows)]
-
-            pl.when(pl.program_id(0) > 0)(below)
-        else:
-            below()
-
-    block = pl.BlockSpec((1, 1, rows, columns), lambda i, *_: (i + first - skip, 0, 0, 0))
-    specs = [pl.BlockSpec((y.shape[0], columns), lambda i, *_: (0, 0)), block]
-    specs += [pl.BlockSpec((1, rows, part.shape[-1]), lambda i, *_: (jnp.maximum(i - skip, 0), 0, 0)) for part in flat]
-    operands = [y, base, *flat]
-    aliases = {}
-    if target is not None:
-        specs.append(pl.BlockSpec(memory_space=pl.ANY))
-        operands.append(target)
-        aliases = {len(operands): 0}
+            out_ref[n, 0] = base_ref[n, 0] - product(high, low, y_high[...], y_low[...])
+
+    block = pl.BlockSpec(
+        tuple(pl.Element(n) for n in (step, 1, rows, columns)), lambda i, *_: (i * step + 1, 0, 0, 0)
+    )
     return pl.pallas_call(
         kernel,
         out_shape=jax.ShapeDtypeStruct(base.shape, F32),
         grid_spec=pltpu.PrefetchScalarGridSpec(
             num_scalar_prefetch=1,
-            grid=(blocks + skip,),
-            in_specs=specs,
+            grid=(blocks // step,),
+            in_specs=[pl.BlockSpec(y.shape, lambda i, *_: (0, 0)), block]
+            + [spec for part in specs for spec in part]
+            + [pl.BlockSpec(memory_space=pl.ANY)] * (target is not None),
             out_specs=block,
             scratch_shapes=[pltpu.VMEM((depth, columns), BF16), pltpu.VMEM((depth, columns), BF16)],
         ),
-        input_output_aliases=aliases,
+        input_output_aliases={2 if target is None else 3 + count: 0},
         compiler_params=pltpu.CompilerParams(vmem_limit_bytes=48 << 20),
         cost_estimate=pl.CostEstimate(
             flops=6 * blocks * rows * depth * columns,
@@ -217,45 +234,7 @@
             transcendentals=0,
         ),
         name="update",
-    )(jnp.concatenate([position, places]), *operands)
-
-
-def finish(y, place, piece, out, first):
-    offsets = [offset for _, offset in piece]
-    piece = [part for part, _ in piece]
-    blocks = min(part.shape[0] for part in piece)
-    _, rows, width = piece[0].shape
-    columns = y.shape[1]
-    count = len(piece)
-
-    def kernel(place, y_ref, *refs):
-        y_high, y_low = split(y_ref[...])
-        high, low = split(sum(ref[0] for ref in refs[:count]))
-        wide = jnp.concatenate([high, low, high], axis=1)
-        stack = jnp.concatenate([y_high, y_high, y_low], axis=0)
-        refs[-1][0, 0] = refs[count][0, 0] - jnp.dot(wide, stack, preferred_element_type=F32)
-
-    block = pl.BlockSpec((1, 1, rows, columns), lambda i, *_: (i + first, 0, 0, 0))
-    return pl.pallas_call(
-        kernel,
-        out_shape=jax.ShapeDtypeStruct(out.shape, F32),
-        grid_spec=pltpu.PrefetchScalarGridSpec(
-            num_scalar_prefetch=1,
-            grid=(blocks,),
-            in_specs=[pl.BlockSpec((width, columns), lambda i, place: (place[0], 0))]
-            + [pl.BlockSpec((1, rows, width), lambda i, *_, offset=offset: (i + offset, 0, 0)) for offset in offsets]
-            + [block],
-            out_specs=block,
-        ),
-        input_output_aliases={2 + count: 0},
-        compiler_params=pltpu.CompilerParams(vmem_limit_bytes=48 << 20),
-        cost_estimate=pl.CostEstimate(
-            flops=6 * blocks * rows * width * columns,
-            bytes_accessed=4 * blocks * rows * (width + 2 * columns),
-            transcendentals=0,
-        ),
-        name="finish",
-    )(place, y, *piece, out)
+    )(places, y, base, *(part for parts in flat for part in parts), *([] if target is None else [target]))
 
 
 def over_row(block, size):
@@ -281,9 +260,10 @@
         codes, sides = over_row(right_sides[0, 0], row_count)
         head = lax.all_gather(mine[0], "real", axis=1, tiled=True)
         codes, heads = over_row(head[None], row_count)
-        y = solve(position, codes, [[part] for part in heads], jnp.zeros((1,), jnp.int32), sides)
+        whole = jnp.zeros((1,), jnp.int32)
+        y, result = solve(position, codes, [[part] for part in heads], whole, sides, right_sides.shape)
         rest = lax.all_gather(mine[1:], "real", axis=2, tiled=True)
-        return update(y, position, jnp.zeros((1,), jnp.int32), [[rest]], right_sides, 1, with_head=True)
+        return update(y, whole, [[rest]], right_sides, result)
 
     lanes = 2
     here = lax.axis_index("real")
@@ -305,50 +285,48 @@
     lane = lambda value: hop(value, 1)
     middle = lambda value: move(value, [(1, 2), (2, 1)])
     out = lambda value: move(value, [(1, 0), (2, 3)])
-    outer_lane = lambda value: lax.ppermute(value, "real", [(n, n ^ 1) for n in (0, 1, 6, 7)])
 
     trailing = mine.shape[0] - 1
-    cut = 1 + (trailing + 1) // 2
+    cut = trailing - trailing // 3
     own = mine[1:]
-    halves = [slice(0, cut - 1), slice(cut - 1, trailing)]
+    halves = [slice(0, cut), slice(cut, trailing)]
 
     h_own = mine[0:1]
     h_line = [h_own] + [hop(h_own, bits) for bits in (2, 4, 6)]
-    s1 = [lane(own[halves[0]]), None]
+    middle_row = (trailing + 1) // 2
+    s1 = [lane(own[:middle_row]), None]
+    start = after(own, h_line[1])
+    e1, m1 = ends(start), middle(start)
     h_line = jnp.concatenate(h_line)
-    start = after(own, h_line)
-    e1, m1 = ends(start), middle(start)
     h_all = jnp.concatenate([h_line, lane(h_line)])
-    s1[1] = lane(after(own[halves[1]], s1[0]))
+    s1[1] = lane(after(own[middle_row:], s1[0]))
     s1 = jnp.concatenate(s1)
     owners = jnp.stack([here ^ bits for bits in (0, 2, 4, 6, 1, 3, 5, 7)]).astype(jnp.int32)
-    codes, sides = over_row(after(right_sides, h_line)[0, 0], row_count)
+    codes, sides = over_row(right_sides[0, 0], row_count)
     codes, heads = over_row(h_all, row_count)
 
-    held = (e1, m1, s1)
-    o2, m2, s2 = out(after(m1, *held)), middle(after(e1, *held)), lane(after(e1, *held))
-    held = (o2, m2, s2)
-    o3, m3, s3 = out(after(m2, *held)), middle(after(s1, *held)), lane(after(pick(o2, m2), *held))
-    heads[0] = after(heads[0], *held)
-    y = solve(position, codes, [[part] for part in heads], owners, sides)
-    last = [outer_lane(after(o3[halves[0]], y)), out(after(s3[halves[1]], y))]
-
-    places = [
+    o2, m2 = out(after(m1, e1)), middle(after(e1, m1, sides[1]))
+    s2 = lane(after(e1, s1))
+    first, second = halves
+    o3 = out(after(m2, o2))
+    both = after(pick(o2, m2), s2)
+    s3 = [lane(both[first]), None]
+    heads[0] = after(heads[0], o2, m2)
+    y, result = solve(position, codes, [[part] for part in heads], owners, sides, right_sides.shape)
+    s3[1] = lane(after(both[second], y))
+    last = [ends(after(s3[0], y)), lane(pick(o3[second], m1[second]))]
+
+    near_y = [
         here,
         spot(partner, side),
         spot(z, 1 - side),
         pick(spot(other, side), spot(mirror, side)),
         spot(partner, 1 - side),
-        pick(spot(mirror, side), spot(other, side)),
-        spot(other, 1 - side),
     ]
-    places = jnp.stack(places).astype(jnp.int32)
-    pieces = [[own], [e1], [s1], [m1, o2], [s2], [m2, o3], [s3]]
-    result = update(y, position, places, pieces, right_sides, 1, with_head=True)
-    place = spot(mirror, 1 - side)[None].astype(jnp.int32)
-    for k, first in ((1, cut), (0, 1)):
-        result = finish(y, place, [(m3, first - 1), (last[k], 0)], result, first)
-    return result
+    far_y = [pick(spot(mirror, side), spot(other, side)), spot(other, 1 - side), spot(mirror, 1 - side)]
+    near_y, far_y = (jnp.stack(places).astype(jnp.int32) for places in (near_y, far_y))
+    result = update(y, near_y, [[own], [e1], [s1], [m1, o2], [s2]], right_sides, result)
+    return update(y, far_y, [[m2, o3], [tuple(s3)], [tuple(last)]], result)
 
 
 def solution(mesh):

time: 144 us -> 129 us (0.90)
  local copies, waits for them, and re-layouts: 16.2 us -> 7.95 us
  starting transfers between devices: 29.8 us -> 24.8 us
  Pallas kernels: 41.1 us -> 36.7 us
  waiting for transfers between devices: 54.6 us -> 58.5 us
    ppermute x9 -> x12, waiting for transfers between devices: 24.1 us -> 33.8 us  [hop(): lax.ppermute(value, 'real', [(n, n ^ bits) for n in range(real_count)])]
    pallas_call x3 -> x1, Pallas kernels: 26.1 us -> 17.3 us  [solve(): pl.pallas_call(kernel, out_shape=[jax.ShapeDtypeStruct((window, columns),...]
    ppermute x6, waiting for transfers between devices: 15.4 us -> 8.55 us  [over_row(): held = held + [lax.ppermute(value, 'row', pairs) for value in held]]
    unnamed x27 -> x15, local copies, waits for them, and re-layouts: 9 us -> 3.75 us
    pallas_call x1 -> x2, Pallas kernels: 15 us -> 19.3 us  [update(): pl.pallas_call(kernel, out_shape=jax.ShapeDtypeStruct(base.shape, F32), g...]
    slice x4, local copies, waits for them, and re-layouts: 3.13 us -> 0.16 us  [the longest x1 0.05 us: body(): s3 = [lane(both[first]), None]]
    ppermute x1 -> x0, starting transfers between devices: 2.62 us -> none  [body(): lax.ppermute(value, 'real', [(n, n ^ 1) for n in (0, 1, 6, 7)])]
    ppermute x6 -> x4, starting transfers between devices: 6.06 us -> 4.21 us  [move(): lax.ppermute(value, 'real', [(a * lanes + n, b * lanes + n) for a, b in p...]
  transfers between devices with their start and end apart: 22 -> 22, of which waited for: 8 -> 9; matrix products, arithmetic and copies ran while one was open for 8% -> 5% of each run, Pallas kernels for 25% -> 22%
where the time goes in v3:
time: 129 us; the launch traced here: 128 us
  waiting for transfers between devices  58.5 us (45%)
  Pallas kernels  36.7 us (28%)
  starting transfers between devices  24.8 us (19%)
  local copies, waits for them, and re-layouts  7.95 us (6%)
    ppermute x12, waiting for transfers between devices, hop(): lax.ppermute(value, 'real', [(n, n ^ bits) for n in range(real_count)])  33.8 us
    pallas_call x2, Pallas kernels, update(): pl.pallas_call(kernel, out_shape=jax.ShapeDtypeStruct(base.shape, F32), g...  19.3 us
    ppermute x12, starting transfers between devices, hop(): lax.ppermute(value, 'real', [(n, n ^ bits) for n in range(real_count)])  17.8 us
    pallas_call x1, Pallas kernels, solve(): pl.pallas_call(kernel, out_shape=[jax.ShapeDtypeStruct((window, columns),...  17.3 us
    ppermute x4, waiting for transfers between devices, move(): lax.ppermute(value, 'real', [(a * lanes + n, b * lanes + n) for a, b in p...  16.1 us
    ppermute x6, waiting for transfers between devices, over_row(): held = held + [lax.ppermute(value, 'row', pairs) for value in held]  8.55 us
    ppermute x4, starting transfers between devices, move(): lax.ppermute(value, 'real', [(a * lanes + n, b * lanes + n) for a, b in p...  4.21 us
    unnamed x15, local copies, waits for them, and re-layouts  3.75 us
  transfers between devices with their start and end apart: 22, of which 9 were waited for; matrix products, arithmetic and copies ran while one was open for 5% of the time, Pallas kernels for 22%

profile of v3, /device:TPU:0, one launch (start us, length us, event | category | flops | bytes accessed | tf_op | source)
XLA Modules:
  0.0 128.4 jit_solution(10155014982305256139)
XLA Ops:
  1.0 3.1 %collective-permute-start = (f32[1,256,128]{2,1,0:T(8,128)S(1)}, f32[1,256,128]{2,1,0:T(8,128)S(1)}, u32[]{:S(2)}, u32[]{:S(2)}) collective-permute-start(f32[1,256,128]{2,1,0:T(8,128)S(1)} %slice_bitcast_fusion.4), channel_id=1, source_target_pairs={{0,2},{1,3},{2,0},{3,1},{4,6},{5,7},{6,4},{7,5},{8,10},{9,11},{10,... | collective-permute-start | bytes 393224 | tf_op jit(solution)/shard_map/ppermute | solution.py:279
  4.1 2.6 %collective-permute-start.1 = (f32[1,256,128]{2,1,0:T(8,128)S(1)}, f32[1,256,128]{2,1,0:T(8,128)S(1)}, u32[]{:S(2)}, u32[]{:S(2)}) collective-permute-start(f32[1,256,128]{2,1,0:T(8,128)S(1)} %slice_bitcast_fusion.4), channel_id=1, source_target_pairs={{0,4},{1,5},{2,6},{3,7},{4,0},{5,1},{6,2},{7,3},{8,12},{9,13},{10,... | collective-permute-start | bytes 393224 | tf_op jit(solution)/shard_map/ppermute | solution.py:279
  6.7 1.9 %slice_bitcast_fusion.3.refs_4_ = f32[256,512]{1,0:T(8,128)} fusion(f32[10,1,256,512]{3,2,1,0:T(8,128)} %refs_1_.1), kind=kLoop, calls=%fused_computation.5 | loop fusion | bytes 1048576 | tf_op jit(solution)/shard_map/squeeze | solution.py:305
  8.6 1.7 %collective-permute-start.7 = (f32[256,512]{1,0:T(8,128)}, f32[256,512]{1,0:T(8,128)}, u32[]{:S(2)}, u32[]{:S(2)}) collective-permute-start(f32[256,512]{1,0:T(8,128)} %slice_bitcast_fusion.3.refs_4_), channel_id=1, source_target_pairs={{0,16},{8,24},{16,0},{24,8},{1,17},{9,25},{17,1},{25,9},{2,18},{10... | collective-permute-start | bytes 1572872 | tf_op jit(solution)/shard_map/ppermute | solution.py:245
  10.3 1.6 %collective-permute-start.14 = (f32[5,256,128]{2,1,0:T(8,128)S(1)}, f32[5,256,128]{2,1,0:T(8,128)S(1)}, u32[]{:S(2)}, u32[]{:S(2)}) collective-permute-start(f32[5,256,128]{2,1,0:T(8,128)S(1)} %slice_bitcast_fusion.1), channel_id=1, source_target_pairs={{0,1},{1,0},{2,3},{3,2},{4,5},{5,4},{6,7},{7,6},{8,9},{9,8},{10,11... | collective-permute-start | bytes 1966088 | tf_op jit(solution)/shard_map/ppermute | solution.py:279
  12.8 4.3 %collective-permute-done.1 = f32[1,256,128]{2,1,0:T(8,128)S(1)} collective-permute-done((f32[1,256,128]{2,1,0:T(8,128)S(1)}, f32[1,256,128]{2,1,0:T(8,128)S(1)}, u32[]{:S(2)}, u32[]{:S(2)}) %collective-permute-start.1) | collective-permute-done | bytes 131104 | tf_op jit(solution)/shard_map/ppermute | solution.py:279
  17.1 1.6 %collective-permute-start.3 = (f32[4,256,128]{2,1,0:T(8,128)S(1)}, f32[4,256,128]{2,1,0:T(8,128)S(1)}, u32[]{:S(2)}, u32[]{:S(2)}) collective-permute-start(f32[4,256,128]{2,1,0:T(8,128)S(1)} %pad_maximum_fusion), channel_id=1, source_target_pairs={{0,1},{1,0},{2,3},{3,2},{4,5},{5,4},{6,7},{7,6},{8,9},{9,8},{10,11... | collective-permute-start | bytes 1572872 | tf_op jit(solution)/shard_map/ppermute | solution.py:279
  21.3 15.7 %collective-permute-done.3 = f32[4,256,128]{2,1,0:T(8,128)S(1)} collective-permute-done((f32[4,256,128]{2,1,0:T(8,128)S(1)}, f32[4,256,128]{2,1,0:T(8,128)S(1)}, u32[]{:S(2)}, u32[]{:S(2)}) %collective-permute-start.3) | collective-permute-done | bytes 524320 | tf_op jit(solution)/shard_map/ppermute | solution.py:279
  38.5 1.6 %collective-permute-start.15 = (f32[4,256,128]{2,1,0:T(8,128)S(1)}, f32[4,256,128]{2,1,0:T(8,128)S(1)}, u32[]{:S(2)}, u32[]{:S(2)}) collective-permute-start(f32[4,256,128]{2,1,0:T(8,128)S(1)} %slice_bitcast_fusion.2), channel_id=1, source_target_pairs={{0,1},{1,0},{2,3},{3,2},{4,5},{5,4},{6,7},{7,6},{8,9},{9,8},{10,11... | collective-permute-start | bytes 1572872 | tf_op jit(solution)/shard_map/ppermute | solution.py:279
  40.1 1.6 %collective-permute-done.5.refs_3_ = f32[9,256,128]{2,1,0:T(8,128)} collective-permute-done((f32[9,256,128]{2,1,0:T(8,128)S(1)}, f32[9,256,128]{2,1,0:T(8,128)}, u32[]{:S(2)}, u32[]{:S(2)}) %collective-permute-start.5) | collective-permute-done | bytes 1179680 | tf_op jit(solution)/shard_map/ppermute | solution.py:279
  41.7 1.3 collective-permute-start.6
  43.8 6.5 %collective-permute-done.15 = f32[4,256,128]{2,1,0:T(8,128)S(1)} collective-permute-done((f32[4,256,128]{2,1,0:T(8,128)S(1)}, f32[4,256,128]{2,1,0:T(8,128)S(1)}, u32[]{:S(2)}, u32[]{:S(2)}) %collective-permute-start.15) | collective-permute-done | bytes 524320 | tf_op jit(solution)/shard_map/ppermute | solution.py:279
  51.4 1.3 %collective-permute-start.16 = (f32[9,256,128]{2,1,0:T(8,128)}, f32[9,256,128]{2,1,0:T(8,128)}, u32[]{:S(2)}, u32[]{:S(2)}) collective-permute-start(f32[9,256,128]{2,1,0:T(8,128)} %collective-permute-done.5.refs_3_), channel_id=1, source_target_pairs={{0,1},{1,0},{2,3},{3,2},{4,5},{5,4},{6,7},{7,6},{8,9},{9,8},{10,11... | collective-permute-start | bytes 3538952 | tf_op jit(solution)/shard_map/ppermute | solution.py:279
  52.7 8.5 %collective-permute-done.9.refs_1_ = f32[8,256,128]{2,1,0:T(8,128)} collective-permute-done((f32[8,256,128]{2,1,0:T(8,128)}, f32[8,256,128]{2,1,0:T(8,128)}, u32[]{:S(2)}, u32[]{:S(2)}) %collective-permute-start.9) | collective-permute-done | bytes 1048608 | tf_op jit(solution)/shard_map/ppermute | solution.py:245
  61.2 9.2 %collective-permute-done.6.refs_6_ = f32[9,256,128]{2,1,0:T(8,128)S(1)} collective-permute-done((f32[9,256,128]{2,1,0:T(8,128)S(1)}, f32[9,256,128]{2,1,0:T(8,128)S(1)}, u32[]{:S(2)}, u32[]{:S(2)}) %collective-permute-start.6) | collective-permute-done | bytes 1179680 | tf_op jit(solution)/shard_map/ppermute | solution.py:282
  71.3 5.3 %collective-permute-done.16.refs_7_ = f32[9,256,128]{2,1,0:T(8,128)} collective-permute-done((f32[9,256,128]{2,1,0:T(8,128)}, f32[9,256,128]{2,1,0:T(8,128)}, u32[]{:S(2)}, u32[]{:S(2)}) %collective-permute-start.16) | collective-permute-done | bytes 1179680 | tf_op jit(solution)/shard_map/ppermute | solution.py:279
  76.6 1.5 %collective-permute-start.17 = (f32[9,256,128]{2,1,0:T(8,128)S(1)}, f32[9,256,128]{2,1,0:T(8,128)S(1)}, u32[]{:S(2)}, u32[]{:S(2)}) collective-permute-start(f32[9,256,128]{2,1,0:T(8,128)S(1)} %collective-permute-done.8.refs_2_), channel_id=1, source_target_pairs={{2,0},{3,1},{4,6},{5,7},{10,8},{11,9},{12,14},{13,15},{18,16},{19,... | collective-permute-start | bytes 3538952 | tf_op jit(solution)/shard_map/ppermute | solution.py:282
  78.2 1.2 collective-permute-start.18
  79.4 17.3 %solve.1 = (f32[1024,512]{1,0:T(8,128)}, f32[10,1,256,512]{3,2,1,0:T(8,128)}) custom-call(s32[33]{0:T(128)S(1)} %concatenate.14.place, f32[8,256,128]{2,1,0:T(8,128)} %constant_dynamic-update-slice_fusion.refs_0_, f32[8,256,128]{2,1,0:T(8,128)} %collective-permute-done.9.refs_1_, f32[8,256,128]{2,1,0:T(8,128)} %collective-permute-done.10.refs_2_, ...), custom_call_target="tpu_custom_call" | custom-call | flops 16106127360 | bytes 8388608 | tf_op jit(solution)/shard_map/solve/pallas_call | solution.py:137
  96.7 2.8 %collective-permute-start.20 = (f32[6,256,128]{2,1,0:T(8,128)S(1)}, f32[6,256,128]{2,1,0:T(8,128)S(1)}, u32[]{:S(2)}, u32[]{:S(2)}) collective-permute-start(f32[6,256,128]{2,1,0:T(8,128)S(1)} %collective-permute-done.18.refs_4_), channel_id=1, source_target_pairs={{0,2},{1,3},{2,0},{3,1},{4,6},{5,7},{6,4},{7,5},{8,10},{9,11},{10,... | collective-permute-start | bytes 2359304 | tf_op jit(solution)/shard_map/ppermute | solution.py:279
  100.6 6.8 %collective-permute-done.17.refs_3_ = f32[9,256,128]{2,1,0:T(8,128)S(1)} collective-permute-done((f32[9,256,128]{2,1,0:T(8,128)S(1)}, f32[9,256,128]{2,1,0:T(8,128)S(1)}, u32[]{:S(2)}, u32[]{:S(2)}) %collective-permute-start.17) | collective-permute-done | bytes 1179680 | tf_op jit(solution)/shard_map/ppermute | solution.py:282
  107.5 1.2 collective-permute-start.21
  108.6 10.6 %update.2.refs_1_ = f32[10,1,256,512]{3,2,1,0:T(8,128)} custom-call(s32[5]{0:T(128)S(1)} %stack.69.place, f32[1024,512]{1,0:T(8,128)} %get-tuple-element.21.refs_0_, f32[10,1,256,512]{3,2,1,0:T(8,128)} %refs_1_.1, f32[9,256,128]{2,1,0:T(8,128)S(1)} %slice_bitcast_fusion.refs_2_, ...), custom_call_target="tpu_custom_call", output_to_operand_aliasing={{}: (9, {})} | custom-call | flops 4529848320 | bytes 15335424 | tf_op jit(solution)/shard_map/update/pallas_call | solution.py:217
  119.6 8.8 %update.3 = f32[10,1,256,512]{3,2,1,0:T(8,128)} custom-call(s32[3]{0:T(128)S(1)} %pad_add_fusion.place, f32[1024,512]{1,0:T(8,128)} %get-tuple-element.21.refs_0_, f32[10,1,256,512]{3,2,1,0:T(8,128)} %update.2.refs_1_, f32[9,256,128]{2,1,0:T(8,128)S(1)} %collective-permute-done.8.refs_2_, ...), custom_call_target="tpu_custom_call", output_to_operand_aliasing={{}: (2, {})} | custom-call | flops 2717908992 | bytes 12976128 | tf_op jit(solution)/shard_map/update/pallas_call | solution.py:217
  (53 shorter events, 10.3 us)
Async XLA Ops:
  1.0 11.0 %collective-permute-start = (f32[1,256,128]{2,1,0:T(8,128)S(1)}, f32[1,256,128]{2,1,0:T(8,128)S(1)}, u32[]{:S(2)}, u32[]{:S(2)}) collective-permute-start(f32[1,256,128]{2,1,0:T(8,128)S(1)} %slice_bitcast_fusion.4), channel_id=1, source_target_pairs={{0,2},{1,3},{2,0},{3,1},{4,6},{5,7},{6,4},{7,5},{8,10},{9,11},{10,... | collective-permute-start | bytes 393224 | tf_op jit(solution)/shard_map/ppermute | solution.py:279
  4.1 12.9 %collective-permute-start.1 = (f32[1,256,128]{2,1,0:T(8,128)S(1)}, f32[1,256,128]{2,1,0:T(8,128)S(1)}, u32[]{:S(2)}, u32[]{:S(2)}) collective-permute-start(f32[1,256,128]{2,1,0:T(8,128)S(1)} %slice_bitcast_fusion.4), channel_id=1, source_target_pairs={{0,4},{1,5},{2,6},{3,7},{4,0},{5,1},{6,2},{7,3},{8,12},{9,13},{10,... | collective-permute-start | bytes 393224 | tf_op jit(solution)/shard_map/ppermute | solution.py:279
  6.7 10.4 %collective-permute-start.2 = (f32[1,256,128]{2,1,0:T(8,128)S(1)}, f32[1,256,128]{2,1,0:T(8,128)S(1)}, u32[]{:S(2)}, u32[]{:S(2)}) collective-permute-start(f32[1,256,128]{2,1,0:T(8,128)S(1)} %slice_bitcast_fusion.4), channel_id=1, source_target_pairs={{0,6},{1,7},{2,4},{3,5},{4,2},{5,3},{6,0},{7,1},{8,14},{9,15},{10,... | collective-permute-start | bytes 393224 | tf_op jit(solution)/shard_map/ppermute | solution.py:279
  8.6 34.4 %collective-permute-start.7 = (f32[256,512]{1,0:T(8,128)}, f32[256,512]{1,0:T(8,128)}, u32[]{:S(2)}, u32[]{:S(2)}) collective-permute-start(f32[256,512]{1,0:T(8,128)} %slice_bitcast_fusion.3.refs_4_), channel_id=1, source_target_pairs={{0,16},{8,24},{16,0},{24,8},{1,17},{9,25},{17,1},{25,9},{2,18},{10... | collective-permute-start | bytes 1572872 | tf_op jit(solution)/shard_map/ppermute | solution.py:245
  10.3 28.1 %collective-permute-start.14 = (f32[5,256,128]{2,1,0:T(8,128)S(1)}, f32[5,256,128]{2,1,0:T(8,128)S(1)}, u32[]{:S(2)}, u32[]{:S(2)}) collective-permute-start(f32[5,256,128]{2,1,0:T(8,128)S(1)} %slice_bitcast_fusion.1), channel_id=1, source_target_pairs={{0,1},{1,0},{2,3},{3,2},{4,5},{5,4},{6,7},{7,6},{8,9},{9,8},{10,11... | collective-permute-start | bytes 1966088 | tf_op jit(solution)/shard_map/ppermute | solution.py:279
  12.0 28.0 %collective-permute-start.4 = (f32[9,256,128]{2,1,0:T(8,128)S(1)}, f32[9,256,128]{2,1,0:T(8,128)S(1)}, u32[]{:S(2)}, u32[]{:S(2)}) collective-permute-start(f32[9,256,128]{2,1,0:T(8,128)S(1)} %slice_bitcast_fusion.refs_2_), channel_id=1, source_target_pairs={{2,4},{3,5},{4,2},{5,3},{10,12},{11,13},{12,10},{13,11},{18,20},{1... | collective-permute-start | bytes 3538952 | tf_op jit(solution)/shard_map/ppermute | solution.py:282
  17.1 24.6 %collective-permute-start.5 = (f32[9,256,128]{2,1,0:T(8,128)S(1)}, f32[9,256,128]{2,1,0:T(8,128)}, u32[]{:S(2)}, u32[]{:S(2)}) collective-permute-start(f32[9,256,128]{2,1,0:T(8,128)S(1)} %slice_bitcast_fusion.refs_2_), channel_id=1, source_target_pairs={{0,2},{1,3},{2,0},{3,1},{4,6},{5,7},{6,4},{7,5},{8,10},{9,11},{10,... | collective-permute-start | bytes 3538952 | tf_op jit(solution)/shard_map/ppermute | solution.py:279
  17.1 19.9 %collective-permute-start.3 = (f32[4,256,128]{2,1,0:T(8,128)S(1)}, f32[4,256,128]{2,1,0:T(8,128)S(1)}, u32[]{:S(2)}, u32[]{:S(2)}) collective-permute-start(f32[4,256,128]{2,1,0:T(8,128)S(1)} %pad_maximum_fusion), channel_id=1, source_target_pairs={{0,1},{1,0},{2,3},{3,2},{4,5},{5,4},{6,7},{7,6},{8,9},{9,8},{10,11... | collective-permute-start | bytes 1572872 | tf_op jit(solution)/shard_map/ppermute | solution.py:279
  37.9 23.3 %collective-permute-start.9 = (f32[8,256,128]{2,1,0:T(8,128)}, f32[8,256,128]{2,1,0:T(8,128)}, u32[]{:S(2)}, u32[]{:S(2)}) collective-permute-start(f32[8,256,128]{2,1,0:T(8,128)} %constant_dynamic-update-slice_fusion.refs_0_), channel_id=1, source_target_pairs={{0,16},{8,24},{16,0},{24,8},{1,17},{9,25},{17,1},{25,9},{2,18},{10... | collective-permute-start | bytes 3145736 | tf_op jit(solution)/shard_map/ppermute | solution.py:245
  38.5 11.8 %collective-permute-start.15 = (f32[4,256,128]{2,1,0:T(8,128)S(1)}, f32[4,256,128]{2,1,0:T(8,128)S(1)}, u32[]{:S(2)}, u32[]{:S(2)}) collective-permute-start(f32[4,256,128]{2,1,0:T(8,128)S(1)} %slice_bitcast_fusion.2), channel_id=1, source_target_pairs={{0,1},{1,0},{2,3},{3,2},{4,5},{5,4},{6,7},{7,6},{8,9},{9,8},{10,11... | collective-permute-start | bytes 1572872 | tf_op jit(solution)/shard_map/ppermute | solution.py:279
  41.7 28.8 %collective-permute-start.6 = (f32[9,256,128]{2,1,0:T(8,128)S(1)}, f32[9,256,128]{2,1,0:T(8,128)S(1)}, u32[]{:S(2)}, u32[]{:S(2)}) collective-permute-start(f32[9,256,128]{2,1,0:T(8,128)S(1)} %collective-permute-done.4.refs_5_), channel_id=1, source_target_pairs={{2,0},{3,1},{4,6},{5,7},{10,8},{11,9},{12,14},{13,15},{18,16},{19,... | collective-permute-start | bytes 3538952 | tf_op jit(solution)/shard_map/ppermute | solution.py:282
  43.0 27.5 %collective-permute-start.8 = (f32[9,256,128]{2,1,0:T(8,128)}, f32[9,256,128]{2,1,0:T(8,128)S(1)}, u32[]{:S(2)}, u32[]{:S(2)}) collective-permute-start(f32[9,256,128]{2,1,0:T(8,128)} %collective-permute-done.5.refs_3_), channel_id=1, source_target_pairs={{2,4},{3,5},{4,2},{5,3},{10,12},{11,13},{12,10},{13,11},{18,20},{1... | collective-permute-start | bytes 3538952 | tf_op jit(solution)/shard_map/ppermute | solution.py:282
  51.4 25.3 %collective-permute-start.16 = (f32[9,256,128]{2,1,0:T(8,128)}, f32[9,256,128]{2,1,0:T(8,128)}, u32[]{:S(2)}, u32[]{:S(2)}) collective-permute-start(f32[9,256,128]{2,1,0:T(8,128)} %collective-permute-done.5.refs_3_), channel_id=1, source_target_pairs={{0,1},{1,0},{2,3},{3,2},{4,5},{5,4},{6,7},{7,6},{8,9},{9,8},{10,11... | collective-permute-start | bytes 3538952 | tf_op jit(solution)/shard_map/ppermute | solution.py:279
  52.7 26.7 %collective-permute-start.10 = (f32[8,256,128]{2,1,0:T(8,128)}, f32[8,256,128]{2,1,0:T(8,128)}, u32[]{:S(2)}, u32[]{:S(2)}) collective-permute-start(f32[8,256,128]{2,1,0:T(8,128)} %constant_dynamic-update-slice_fusion.refs_0_), channel_id=1, source_target_pairs={{0,8},{8,0},{16,24},{24,16},{1,9},{9,1},{17,25},{25,17},{2,10},{10... | collective-permute-start | bytes 3145736 | tf_op jit(solution)/shard_map/ppermute | solution.py:245
  61.2 18.1 %collective-permute-start.11 = (f32[8,256,128]{2,1,0:T(8,128)}, f32[8,256,128]{2,1,0:T(8,128)}, u32[]{:S(2)}, u32[]{:S(2)}) collective-permute-start(f32[8,256,128]{2,1,0:T(8,128)} %collective-permute-done.9.refs_1_), channel_id=1, source_target_pairs={{0,8},{8,0},{16,24},{24,16},{1,9},{9,1},{17,25},{25,17},{2,10},{10... | collective-permute-start | bytes 3145736 | tf_op jit(solution)/shard_map/ppermute | solution.py:245
  70.5 7.7 %collective-permute-start.12 = (f32[256,512]{1,0:T(8,128)}, f32[256,512]{1,0:T(8,128)}, u32[]{:S(2)}, u32[]{:S(2)}) collective-permute-start(f32[256,512]{1,0:T(8,128)} %slice_bitcast_fusion.3.refs_4_), channel_id=1, source_target_pairs={{0,8},{8,0},{16,24},{24,16},{1,9},{9,1},{17,25},{25,17},{2,10},{10... | collective-permute-start | bytes 1572872 | tf_op jit(solution)/shard_map/ppermute | solution.py:245
  70.5 8.9 %collective-permute-start.13 = (f32[256,512]{1,0:T(8,128)}, f32[256,512]{1,0:T(8,128)}, u32[]{:S(2)}, u32[]{:S(2)}) collective-permute-start(f32[256,512]{1,0:T(8,128)} %collective-permute-done.7.refs_5_), channel_id=1, source_target_pairs={{0,8},{8,0},{16,24},{24,16},{1,9},{9,1},{17,25},{25,17},{2,10},{10... | collective-permute-start | bytes 1572872 | tf_op jit(solution)/shard_map/ppermute | solution.py:245
  76.6 30.8 %collective-permute-start.17 = (f32[9,256,128]{2,1,0:T(8,128)S(1)}, f32[9,256,128]{2,1,0:T(8,128)S(1)}, u32[]{:S(2)}, u32[]{:S(2)}) collective-permute-start(f32[9,256,128]{2,1,0:T(8,128)S(1)} %collective-permute-done.8.refs_2_), channel_id=1, source_target_pairs={{2,0},{3,1},{4,6},{5,7},{10,8},{11,9},{12,14},{13,15},{18,16},{19,... | collective-permute-start | bytes 3538952 | tf_op jit(solution)/shard_map/ppermute | solution.py:282
  78.2 29.3 %copy-start.3 = (f32[9,256,128]{2,1,0:T(8,128)S(1)}, f32[9,256,128]{2,1,0:T(8,128)}, u32[]{:S(2)}) copy-start(f32[9,256,128]{2,1,0:T(8,128)} %copy-done.2) | copy-start | bytes 3538948
  78.2 18.5 %collective-permute-start.18 = (f32[6,256,128]{2,1,0:T(8,128)S(1)}, f32[6,256,128]{2,1,0:T(8,128)S(1)}, u32[]{:S(2)}, u32[]{:S(2)}) collective-permute-start(f32[6,256,128]{2,1,0:T(8,128)S(1)} %slice.50), channel_id=1, source_target_pairs={{0,1},{1,0},{2,3},{3,2},{4,5},{5,4},{6,7},{7,6},{8,9},{9,8},{10,11... | collective-permute-start | bytes 2359304 | tf_op jit(solution)/shard_map/ppermute | solution.py:279
  96.7 11.9 %copy-start.1 = (f32[9,256,128]{2,1,0:T(8,128)S(1)}, f32[9,256,128]{2,1,0:T(8,128)}, u32[]{:S(2)}) copy-start(f32[9,256,128]{2,1,0:T(8,128)} %copy-done) | copy-start | bytes 3538948
  96.7 22.8 %collective-permute-start.20 = (f32[6,256,128]{2,1,0:T(8,128)S(1)}, f32[6,256,128]{2,1,0:T(8,128)S(1)}, u32[]{:S(2)}, u32[]{:S(2)}) collective-permute-start(f32[6,256,128]{2,1,0:T(8,128)S(1)} %collective-permute-done.18.refs_4_), channel_id=1, source_target_pairs={{0,2},{1,3},{2,0},{3,1},{4,6},{5,7},{6,4},{7,5},{8,10},{9,11},{10,... | collective-permute-start | bytes 2359304 | tf_op jit(solution)/shard_map/ppermute | solution.py:279
  99.6 19.6 %collective-permute-start.19 = (f32[3,256,128]{2,1,0:T(8,128)S(1)}, f32[3,256,128]{2,1,0:T(8,128)S(1)}, u32[]{:S(2)}, u32[]{:S(2)}) collective-permute-start(f32[3,256,128]{2,1,0:T(8,128)S(1)} %slice.51), channel_id=1, source_target_pairs={{0,1},{1,0},{2,3},{3,2},{4,5},{5,4},{6,7},{7,6},{8,9},{9,8},{10,11... | collective-permute-start | bytes 1179656 | tf_op jit(solution)/shard_map/ppermute | solution.py:279
  107.5 12.1 %collective-permute-start.21 = (f32[3,256,128]{2,1,0:T(8,128)S(1)}, f32[3,256,128]{2,1,0:T(8,128)S(1)}, u32[]{:S(2)}, u32[]{:S(2)}) collective-permute-start(f32[3,256,128]{2,1,0:T(8,128)S(1)} %slice_select_fusion), channel_id=1, source_target_pairs={{0,1},{1,0},{2,3},{3,2},{4,5},{5,4},{6,7},{7,6},{8,9},{9,8},{10,11... | collective-permute-start | bytes 1179656 | tf_op jit(solution)/shard_map/ppermute | solution.py:279
  (3 other events, 21.6 us)

commit v4 on v3

v4 whole, which is shorter than its diff:
```python
import functools
import math

import jax
import jax.numpy as jnp
from jax import lax
from jax.experimental import pallas as pl
from jax.experimental.pallas import tpu as pltpu
from jax.sharding import PartitionSpec as P

F32, BF16 = jnp.float32, jnp.bfloat16
TILE, HALF, BASE = 128, 64, 16


def split(value):
    high = value.astype(BF16)
    return high, (value - high.astype(F32)).astype(BF16)


def product(a_high, a_low, b_high, b_low):
    wide = jnp.concatenate([a_high, a_low, a_high], axis=1)
    tall = jnp.concatenate([b_high, b_high, b_low], axis=0)
    return jnp.dot(wide, tall, preferred_element_type=F32)


def half_inverses(tiles):
    count = len(tiles)
    lane = lax.broadcasted_iota(jnp.int32, (BASE, TILE), 1)
    row = lax.broadcasted_iota(jnp.int32, (BASE, TILE), 0)
    packed = []
    for tile in tiles:
        kept = jnp.zeros((BASE, TILE), F32)
        for g in range(TILE // BASE):
            kept = jnp.where(lane // BASE == g, tile[g * BASE : (g + 1) * BASE], kept)
        packed.append(kept)
    packed = jnp.concatenate(packed, axis=0)
    k = lax.broadcasted_iota(jnp.int32, (TILE, TILE), 0)
    m = lax.broadcasted_iota(jnp.int32, (TILE, TILE), 1)
    high, rest = split(packed)
    middle = (packed - high.astype(F32) - rest.astype(F32)).astype(BF16)
    parts = jnp.concatenate([high, rest, middle], axis=1)
    columns = []
    for j in range(BASE):
        spread = (k == (m // BASE) * BASE + j).astype(F32).astype(BF16)
        tall = jnp.concatenate([spread] * 3, axis=0)
        columns.append(jnp.dot(parts, tall, preferred_element_type=F32).reshape(count, BASE, TILE))
    diagonal = columns[0]
    for j in range(1, BASE):
        diagonal = jnp.where(row[None] == j, columns[j], diagonal)
    scale = 1.0 / diagonal
    x = jnp.where((row == lane % BASE)[None], scale, 0.0)
    for j in range(BASE - 1):
        x = x - jnp.where(row[None] > j, columns[j] * scale, 0.0) * x[:, j : j + 1]
    inverses = [
        jnp.where(k // BASE == m // BASE, jnp.concatenate([x[t]] * (TILE // BASE), axis=0), 0.0) for t in range(count)
    ]
    size = BASE
    while size < HALF:
        joined = (k // (2 * size) == m // (2 * size)) & (k // size != m // size)
        halves = [split(w) for w in inverses]
        crossed = [product(*w, *split(jnp.where(joined, tile, 0.0))) for w, tile in zip(halves, tiles)]
        inverses = [w - product(*split(c), *h) for w, c, h in zip(inverses, crossed, halves)]
        size *= 2
    return inverses


def solve_kernel(codes, counts, place, head_refs, side_refs, y_ref, out_ref, l_high, l_low, y_high, y_low, landing, head_sems, side_sems):
    rows, width = head_refs[0].shape[-2:]
    window = l_high.shape[0]
    per_row = len(head_refs) // len(codes)
    head_copies, side_copies = [], []
    for c, code in enumerate(codes):
        at = pl.ds(pl.multiple_of((place[0] ^ code) * rows, rows), rows)
        begin = c * sum(counts)
        for p in range(per_row):
            n = c * per_row + p
            into = landing.at[begin : begin + counts[p]]
            head_copies.append(pltpu.make_async_copy(head_refs[n], into, head_sems.at[n]))
            begin += counts[p]
        side_copies.append(pltpu.make_async_copy(side_refs[c], y_ref.at[at], side_sems.at[c]))
    for copy in head_copies + side_copies:
        copy.start()
    for c, code in enumerate(codes):
        at = pl.ds(pl.multiple_of((place[0] ^ code) * rows, rows), rows)
        n = c * sum(counts)
        for p in range(per_row):
            head_copies[c * per_row + p].wait()
            for k in range(counts[p]):
                across = pl.ds(pl.multiple_of(place[1 + n] * width, width), width)
                high, low = split(landing[n])
                l_high[at, across] = high
                l_low[at, across] = low
                n += 1
    for copy in side_copies:
        copy.wait()
    tiles = []
    for t in range(window // TILE):
        at = slice(t * TILE, (t + 1) * TILE)
        tiles.append(l_high[at, at].astype(F32) + l_low[at, at].astype(F32))
    inverses = half_inverses(tiles)
    ready = y_ref[:TILE]
    for t in range(window // TILE):
        begin = t * TILE
        value = ready
        if t:
            before = slice(begin - TILE, begin)
            at = slice(begin, begin + TILE)
            value = value - product(l_high[at, before], l_low[at, before], *solved)
        w = inverses[t]
        answers = []
        for h in range(TILE // HALF):
            part = value[h * HALF : (h + 1) * HALF]
            at = slice(begin + h * HALF, begin + (h + 1) * HALF)
            if h:
                inside = slice(begin, begin + h * HALF)
                part = part - product(l_high[at, inside], l_low[at, inside], *answers[0])
            inv = w[h * HALF : (h + 1) * HALF, h * HALF : (h + 1) * HALF]
            answer = product(*split(inv), *split(part))
            y_ref[at] = answer
            answers.append(split(answer))
            if h == 0 and begin + TILE < window:
                following = slice(begin + TILE, begin + 2 * TILE)
                ready = y_ref[following]
                if t:
                    ready = ready - product(
                        l_high[following, :begin], l_low[following, :begin], y_high[:begin], y_low[:begin]
                    )
        solved = [jnp.concatenate(both, axis=0) for both in zip(*answers)]
        y_high[begin : begin + TILE], y_low[begin : begin + TILE] = solved
    at = pl.ds(pl.multiple_of(place[0] * rows, rows), rows)
    copy = pltpu.make_async_copy(y_ref.at[at], out_ref.at[0, 0], side_sems.at[0])
    copy.start()
    copy.wait()


def solve(position, codes, heads, owners, sides, out_shape):
    counts = [part.shape[0] for part in heads[0]]
    window = sum(counts) * heads[0][0].shape[-1]
    columns = sides[0].shape[-1]
    flat = [part for parts in heads for part in parts]
    total = len(flat)
    place = jnp.concatenate([position] + [owners] * len(codes))

    def kernel(place, *refs):
        head_refs, side_refs = refs[:total], refs[total : total + len(codes)]
        solve_kernel(codes, counts, place, head_refs, side_refs, *refs[total + len(codes) :])

    return pl.pallas_call(
        kernel,
        out_shape=[jax.ShapeDtypeStruct((window, columns), F32), jax.ShapeDtypeStruct(out_shape, F32)],
        in_specs=[pl.BlockSpec(memory_space=pltpu.SMEM)] + [pl.BlockSpec(memory_space=pl.ANY)] * (total + len(codes)),
        out_specs=[pl.BlockSpec(memory_space=pltpu.VMEM), pl.BlockSpec(memory_space=pl.ANY)],
        scratch_shapes=[
            pltpu.VMEM((window, window), BF16),
            pltpu.VMEM((window, window), BF16),
            pltpu.VMEM((window, columns), BF16),
            pltpu.VMEM((window, columns), BF16),
            pltpu.VMEM((len(codes) * sum(counts), *flat[0].shape[1:]), F32),
            pltpu.SemaphoreType.DMA((total,)),
            pltpu.SemaphoreType.DMA((len(codes),)),
        ],
        compiler_params=pltpu.CompilerParams(vmem_limit_bytes=48 << 20),
        cost_estimate=pl.CostEstimate(
            flops=30 * window * window * columns, bytes_accessed=4 * window * (window + 2 * columns), transcendentals=0
        ),
        name="solve",
    )(place, *flat, *sides)


def load(places, begin, widths, y_ref, y_high, y_low):
    at = 0
    for n, width in enumerate(widths):
        high, low = split(y_ref[pl.ds(pl.multiple_of(places[begin + n] * width, width), width)])
        y_high[at : at + width] = high
        y_low[at : at + width] = low
        at += width


def update_first(y, places, pieces, base):
    flat = [part for piece in pieces for part in piece]
    blocks, rows, _ = flat[0].shape
    columns = y.shape[1]
    widths = [piece[0].shape[-1] for piece in pieces]
    count, depth = len(flat), sum(widths)
    step = next(n for n in (3, 2, 1) if blocks % n == 0)

    def kernel(place, y_ref, base_ref, *refs):
        piece_refs, (acc_ref, y_high, y_low, done) = refs[:count], refs[count:]
        load(place, 0, widths, y_ref, y_high, y_low)
        done[0] = 0

        def body(base_block, *piece_blocks):
            for n in range(step):
                parts = iter(piece_blocks)
                wide = [sum(next(parts)[n] for _ in piece) for piece in pieces]
                high, low = split(jnp.concatenate(wide, axis=1))
                value = base_block[n, 0] - product(high, low, y_high[...], y_low[...])
                acc_ref[done[0] + n] = value
            done[0] += step

        pltpu.emit_pipeline(
            body,
            grid=(blocks // step,),
            in_specs=[pl.BlockSpec((step, 1, rows, columns), lambda i: (i, 0, 0, 0))]
            + [pl.BlockSpec((step, rows, part.shape[-1]), lambda i: (i, 0, 0)) for part in flat],
        )(base_ref.at[pl.ds(1, blocks)], *piece_refs)

    anywhere = pl.BlockSpec(memory_space=pl.ANY)
    inside = pl.BlockSpec(memory_space=pltpu.VMEM)
    return pl.pallas_call(
        kernel,
        out_shape=jax.ShapeDtypeStruct((blocks, rows, columns), F32),
        in_specs=[pl.BlockSpec(memory_space=pltpu.SMEM), inside] + [anywhere] * (1 + count),
        out_specs=inside,
        scratch_shapes=[
            pltpu.VMEM((depth, columns), BF16),
            pltpu.VMEM((depth, columns), BF16),
            pltpu.SMEM((1,), jnp.int32),
        ],
        compiler_params=pltpu.CompilerParams(vmem_limit_bytes=44 << 20),
        cost_estimate=pl.CostEstimate(
            flops=6 * blocks * rows * depth * columns,
            bytes_accessed=4 * blocks * rows * (depth + 2 * columns),
            transcendentals=0,
        ),
        name="update_first",
    )(places, y, base, *flat)


def update_last(y, places, pieces, acc, target):
    flat = [part for piece in pieces for laid in piece for part in laid]
    blocks, rows, columns = acc.shape
    widths = [piece[0][0].shape[-1] for piece in pieces]
    count, depth = len(flat), sum(widths)

    def kernel(place, y_ref, acc_ref, *refs):
        piece_refs = refs[:count]
        out_ref, y_high, y_low, done, sems = refs[count + 1 :]
        load(place, 0, widths, y_ref, y_high, y_low)
        copies = []
        for i in range(blocks):
            at, wide = 0, []
            for piece in pieces:
                value = 0
                for laid in piece:
                    begin = 0
                    for part in laid:
                        if begin <= i < begin + part.shape[0]:
                            value = value + piece_refs[at][i - begin]
                        begin += part.shape[0]
                        at += 1
                wide.append(value)
            high, low = split(jnp.concatenate(wide, axis=1))
            done[i] = acc_ref[i] - product(high, low, y_high[...], y_low[...])
            copies.append(pltpu.make_async_copy(done.at[i], out_ref.at[i + 1, 0], sems.at[i]))
            copies[-1].start()
        for copy in copies:
            copy.wait()

    anywhere = pl.BlockSpec(memory_space=pl.ANY)
    inside = pl.BlockSpec(memory_space=pltpu.VMEM)
    return pl.pallas_call(
        kernel,
        out_shape=jax.ShapeDtypeStruct(target.shape, F32),
        in_specs=[pl.BlockSpec(memory_space=pltpu.SMEM)] + [inside] * (2 + count) + [anywhere],
        out_specs=anywhere,
        scratch_shapes=[
            pltpu.VMEM((depth, columns), BF16),
            pltpu.VMEM((depth, columns), BF16),
            pltpu.VMEM((blocks, rows, columns), F32),
            pltpu.SemaphoreType.DMA((blocks,)),
        ],
        input_output_aliases={3 + count: 0},
        compiler_params=pltpu.CompilerParams(vmem_limit_bytes=44 << 20),
        cost_estimate=pl.CostEstimate(
            flops=6 * blocks * rows * depth * columns,
            bytes_accessed=4 * blocks * rows * (depth + 2 * columns),
            transcendentals=0,
        ),
        name="update_last",
    )(places, y, acc, *flat, target)


def over_row(block, size):
    codes, held = [0], [block]
    bit = size // 2
    while bit:
        pairs = [(n, n ^ bit) for n in range(size)]
        held = held + [lax.ppermute(value, "row", pairs) for value in held]
        codes = codes + [code ^ bit for code in codes]
        bit //= 2
    return codes, held


def after(value, *others):
    return lax.optimization_barrier((value, *others))[0]


def body(right_sides, factor):
    row_count, real_count = lax.axis_size("row"), lax.axis_size("real")
    position = lax.axis_index("row")[None]
    mine = factor[:, 0]
    if real_count != 8:
        codes, sides = over_row(right_sides[0, 0], row_count)
        head = lax.all_gather(mine[0], "real", axis=1, tiled=True)
        codes, heads = over_row(head[None], row_count)
        whole = jnp.zeros((1,), jnp.int32)
        y, result = solve(position, codes, [[part] for part in heads], whole, sides, right_sides.shape)
        rest = lax.all_gather(mine[1:], "real", axis=2, tiled=True)
        half = rest.shape[2] // 2
        acc = update_first(y, whole, [[rest[:, :, :half]]], right_sides)
        return update_last(y, whole + 1, [[[rest[:, :, half:]]]], acc, result)

    lanes = 2
    here = lax.axis_index("real")
    z, side = here // lanes, here % lanes
    outer = (z == 0) | (z == 3)
    pick = lambda a, b: jnp.where(outer, a, b)
    mirror = 3 - z
    partner = z ^ 1
    other = mirror ^ 1
    spot = lambda at, which: at * lanes + which

    def hop(value, bits):
        return lax.ppermute(value, "real", [(n, n ^ bits) for n in range(real_count)])

    def move(value, pairs):
        return lax.ppermute(value, "real", [(a * lanes + n, b * lanes + n) for a, b in pairs for n in range(lanes)])

    ends = lambda value: hop(value, 2)
    lane = lambda value: hop(value, 1)
    middle = lambda value: move(value, [(1, 2), (2, 1)])
    out = lambda value: move(value, [(1, 0), (2, 3)])

    trailing = mine.shape[0] - 1
    cut = (trailing + 1) // 2
    own = mine[1:]
    halves = [slice(0, cut), slice(cut, trailing)]

    h_own = mine[0:1]
    h_line = [h_own] + [hop(h_own, bits) for bits in (2, 4, 6)]
    middle_row = (trailing + 1) // 2
    s1 = [lane(own[:middle_row]), None]
    start = after(own, h_line[1])
    e1, m1 = ends(start), middle(start)
    far_head = h_line[2]
    h_line = jnp.concatenate(h_line)
    h_all = jnp.concatenate([h_line, lane(h_line)])
    s1[1] = lane(after(own[middle_row:], s1[0]))
    s1 = jnp.concatenate(s1)
    owners = jnp.stack([here ^ bits for bits in (0, 2, 4, 6, 1, 3, 5, 7)]).astype(jnp.int32)
    codes, sides = over_row(after(right_sides, far_head)[0, 0], row_count)
    codes, heads = over_row(after(h_all, sides[1]), row_count)

    first, second = halves
    o2 = out(after(m1, e1))
    m2 = middle(e1)
    s2 = lane(after(e1, s1))
    o3 = [out(m2[rows]) for rows in halves]
    both = [pick(o2, m2)[rows] for rows in halves]
    s3 = [lane(after(both[0], s2)), None]
    heads[0] = after(heads[0], o2, m2)
    y, result = solve(position, codes, [[part] for part in heads], owners, sides, right_sides.shape)
    s3[1] = lane(after(both[1], y))
    last = [ends(after(s3[0], y, o3[1])), lane(pick(o3[1], m1[second]))]

    near_y = [
        here,
        spot(partner, side),
        spot(z, 1 - side),
        pick(spot(other, side), spot(mirror, side)),
        spot(partner, 1 - side),
    ]
    far_y = [pick(spot(mirror, side), spot(other, side)), spot(other, 1 - side), spot(mirror, 1 - side)]
    near_y, far_y = (jnp.stack(places).astype(jnp.int32) for places in (near_y, far_y))
    acc = update_first(y, near_y, [[own], [e1], [s1], [m1, o2], [s2]], right_sides)
    return update_last(y, far_y, [[[m2], o3], [s3], [last]], acc, result)


def solution(mesh):
    placed = (P(None, "row", None, "real"), P(None, "row", None, "real"))
    return jax.shard_map(
        body, mesh=mesh, in_specs=placed, out_specs=P(None, "row", None, "real"), check_vma=False
    )
```

time: 129 us -> 125 us (0.969)
  Pallas kernels: 36.7 us -> 30.7 us
  waiting for transfers between devices: 58.5 us -> 54.2 us
  starting transfers between devices: 24.8 us -> 28.6 us
  local copies, waits for them, and re-layouts: 7.95 us -> 10.7 us
    ppermute x12, waiting for transfers between devices: 33.8 us -> 25.7 us  [hop(): lax.ppermute(value, 'real', [(n, n ^ bits) for n in range(real_count)])]
    ppermute x4 -> x5, waiting for transfers between devices: 16.1 us -> 20.6 us  [move(): lax.ppermute(value, 'real', [(a * lanes + n, b * lanes + n) for a, b in p...]
    pallas_call x1, Pallas kernels: 17.3 us -> 13.1 us  [solve(): pl.pallas_call(kernel, out_shape=[jax.ShapeDtypeStruct((window, columns),...]
    pallas_call x2, Pallas kernels: 19.3 us -> 17.6 us  [the longest x1 11 us: update_first(): pl.pallas_call(kernel, out_shape=jax.ShapeDtypeStruct((blocks, rows, colu...]
    ppermute x12, starting transfers between devices: 17.8 us -> 19.5 us  [hop(): lax.ppermute(value, 'real', [(n, n ^ bits) for n in range(real_count)])]
    unnamed x15 -> x17, local copies, waits for them, and re-layouts: 3.75 us -> 5.32 us
    ppermute x4 -> x5, starting transfers between devices: 4.21 us -> 5.64 us  [move(): lax.ppermute(value, 'real', [(a * lanes + n, b * lanes + n) for a, b in p...]
  transfers between devices with their start and end apart: 22 -> 23, of which waited for: 9 -> 8; matrix products, arithmetic and copies ran while one was open for 5% -> 6% of each run, Pallas kernels for 22% -> 19%
where the time goes in v4:
time: 125 us
  waiting for transfers between devices  54.2 us (43%)
  Pallas kernels  30.7 us (25%)
  starting transfers between devices  28.6 us (23%)
  local copies, waits for them, and re-layouts  10.7 us (9%)
    ppermute x12, waiting for transfers between devices, hop(): lax.ppermute(value, 'real', [(n, n ^ bits) for n in range(real_count)])  25.7 us
    ppermute x5, waiting for transfers between devices, move(): lax.ppermute(value, 'real', [(a * lanes + n, b * lanes + n) for a, b in p...  20.6 us
    ppermute x12, starting transfers between devices, hop(): lax.ppermute(value, 'real', [(n, n ^ bits) for n in range(real_count)])  19.5 us
    pallas_call x1, Pallas kernels, solve(): pl.pallas_call(kernel, out_shape=[jax.ShapeDtypeStruct((window, columns),...  13.1 us
    pallas_call x1, Pallas kernels, update_first(): pl.pallas_call(kernel, out_shape=jax.ShapeDtypeStruct((blocks, rows, colu...  11 us
    ppermute x6, waiting for transfers between devices, over_row(): held = held + [lax.ppermute(value, 'row', pairs) for value in held]  7.83 us
    pallas_call x1, Pallas kernels, update_last(): pl.pallas_call(kernel, out_shape=jax.ShapeDtypeStruct(target.shape, F32),...  6.52 us
    ppermute x5, starting transfers between devices, move(): lax.ppermute(value, 'real', [(a * lanes + n, b * lanes + n) for a, b in p...  5.64 us
  transfers between devices with their start and end apart: 23, of which 8 were waited for; matrix products, arithmetic and copies ran while one was open for 6% of the time, Pallas kernels for 19%

profile of v4, /device:TPU:0, one launch (start us, length us, event | category | flops | bytes accessed | tf_op | source)
XLA Modules:
  0.0 124.8 jit_solution(17336466062251502187)
XLA Ops:
  1.0 3.1 %collective-permute-start = (f32[1,256,128]{2,1,0:T(8,128)S(1)}, f32[1,256,128]{2,1,0:T(8,128)S(1)}, u32[]{:S(2)}, u32[]{:S(2)}) collective-permute-start(f32[1,256,128]{2,1,0:T(8,128)S(1)} %slice_bitcast_fusion.4), channel_id=1, source_target_pairs={{0,2},{1,3},{2,0},{3,1},{4,6},{5,7},{6,4},{7,5},{8,10},{9,11},{10,... | collective-permute-start | bytes 393224 | tf_op jit(solution)/shard_map/ppermute | solution.py:325
  4.1 2.6 %collective-permute-start.1 = (f32[1,256,128]{2,1,0:T(8,128)S(1)}, f32[1,256,128]{2,1,0:T(8,128)S(1)}, u32[]{:S(2)}, u32[]{:S(2)}) collective-permute-start(f32[1,256,128]{2,1,0:T(8,128)S(1)} %slice_bitcast_fusion.4), channel_id=1, source_target_pairs={{0,4},{1,5},{2,6},{3,7},{4,0},{5,1},{6,2},{7,3},{8,12},{9,13},{10,... | collective-permute-start | bytes 393224 | tf_op jit(solution)/shard_map/ppermute | solution.py:325
  7.8 1.8 %collective-permute-start.14 = (f32[5,256,128]{2,1,0:T(8,128)S(1)}, f32[5,256,128]{2,1,0:T(8,128)S(1)}, u32[]{:S(2)}, u32[]{:S(2)}) collective-permute-start(f32[5,256,128]{2,1,0:T(8,128)S(1)} %slice_bitcast_fusion.1), channel_id=1, source_target_pairs={{0,1},{1,0},{2,3},{3,2},{4,5},{5,4},{6,7},{7,6},{8,9},{9,8},{10,11... | collective-permute-start | bytes 1966088 | tf_op jit(solution)/shard_map/ppermute | solution.py:325
  10.5 3.6 %collective-permute-start.6 = (f32[9,256,128]{2,1,0:T(8,128)S(1)}, f32[9,256,128]{2,1,0:T(8,128)}, u32[]{:S(2)}, u32[]{:S(2)}) collective-permute-start(f32[9,256,128]{2,1,0:T(8,128)S(1)} %slice_bitcast_fusion.refs_0_), channel_id=1, source_target_pairs={{0,2},{1,3},{2,0},{3,1},{4,6},{5,7},{6,4},{7,5},{8,10},{9,11},{10,... | collective-permute-start | bytes 3538952 | tf_op jit(solution)/shard_map/ppermute | solution.py:325
  14.0 3.0 %collective-permute-done.1 = f32[1,256,128]{2,1,0:T(8,128)S(1)} collective-permute-done((f32[1,256,128]{2,1,0:T(8,128)S(1)}, f32[1,256,128]{2,1,0:T(8,128)S(1)}, u32[]{:S(2)}, u32[]{:S(2)}) %collective-permute-start.1) | collective-permute-done | bytes 131104 | tf_op jit(solution)/shard_map/ppermute | solution.py:325
  17.1 1.6 %collective-permute-start.3 = (f32[4,256,128]{2,1,0:T(8,128)S(1)}, f32[4,256,128]{2,1,0:T(8,128)S(1)}, u32[]{:S(2)}, u32[]{:S(2)}) collective-permute-start(f32[4,256,128]{2,1,0:T(8,128)S(1)} %pad_maximum_fusion), channel_id=1, source_target_pairs={{0,1},{1,0},{2,3},{3,2},{4,5},{5,4},{6,7},{7,6},{8,9},{9,8},{10,11... | collective-permute-start | bytes 1572872 | tf_op jit(solution)/shard_map/ppermute | solution.py:325
  18.7 1.9 %slice_bitcast_fusion.3.refs_4_ = f32[256,512]{1,0:T(8,128)} fusion(f32[10,1,256,512]{3,2,1,0:T(8,128)} %base_ref.1), kind=kLoop, calls=%fused_computation.6 | loop fusion | bytes 1048576 | tf_op jit(solution)/shard_map/squeeze | solution.py:352
  24.7 10.4 %collective-permute-done.3 = f32[4,256,128]{2,1,0:T(8,128)S(1)} collective-permute-done((f32[4,256,128]{2,1,0:T(8,128)S(1)}, f32[4,256,128]{2,1,0:T(8,128)S(1)}, u32[]{:S(2)}, u32[]{:S(2)}) %collective-permute-start.3) | collective-permute-done | bytes 524320 | tf_op jit(solution)/shard_map/ppermute | solution.py:325
  35.9 1.5 %collective-permute-start.9 = (f32[8,256,128]{2,1,0:T(8,128)}, f32[8,256,128]{2,1,0:T(8,128)}, u32[]{:S(2)}, u32[]{:S(2)}) collective-permute-start(f32[8,256,128]{2,1,0:T(8,128)} %constant_dynamic-update-slice_fusion.refs_0_), channel_id=1, source_target_pairs={{0,16},{8,24},{16,0},{24,8},{1,17},{9,25},{17,1},{25,9},{2,18},{10... | collective-permute-start | bytes 3145736 | tf_op jit(solution)/shard_map/ppermute | solution.py:289
  37.4 1.6 %collective-permute-start.15 = (f32[4,256,128]{2,1,0:T(8,128)S(1)}, f32[4,256,128]{2,1,0:T(8,128)S(1)}, u32[]{:S(2)}, u32[]{:S(2)}) collective-permute-start(f32[4,256,128]{2,1,0:T(8,128)S(1)} %slice_bitcast_fusion.2), channel_id=1, source_target_pairs={{0,1},{1,0},{2,3},{3,2},{4,5},{5,4},{6,7},{7,6},{8,9},{9,8},{10,11... | collective-permute-start | bytes 1572872 | tf_op jit(solution)/shard_map/ppermute | solution.py:325
  39.0 2.3 %collective-permute-done.6.refs_1_ = f32[9,256,128]{2,1,0:T(8,128)} collective-permute-done((f32[9,256,128]{2,1,0:T(8,128)S(1)}, f32[9,256,128]{2,1,0:T(8,128)}, u32[]{:S(2)}, u32[]{:S(2)}) %collective-permute-start.6) | collective-permute-done | bytes 1179680 | tf_op jit(solution)/shard_map/ppermute | solution.py:325
  43.5 5.8 %collective-permute-done.15 = f32[4,256,128]{2,1,0:T(8,128)S(1)} collective-permute-done((f32[4,256,128]{2,1,0:T(8,128)S(1)}, f32[4,256,128]{2,1,0:T(8,128)S(1)}, u32[]{:S(2)}, u32[]{:S(2)}) %collective-permute-start.15) | collective-permute-done | bytes 524320 | tf_op jit(solution)/shard_map/ppermute | solution.py:325
  50.4 1.5 %collective-permute-start.16 = (f32[9,256,128]{2,1,0:T(8,128)}, f32[9,256,128]{2,1,0:T(8,128)}, u32[]{:S(2)}, u32[]{:S(2)}) collective-permute-start(f32[9,256,128]{2,1,0:T(8,128)} %collective-permute-done.6.refs_1_), channel_id=1, source_target_pairs={{0,1},{1,0},{2,3},{3,2},{4,5},{5,4},{6,7},{7,6},{8,9},{9,8},{10,11... | collective-permute-start | bytes 3538952 | tf_op jit(solution)/shard_map/ppermute | solution.py:325
  51.9 7.8 %collective-permute-done.9.refs_1_ = f32[8,256,128]{2,1,0:T(8,128)} collective-permute-done((f32[8,256,128]{2,1,0:T(8,128)}, f32[8,256,128]{2,1,0:T(8,128)}, u32[]{:S(2)}, u32[]{:S(2)}) %collective-permute-start.9) | collective-permute-done | bytes 1048608 | tf_op jit(solution)/shard_map/ppermute | solution.py:289
  59.7 10.9 %collective-permute-done.7.refs_4_ = f32[9,256,128]{2,1,0:T(8,128)S(1)} collective-permute-done((f32[9,256,128]{2,1,0:T(8,128)S(1)}, f32[9,256,128]{2,1,0:T(8,128)S(1)}, u32[]{:S(2)}, u32[]{:S(2)}) %collective-permute-start.7) | collective-permute-done | bytes 1179680 | tf_op jit(solution)/shard_map/ppermute | solution.py:328
  71.6 4.1 %collective-permute-done.16.refs_5_ = f32[9,256,128]{2,1,0:T(8,128)} collective-permute-done((f32[9,256,128]{2,1,0:T(8,128)}, f32[9,256,128]{2,1,0:T(8,128)}, u32[]{:S(2)}, u32[]{:S(2)}) %collective-permute-start.16) | collective-permute-done | bytes 1179680 | tf_op jit(solution)/shard_map/ppermute | solution.py:325
  77.1 1.6 %collective-permute-start.18 = (f32[4,256,128]{2,1,0:T(8,128)S(1)}, f32[4,256,128]{2,1,0:T(8,128)S(1)}, u32[]{:S(2)}, u32[]{:S(2)}) collective-permute-start(f32[4,256,128]{2,1,0:T(8,128)S(1)} %slice.62), channel_id=1, source_target_pairs={{2,0},{3,1},{4,6},{5,7},{10,8},{11,9},{12,14},{13,15},{18,16},{19,... | collective-permute-start | bytes 1572872 | tf_op jit(solution)/shard_map/ppermute | solution.py:328
  78.7 1.6 %collective-permute-start.19 = (f32[5,256,128]{2,1,0:T(8,128)S(1)}, f32[5,256,128]{2,1,0:T(8,128)S(1)}, u32[]{:S(2)}, u32[]{:S(2)}) collective-permute-start(f32[5,256,128]{2,1,0:T(8,128)S(1)} %slice.63), channel_id=1, source_target_pairs={{0,1},{1,0},{2,3},{3,2},{4,5},{5,4},{6,7},{7,6},{8,9},{9,8},{10,11... | collective-permute-start | bytes 1966088 | tf_op jit(solution)/shard_map/ppermute | solution.py:325
  80.3 13.1 %solve.1 = (f32[1024,512]{1,0:T(8,128)}, f32[10,1,256,512]{3,2,1,0:T(8,128)}) custom-call(s32[33]{0:T(128)S(1)} %concatenate.14.place, f32[8,256,128]{2,1,0:T(8,128)} %constant_dynamic-update-slice_fusion.refs_0_, f32[8,256,128]{2,1,0:T(8,128)} %collective-permute-done.9.refs_1_, f32[8,256,128]{2,1,0:T(8,128)} %collective-permute-done.10.refs_2_, ...), custom_call_target="tpu_custom_call" | custom-call | flops 16106127360 | bytes 8388608 | tf_op jit(solution)/shard_map/solve/pallas_call | solution.py:148
  94.0 9.7 %collective-permute-done.18.refs_2_ = f32[4,256,128]{2,1,0:T(8,128)S(1)} collective-permute-done((f32[4,256,128]{2,1,0:T(8,128)S(1)}, f32[4,256,128]{2,1,0:T(8,128)S(1)}, u32[]{:S(2)}, u32[]{:S(2)}) %collective-permute-start.18) | collective-permute-done | bytes 524320 | tf_op jit(solution)/shard_map/ppermute | solution.py:328
  103.8 1.6 %collective-permute-start.22 = (f32[4,256,128]{2,1,0:T(8,128)S(1)}, f32[4,256,128]{2,1,0:T(8,128)S(1)}, u32[]{:S(2)}, u32[]{:S(2)}) collective-permute-start(f32[4,256,128]{2,1,0:T(8,128)S(1)} %slice_select_fusion), channel_id=1, source_target_pairs={{0,1},{1,0},{2,3},{3,2},{4,5},{5,4},{6,7},{7,6},{8,9},{9,8},{10,11... | collective-permute-start | bytes 1572872 | tf_op jit(solution)/shard_map/ppermute | solution.py:325
  105.5 1.6 %copy-done = f32[1024,512]{1,0:T(8,128)S(1)} copy-done((f32[1024,512]{1,0:T(8,128)S(1)}, f32[1024,512]{1,0:T(8,128)}, u32[]{:S(2)}) %copy-start) | copy-done | bytes 2097176
  107.1 11.0 %update_first.1.acc_ref = f32[9,256,512]{2,1,0:T(8,128)} custom-call(s32[5]{0:T(128)S(1)} %stack.69.place, f32[1024,512]{1,0:T(8,128)S(1)} %copy-done, f32[10,1,256,512]{3,2,1,0:T(8,128)} %base_ref.1, f32[9,256,128]{2,1,0:T(8,128)S(1)} %slice_bitcast_fusion.refs_0_, f32[9,256,128]{2,1,0:T(8,128)} %collective-permute-done.6.refs_1_, ...), custom_call_target="tpu_custom_call" | custom-call | flops 4529848320 | bytes 15335424 | tf_op jit(solution)/shard_map/update_first/pallas_call | solution.py:210
  118.1 6.5 %update_last.1 = f32[10,1,256,512]{3,2,1,0:T(8,128)} custom-call(s32[3]{0:T(128)S(1)} %pad_add_fusion.place, f32[1024,512]{1,0:T(8,128)S(1)} %copy-done, f32[9,256,512]{2,1,0:T(8,128)} %update_first.1.acc_ref, f32[9,256,128]{2,1,0:T(8,128)S(1)} %collective-permute-done.8.refs_0_, ...), custom_call_target="tpu_custom_call", output_to_operand_aliasing={{}: (10, {})} | custom-call | flops 2717908992 | bytes 12976128 | tf_op jit(solution)/shard_map/update_last/pallas_call | solution.py:262
  (59 shorter events, 14.2 us)
Async XLA Ops:
  1.0 8.7 %collective-permute-start = (f32[1,256,128]{2,1,0:T(8,128)S(1)}, f32[1,256,128]{2,1,0:T(8,128)S(1)}, u32[]{:S(2)}, u32[]{:S(2)}) collective-permute-start(f32[1,256,128]{2,1,0:T(8,128)S(1)} %slice_bitcast_fusion.4), channel_id=1, source_target_pairs={{0,2},{1,3},{2,0},{3,1},{4,6},{5,7},{6,4},{7,5},{8,10},{9,11},{10,... | collective-permute-start | bytes 393224 | tf_op jit(solution)/shard_map/ppermute | solution.py:325
  4.1 12.9 %collective-permute-start.1 = (f32[1,256,128]{2,1,0:T(8,128)S(1)}, f32[1,256,128]{2,1,0:T(8,128)S(1)}, u32[]{:S(2)}, u32[]{:S(2)}) collective-permute-start(f32[1,256,128]{2,1,0:T(8,128)S(1)} %slice_bitcast_fusion.4), channel_id=1, source_target_pairs={{0,4},{1,5},{2,6},{3,7},{4,0},{5,1},{6,2},{7,3},{8,12},{9,13},{10,... | collective-permute-start | bytes 393224 | tf_op jit(solution)/shard_map/ppermute | solution.py:325
  6.7 10.4 %collective-permute-start.2 = (f32[1,256,128]{2,1,0:T(8,128)S(1)}, f32[1,256,128]{2,1,0:T(8,128)S(1)}, u32[]{:S(2)}, u32[]{:S(2)}) collective-permute-start(f32[1,256,128]{2,1,0:T(8,128)S(1)} %slice_bitcast_fusion.4), channel_id=1, source_target_pairs={{0,6},{1,7},{2,4},{3,5},{4,2},{5,3},{6,0},{7,1},{8,14},{9,15},{10,... | collective-permute-start | bytes 393224 | tf_op jit(solution)/shard_map/ppermute | solution.py:325
  7.8 29.6 %collective-permute-start.14 = (f32[5,256,128]{2,1,0:T(8,128)S(1)}, f32[5,256,128]{2,1,0:T(8,128)S(1)}, u32[]{:S(2)}, u32[]{:S(2)}) collective-permute-start(f32[5,256,128]{2,1,0:T(8,128)S(1)} %slice_bitcast_fusion.1), channel_id=1, source_target_pairs={{0,1},{1,0},{2,3},{3,2},{4,5},{5,4},{6,7},{7,6},{8,9},{9,8},{10,11... | collective-permute-start | bytes 1966088 | tf_op jit(solution)/shard_map/ppermute | solution.py:325
  9.7 29.3 %collective-permute-start.5 = (f32[9,256,128]{2,1,0:T(8,128)S(1)}, f32[9,256,128]{2,1,0:T(8,128)S(1)}, u32[]{:S(2)}, u32[]{:S(2)}) collective-permute-start(f32[9,256,128]{2,1,0:T(8,128)S(1)} %slice_bitcast_fusion.refs_0_), channel_id=1, source_target_pairs={{2,4},{3,5},{4,2},{5,3},{10,12},{11,13},{12,10},{13,11},{18,20},{1... | collective-permute-start | bytes 3538952 | tf_op jit(solution)/shard_map/ppermute | solution.py:328
  10.5 30.9 %collective-permute-start.6 = (f32[9,256,128]{2,1,0:T(8,128)S(1)}, f32[9,256,128]{2,1,0:T(8,128)}, u32[]{:S(2)}, u32[]{:S(2)}) collective-permute-start(f32[9,256,128]{2,1,0:T(8,128)S(1)} %slice_bitcast_fusion.refs_0_), channel_id=1, source_target_pairs={{0,2},{1,3},{2,0},{3,1},{4,6},{5,7},{6,4},{7,5},{8,10},{9,11},{10,... | collective-permute-start | bytes 3538952 | tf_op jit(solution)/shard_map/ppermute | solution.py:325
  17.1 18.0 %collective-permute-start.3 = (f32[4,256,128]{2,1,0:T(8,128)S(1)}, f32[4,256,128]{2,1,0:T(8,128)S(1)}, u32[]{:S(2)}, u32[]{:S(2)}) collective-permute-start(f32[4,256,128]{2,1,0:T(8,128)S(1)} %pad_maximum_fusion), channel_id=1, source_target_pairs={{0,1},{1,0},{2,3},{3,2},{4,5},{5,4},{6,7},{7,6},{8,9},{9,8},{10,11... | collective-permute-start | bytes 1572872 | tf_op jit(solution)/shard_map/ppermute | solution.py:325
  20.5 15.4 %collective-permute-start.4 = (f32[256,512]{1,0:T(8,128)}, f32[256,512]{1,0:T(8,128)}, u32[]{:S(2)}, u32[]{:S(2)}) collective-permute-start(f32[256,512]{1,0:T(8,128)} %slice_bitcast_fusion.3.refs_4_), channel_id=1, source_target_pairs={{0,16},{8,24},{16,0},{24,8},{1,17},{9,25},{17,1},{25,9},{2,18},{10... | collective-permute-start | bytes 1572872 | tf_op jit(solution)/shard_map/ppermute | solution.py:289
  35.9 23.8 %collective-permute-start.9 = (f32[8,256,128]{2,1,0:T(8,128)}, f32[8,256,128]{2,1,0:T(8,128)}, u32[]{:S(2)}, u32[]{:S(2)}) collective-permute-start(f32[8,256,128]{2,1,0:T(8,128)} %constant_dynamic-update-slice_fusion.refs_0_), channel_id=1, source_target_pairs={{0,16},{8,24},{16,0},{24,8},{1,17},{9,25},{17,1},{25,9},{2,18},{10... | collective-permute-start | bytes 3145736 | tf_op jit(solution)/shard_map/ppermute | solution.py:289
  37.4 11.9 %collective-permute-start.15 = (f32[4,256,128]{2,1,0:T(8,128)S(1)}, f32[4,256,128]{2,1,0:T(8,128)S(1)}, u32[]{:S(2)}, u32[]{:S(2)}) collective-permute-start(f32[4,256,128]{2,1,0:T(8,128)S(1)} %slice_bitcast_fusion.2), channel_id=1, source_target_pairs={{0,1},{1,0},{2,3},{3,2},{4,5},{5,4},{6,7},{7,6},{8,9},{9,8},{10,11... | collective-permute-start | bytes 1572872 | tf_op jit(solution)/shard_map/ppermute | solution.py:325
  41.4 29.2 %collective-permute-start.7 = (f32[9,256,128]{2,1,0:T(8,128)S(1)}, f32[9,256,128]{2,1,0:T(8,128)S(1)}, u32[]{:S(2)}, u32[]{:S(2)}) collective-permute-start(f32[9,256,128]{2,1,0:T(8,128)S(1)} %collective-permute-done.5.refs_3_), channel_id=1, source_target_pairs={{2,0},{3,1},{4,6},{5,7},{10,8},{11,9},{12,14},{13,15},{18,16},{19,... | collective-permute-start | bytes 3538952 | tf_op jit(solution)/shard_map/ppermute | solution.py:328
  42.7 28.0 %collective-permute-start.8 = (f32[9,256,128]{2,1,0:T(8,128)}, f32[9,256,128]{2,1,0:T(8,128)S(1)}, u32[]{:S(2)}, u32[]{:S(2)}) collective-permute-start(f32[9,256,128]{2,1,0:T(8,128)} %collective-permute-done.6.refs_1_), channel_id=1, source_target_pairs={{2,4},{3,5},{4,2},{5,3},{10,12},{11,13},{12,10},{13,11},{18,20},{1... | collective-permute-start | bytes 3538952 | tf_op jit(solution)/shard_map/ppermute | solution.py:328
  50.4 25.3 %collective-permute-start.16 = (f32[9,256,128]{2,1,0:T(8,128)}, f32[9,256,128]{2,1,0:T(8,128)}, u32[]{:S(2)}, u32[]{:S(2)}) collective-permute-start(f32[9,256,128]{2,1,0:T(8,128)} %collective-permute-done.6.refs_1_), channel_id=1, source_target_pairs={{0,1},{1,0},{2,3},{3,2},{4,5},{5,4},{6,7},{7,6},{8,9},{9,8},{10,11... | collective-permute-start | bytes 3538952 | tf_op jit(solution)/shard_map/ppermute | solution.py:325
  51.9 28.4 %collective-permute-start.10 = (f32[8,256,128]{2,1,0:T(8,128)}, f32[8,256,128]{2,1,0:T(8,128)}, u32[]{:S(2)}, u32[]{:S(2)}) collective-permute-start(f32[8,256,128]{2,1,0:T(8,128)} %constant_dynamic-update-slice_fusion.refs_0_), channel_id=1, source_target_pairs={{0,8},{8,0},{16,24},{24,16},{1,9},{9,1},{17,25},{25,17},{2,10},{10... | collective-permute-start | bytes 3145736 | tf_op jit(solution)/shard_map/ppermute | solution.py:289
  59.7 20.6 %collective-permute-start.11 = (f32[8,256,128]{2,1,0:T(8,128)}, f32[8,256,128]{2,1,0:T(8,128)}, u32[]{:S(2)}, u32[]{:S(2)}) collective-permute-start(f32[8,256,128]{2,1,0:T(8,128)} %collective-permute-done.9.refs_1_), channel_id=1, source_target_pairs={{0,8},{8,0},{16,24},{24,16},{1,9},{9,1},{17,25},{25,17},{2,10},{10... | collective-permute-start | bytes 3145736 | tf_op jit(solution)/shard_map/ppermute | solution.py:289
  70.6 6.5 %collective-permute-start.12 = (f32[256,512]{1,0:T(8,128)}, f32[256,512]{1,0:T(8,128)}, u32[]{:S(2)}, u32[]{:S(2)}) collective-permute-start(f32[256,512]{1,0:T(8,128)} %slice_bitcast_fusion.3.refs_4_), channel_id=1, source_target_pairs={{0,8},{8,0},{16,24},{24,16},{1,9},{9,1},{17,25},{25,17},{2,10},{10... | collective-permute-start | bytes 1572872 | tf_op jit(solution)/shard_map/ppermute | solution.py:289
  70.6 8.1 %collective-permute-start.13 = (f32[256,512]{1,0:T(8,128)}, f32[256,512]{1,0:T(8,128)}, u32[]{:S(2)}, u32[]{:S(2)}) collective-permute-start(f32[256,512]{1,0:T(8,128)} %collective-permute-done.4.refs_5_), channel_id=1, source_target_pairs={{0,8},{8,0},{16,24},{24,16},{1,9},{9,1},{17,25},{25,17},{2,10},{10... | collective-permute-start | bytes 1572872 | tf_op jit(solution)/shard_map/ppermute | solution.py:289
  75.7 42.4 %collective-permute-start.17 = (f32[5,256,128]{2,1,0:T(8,128)S(1)}, f32[5,256,128]{2,1,0:T(8,128)S(1)}, u32[]{:S(2)}, u32[]{:S(2)}) collective-permute-start(f32[5,256,128]{2,1,0:T(8,128)S(1)} %slice.61), channel_id=1, source_target_pairs={{2,0},{3,1},{4,6},{5,7},{10,8},{11,9},{12,14},{13,15},{18,16},{19,... | collective-permute-start | bytes 1966088 | tf_op jit(solution)/shard_map/ppermute | solution.py:328
  77.1 26.7 %copy-start.4 = (f32[9,256,128]{2,1,0:T(8,128)S(1)}, f32[9,256,128]{2,1,0:T(8,128)}, u32[]{:S(2)}) copy-start(f32[9,256,128]{2,1,0:T(8,128)} %copy-done.3) | copy-start | bytes 3538948
  77.1 26.7 %collective-permute-start.18 = (f32[4,256,128]{2,1,0:T(8,128)S(1)}, f32[4,256,128]{2,1,0:T(8,128)S(1)}, u32[]{:S(2)}, u32[]{:S(2)}) collective-permute-start(f32[4,256,128]{2,1,0:T(8,128)S(1)} %slice.62), channel_id=1, source_target_pairs={{2,0},{3,1},{4,6},{5,7},{10,8},{11,9},{12,14},{13,15},{18,16},{19,... | collective-permute-start | bytes 1572872 | tf_op jit(solution)/shard_map/ppermute | solution.py:328
  78.7 25.0 %collective-permute-start.19 = (f32[5,256,128]{2,1,0:T(8,128)S(1)}, f32[5,256,128]{2,1,0:T(8,128)S(1)}, u32[]{:S(2)}, u32[]{:S(2)}) collective-permute-start(f32[5,256,128]{2,1,0:T(8,128)S(1)} %slice.63), channel_id=1, source_target_pairs={{0,1},{1,0},{2,3},{3,2},{4,5},{5,4},{6,7},{7,6},{8,9},{9,8},{10,11... | collective-permute-start | bytes 1966088 | tf_op jit(solution)/shard_map/ppermute | solution.py:325
  93.4 24.7 %collective-permute-start.20 = (f32[4,256,128]{2,1,0:T(8,128)S(1)}, f32[4,256,128]{2,1,0:T(8,128)S(1)}, u32[]{:S(2)}, u32[]{:S(2)}) collective-permute-start(f32[4,256,128]{2,1,0:T(8,128)S(1)} %slice.64), channel_id=1, source_target_pairs={{0,1},{1,0},{2,3},{3,2},{4,5},{5,4},{6,7},{7,6},{8,9},{9,8},{10,11... | collective-permute-start | bytes 1572872 | tf_op jit(solution)/shard_map/ppermute | solution.py:325
  103.8 14.4 %collective-permute-start.21 = (f32[5,256,128]{2,1,0:T(8,128)S(1)}, f32[5,256,128]{2,1,0:T(8,128)S(1)}, u32[]{:S(2)}, u32[]{:S(2)}) collective-permute-start(f32[5,256,128]{2,1,0:T(8,128)S(1)} %collective-permute-done.19.refs_3_), channel_id=1, source_target_pairs={{0,2},{1,3},{2,0},{3,1},{4,6},{5,7},{6,4},{7,5},{8,10},{9,11},{10,... | collective-permute-start | bytes 1966088 | tf_op jit(solution)/shard_map/ppermute | solution.py:325
  103.8 14.3 %collective-permute-start.22 = (f32[4,256,128]{2,1,0:T(8,128)S(1)}, f32[4,256,128]{2,1,0:T(8,128)S(1)}, u32[]{:S(2)}, u32[]{:S(2)}) collective-permute-start(f32[4,256,128]{2,1,0:T(8,128)S(1)} %slice_select_fusion), channel_id=1, source_target_pairs={{0,1},{1,0},{2,3},{3,2},{4,5},{5,4},{6,7},{7,6},{8,9},{9,8},{10,11... | collective-permute-start | bytes 1572872 | tf_op jit(solution)/shard_map/ppermute | solution.py:325
  (5 other events, 34.6 us)

commit v5 on v4

--- a/solution.py
+++ b/solution.py
@@ -209,7 +209,7 @@
     inside = pl.BlockSpec(memory_space=pltpu.VMEM)
     return pl.pallas_call(
         kernel,
-        out_shape=jax.ShapeDtypeStruct((blocks, rows, columns), F32),
+        out_shape=pltpu.VMEM((blocks, rows, columns), F32),
         in_specs=[pl.BlockSpec(memory_space=pltpu.SMEM), inside] + [anywhere] * (1 + count),
         out_specs=inside,
         scratch_shapes=[
@@ -278,7 +278,7 @@
             transcendentals=0,
         ),
         name="update_last",
-    )(places, y, acc, *flat, target)
+    )(places, y, pltpu.with_memory_space_constraint(acc, pltpu.VMEM), *flat, target)
 
 
 def over_row(block, size):
@@ -373,8 +373,9 @@
     ]
     far_y = [pick(spot(mirror, side), spot(other, side)), spot(other, 1 - side), spot(mirror, 1 - side)]
     near_y, far_y = (jnp.stack(places).astype(jnp.int32) for places in (near_y, far_y))
+    inside = lambda parts: [pltpu.with_memory_space_constraint(part, pltpu.VMEM) for part in parts]
     acc = update_first(y, near_y, [[own], [e1], [s1], [m1, o2], [s2]], right_sides)
-    return update_last(y, far_y, [[[m2], o3], [s3], [last]], acc, result)
+    return update_last(y, far_y, [[[m2], o3], [s3], [inside(last)]], acc, result)
 
 
 def solution(mesh):

time: 125 us -> 125 us (level)
  waiting for transfers between devices: 54.2 us -> 57 us
  Pallas kernels: 30.7 us -> 28.4 us
  local copies, waits for them, and re-layouts: 10.7 us -> 9.11 us
  other arithmetic: 0.29 us -> 1.58 us
    unnamed x17 -> x13, local copies, waits for them, and re-layouts: 5.32 us -> 3.74 us
    pallas_call x1, Pallas kernels: 11 us -> 9.67 us  [update_first(): pl.pallas_call(kernel, out_shape=pltpu.VMEM((blocks, rows, columns), F32)...]
    select_n x2, other arithmetic: 0.18 us -> 1.46 us  [body(): pick = lambda a, b: jnp.where(outer, a, b)]
  transfers between devices with their start and end apart: 23 -> 23, of which waited for: 8 -> 10; matrix products, arithmetic and copies ran while one was open for 6% -> 7% of each run, Pallas kernels for 19% -> 18%
where the time goes in v5:
time: 125 us
  waiting for transfers between devices  57 us (46%)
  Pallas kernels  28.4 us (23%)
  starting transfers between devices  28 us (22%)
  local copies, waits for them, and re-layouts  9.11 us (7%)
  other arithmetic  1.58 us (1%)
    ppermute x12, waiting for transfers between devices, hop(): lax.ppermute(value, 'real', [(n, n ^ bits) for n in range(real_count)])  26.5 us
    ppermute x5, waiting for transfers between devices, move(): lax.ppermute(value, 'real', [(a * lanes + n, b * lanes + n) for a, b in p...  21.7 us
    ppermute x12, starting transfers between devices, hop(): lax.ppermute(value, 'real', [(n, n ^ bits) for n in range(real_count)])  19.4 us
    pallas_call x1, Pallas kernels, solve(): pl.pallas_call(kernel, out_shape=[jax.ShapeDtypeStruct((window, columns),...  13 us
    pallas_call x1, Pallas kernels, update_first(): pl.pallas_call(kernel, out_shape=pltpu.VMEM((blocks, rows, columns), F32)...  9.67 us
    ppermute x6, waiting for transfers between devices, over_row(): held = held + [lax.ppermute(value, 'row', pairs) for value in held]  8.81 us
    pallas_call x1, Pallas kernels, update_last(): pl.pallas_call(kernel, out_shape=jax.ShapeDtypeStruct(target.shape, F32),...  5.7 us
    ppermute x5, starting transfers between devices, move(): lax.ppermute(value, 'real', [(a * lanes + n, b * lanes + n) for a, b in p...  5.64 us
  transfers between devices with their start and end apart: 23, of which 10 were waited for; matrix products, arithmetic and copies ran while one was open for 7% of the time, Pallas kernels for 18%

profile of v5, /device:TPU:0, one launch (start us, length us, event | category | flops | bytes accessed | tf_op | source)
XLA Modules:
  0.0 124.5 jit_solution(13642729599108553508)
XLA Ops:
  1.0 3.1 %collective-permute-start = (f32[1,256,128]{2,1,0:T(8,128)S(1)}, f32[1,256,128]{2,1,0:T(8,128)S(1)}, u32[]{:S(2)}, u32[]{:S(2)}) collective-permute-start(f32[1,256,128]{2,1,0:T(8,128)S(1)} %slice_bitcast_fusion.4), channel_id=1, source_target_pairs={{0,2},{1,3},{2,0},{3,1},{4,6},{5,7},{6,4},{7,5},{8,10},{9,11},{10,... | collective-permute-start | bytes 393224 | tf_op jit(solution)/shard_map/ppermute | solution.py:325
  4.1 2.6 %collective-permute-start.1 = (f32[1,256,128]{2,1,0:T(8,128)S(1)}, f32[1,256,128]{2,1,0:T(8,128)S(1)}, u32[]{:S(2)}, u32[]{:S(2)}) collective-permute-start(f32[1,256,128]{2,1,0:T(8,128)S(1)} %slice_bitcast_fusion.4), channel_id=1, source_target_pairs={{0,4},{1,5},{2,6},{3,7},{4,0},{5,1},{6,2},{7,3},{8,12},{9,13},{10,... | collective-permute-start | bytes 393224 | tf_op jit(solution)/shard_map/ppermute | solution.py:325
  7.8 1.8 %collective-permute-start.14 = (f32[5,256,128]{2,1,0:T(8,128)S(1)}, f32[5,256,128]{2,1,0:T(8,128)S(1)}, u32[]{:S(2)}, u32[]{:S(2)}) collective-permute-start(f32[5,256,128]{2,1,0:T(8,128)S(1)} %slice_bitcast_fusion.1), channel_id=1, source_target_pairs={{0,1},{1,0},{2,3},{3,2},{4,5},{5,4},{6,7},{7,6},{8,9},{9,8},{10,11... | collective-permute-start | bytes 1966088 | tf_op jit(solution)/shard_map/ppermute | solution.py:325
  10.5 3.6 %collective-permute-start.6 = (f32[9,256,128]{2,1,0:T(8,128)S(1)}, f32[9,256,128]{2,1,0:T(8,128)}, u32[]{:S(2)}, u32[]{:S(2)}) collective-permute-start(f32[9,256,128]{2,1,0:T(8,128)S(1)} %slice_bitcast_fusion.refs_0_), channel_id=1, source_target_pairs={{0,2},{1,3},{2,0},{3,1},{4,6},{5,7},{6,4},{7,5},{8,10},{9,11},{10,... | collective-permute-start | bytes 3538952 | tf_op jit(solution)/shard_map/ppermute | solution.py:325
  14.0 3.0 %collective-permute-done.1 = f32[1,256,128]{2,1,0:T(8,128)S(1)} collective-permute-done((f32[1,256,128]{2,1,0:T(8,128)S(1)}, f32[1,256,128]{2,1,0:T(8,128)S(1)}, u32[]{:S(2)}, u32[]{:S(2)}) %collective-permute-start.1) | collective-permute-done | bytes 131104 | tf_op jit(solution)/shard_map/ppermute | solution.py:325
  17.1 1.6 %collective-permute-start.3 = (f32[4,256,128]{2,1,0:T(8,128)S(1)}, f32[4,256,128]{2,1,0:T(8,128)S(1)}, u32[]{:S(2)}, u32[]{:S(2)}) collective-permute-start(f32[4,256,128]{2,1,0:T(8,128)S(1)} %pad_maximum_fusion), channel_id=1, source_target_pairs={{0,1},{1,0},{2,3},{3,2},{4,5},{5,4},{6,7},{7,6},{8,9},{9,8},{10,11... | collective-permute-start | bytes 1572872 | tf_op jit(solution)/shard_map/ppermute | solution.py:325
  18.7 1.9 %slice_bitcast_fusion.3.refs_4_ = f32[256,512]{1,0:T(8,128)} fusion(f32[10,1,256,512]{3,2,1,0:T(8,128)} %base_ref.1), kind=kLoop, calls=%fused_computation.6 | loop fusion | bytes 1048576 | tf_op jit(solution)/shard_map/squeeze | solution.py:352
  20.6 1.5 %collective-permute-start.4 = (f32[256,512]{1,0:T(8,128)}, f32[256,512]{1,0:T(8,128)}, u32[]{:S(2)}, u32[]{:S(2)}) collective-permute-start(f32[256,512]{1,0:T(8,128)} %slice_bitcast_fusion.3.refs_4_), channel_id=1, source_target_pairs={{0,16},{8,24},{16,0},{24,8},{1,17},{9,25},{17,1},{25,9},{2,18},{10... | collective-permute-start | bytes 1572872 | tf_op jit(solution)/shard_map/ppermute | solution.py:289
  24.7 10.4 %collective-permute-done.3 = f32[4,256,128]{2,1,0:T(8,128)S(1)} collective-permute-done((f32[4,256,128]{2,1,0:T(8,128)S(1)}, f32[4,256,128]{2,1,0:T(8,128)S(1)}, u32[]{:S(2)}, u32[]{:S(2)}) %collective-permute-start.3) | collective-permute-done | bytes 524320 | tf_op jit(solution)/shard_map/ppermute | solution.py:325
  35.9 1.5 %collective-permute-start.9 = (f32[8,256,128]{2,1,0:T(8,128)}, f32[8,256,128]{2,1,0:T(8,128)}, u32[]{:S(2)}, u32[]{:S(2)}) collective-permute-start(f32[8,256,128]{2,1,0:T(8,128)} %constant_dynamic-update-slice_fusion.refs_0_), channel_id=1, source_target_pairs={{0,16},{8,24},{16,0},{24,8},{1,17},{9,25},{17,1},{25,9},{2,18},{10... | collective-permute-start | bytes 3145736 | tf_op jit(solution)/shard_map/ppermute | solution.py:289
  37.4 1.6 %collective-permute-start.15 = (f32[4,256,128]{2,1,0:T(8,128)S(1)}, f32[4,256,128]{2,1,0:T(8,128)S(1)}, u32[]{:S(2)}, u32[]{:S(2)}) collective-permute-start(f32[4,256,128]{2,1,0:T(8,128)S(1)} %slice_bitcast_fusion.2), channel_id=1, source_target_pairs={{0,1},{1,0},{2,3},{3,2},{4,5},{5,4},{6,7},{7,6},{8,9},{9,8},{10,11... | collective-permute-start | bytes 1572872 | tf_op jit(solution)/shard_map/ppermute | solution.py:325
  39.0 2.3 %collective-permute-done.6.refs_1_ = f32[9,256,128]{2,1,0:T(8,128)} collective-permute-done((f32[9,256,128]{2,1,0:T(8,128)S(1)}, f32[9,256,128]{2,1,0:T(8,128)}, u32[]{:S(2)}, u32[]{:S(2)}) %collective-permute-start.6) | collective-permute-done | bytes 1179680 | tf_op jit(solution)/shard_map/ppermute | solution.py:325
  43.5 5.8 %collective-permute-done.15 = f32[4,256,128]{2,1,0:T(8,128)S(1)} collective-permute-done((f32[4,256,128]{2,1,0:T(8,128)S(1)}, f32[4,256,128]{2,1,0:T(8,128)S(1)}, u32[]{:S(2)}, u32[]{:S(2)}) %collective-permute-start.15) | collective-permute-done | bytes 524320 | tf_op jit(solution)/shard_map/ppermute | solution.py:325
  49.3 1.6 %collective-permute-start.16 = (f32[9,256,128]{2,1,0:T(8,128)}, f32[9,256,128]{2,1,0:T(8,128)}, u32[]{:S(2)}, u32[]{:S(2)}) collective-permute-start(f32[9,256,128]{2,1,0:T(8,128)} %collective-permute-done.6.refs_1_), channel_id=1, source_target_pairs={{0,1},{1,0},{2,3},{3,2},{4,5},{5,4},{6,7},{7,6},{8,9},{9,8},{10,11... | collective-permute-start | bytes 3538952 | tf_op jit(solution)/shard_map/ppermute | solution.py:325
  50.9 8.8 %collective-permute-done.9.refs_1_ = f32[8,256,128]{2,1,0:T(8,128)} collective-permute-done((f32[8,256,128]{2,1,0:T(8,128)}, f32[8,256,128]{2,1,0:T(8,128)}, u32[]{:S(2)}, u32[]{:S(2)}) %collective-permute-start.9) | collective-permute-done | bytes 1048608 | tf_op jit(solution)/shard_map/ppermute | solution.py:289
  59.7 10.9 %collective-permute-done.7.refs_4_ = f32[9,256,128]{2,1,0:T(8,128)S(1)} collective-permute-done((f32[9,256,128]{2,1,0:T(8,128)S(1)}, f32[9,256,128]{2,1,0:T(8,128)S(1)}, u32[]{:S(2)}, u32[]{:S(2)}) %collective-permute-start.7) | collective-permute-done | bytes 1179680 | tf_op jit(solution)/shard_map/ppermute | solution.py:328
  76.1 1.6 %collective-permute-start.18 = (f32[4,256,128]{2,1,0:T(8,128)S(1)}, f32[4,256,128]{2,1,0:T(8,128)S(1)}, u32[]{:S(2)}, u32[]{:S(2)}) collective-permute-start(f32[4,256,128]{2,1,0:T(8,128)S(1)} %slice.62), channel_id=1, source_target_pairs={{2,0},{3,1},{4,6},{5,7},{10,8},{11,9},{12,14},{13,15},{18,16},{19,... | collective-permute-start | bytes 1572872 | tf_op jit(solution)/shard_map/ppermute | solution.py:328
  77.7 1.6 %collective-permute-start.19 = (f32[5,256,128]{2,1,0:T(8,128)S(1)}, f32[5,256,128]{2,1,0:T(8,128)S(1)}, u32[]{:S(2)}, u32[]{:S(2)}) collective-permute-start(f32[5,256,128]{2,1,0:T(8,128)S(1)} %slice.63), channel_id=1, source_target_pairs={{0,1},{1,0},{2,3},{3,2},{4,5},{5,4},{6,7},{7,6},{8,9},{9,8},{10,11... | collective-permute-start | bytes 1966088 | tf_op jit(solution)/shard_map/ppermute | solution.py:325
  79.3 13.0 %solve.1 = (f32[1024,512]{1,0:T(8,128)}, f32[10,1,256,512]{3,2,1,0:T(8,128)}) custom-call(s32[33]{0:T(128)S(1)} %concatenate.14.place, f32[8,256,128]{2,1,0:T(8,128)} %constant_dynamic-update-slice_fusion.refs_0_, f32[8,256,128]{2,1,0:T(8,128)} %collective-permute-done.9.refs_1_, f32[8,256,128]{2,1,0:T(8,128)} %collective-permute-done.10.refs_2_, ...), custom_call_target="tpu_custom_call" | custom-call | flops 16106127360 | bytes 8388608 | tf_op jit(solution)/shard_map/solve/pallas_call | solution.py:148
  92.9 10.8 %collective-permute-done.18.refs_2_ = f32[4,256,128]{2,1,0:T(8,128)S(1)} collective-permute-done((f32[4,256,128]{2,1,0:T(8,128)S(1)}, f32[4,256,128]{2,1,0:T(8,128)S(1)}, u32[]{:S(2)}, u32[]{:S(2)}) %collective-permute-start.18) | collective-permute-done | bytes 524320 | tf_op jit(solution)/shard_map/ppermute | solution.py:328
  103.8 1.5 %collective-permute-start.22 = (f32[4,256,128]{2,1,0:T(8,128)S(1)}, f32[4,256,128]{2,1,0:T(8,128)S(1)}, u32[]{:S(2)}, u32[]{:S(2)}) collective-permute-start(f32[4,256,128]{2,1,0:T(8,128)S(1)} %slice_select_fusion), channel_id=1, source_target_pairs={{0,1},{1,0},{2,3},{3,2},{4,5},{5,4},{6,7},{7,6},{8,9},{9,8},{10,11... | collective-permute-start | bytes 1572872 | tf_op jit(solution)/shard_map/ppermute | solution.py:325
  105.3 9.7 %update_first.1.acc_ref = f32[9,256,512]{2,1,0:T(8,128)S(1)} custom-call(s32[5]{0:T(128)S(1)} %stack.69.place, f32[1024,512]{1,0:T(8,128)} %get-tuple-element.22.y_ref, f32[10,1,256,512]{3,2,1,0:T(8,128)} %base_ref.1, f32[9,256,128]{2,1,0:T(8,128)S(1)} %slice_bitcast_fusion.refs_0_, f32[9,256,128]{2,1,0:T(8,128)} %collective-permute-done.6.refs_1_, ...), custom_call_target="tpu_custom_call" | custom-call | flops 4529848320 | bytes 15335424 | tf_op jit(solution)/shard_map/update_first/pallas_call | solution.py:210
  116.3 2.4 %collective-permute-done.21.refs_5_ = f32[5,256,128]{2,1,0:T(8,128)S(1)} collective-permute-done((f32[5,256,128]{2,1,0:T(8,128)S(1)}, f32[5,256,128]{2,1,0:T(8,128)S(1)}, u32[]{:S(2)}, u32[]{:S(2)}) %collective-permute-start.21) | collective-permute-done | bytes 655392 | tf_op jit(solution)/shard_map/ppermute | solution.py:325
  118.7 5.7 %update_last.1 = f32[10,1,256,512]{3,2,1,0:T(8,128)} custom-call(s32[3]{0:T(128)S(1)} %pad_add_fusion.place, f32[1024,512]{1,0:T(8,128)} %get-tuple-element.22.y_ref, f32[9,256,512]{2,1,0:T(8,128)S(1)} %update_first.1.acc_ref, f32[9,256,128]{2,1,0:T(8,128)S(1)} %collective-permute-done.8.refs_0_, ...), custom_call_target="tpu_custom_call", output_to_operand_aliasing={{}: (10, {})} | custom-call | flops 2717908992 | bytes 12976128 | tf_op jit(solution)/shard_map/update_last/pallas_call | solution.py:262
  (55 shorter events, 16.1 us)
Async XLA Ops:
  1.0 8.7 %collective-permute-start = (f32[1,256,128]{2,1,0:T(8,128)S(1)}, f32[1,256,128]{2,1,0:T(8,128)S(1)}, u32[]{:S(2)}, u32[]{:S(2)}) collective-permute-start(f32[1,256,128]{2,1,0:T(8,128)S(1)} %slice_bitcast_fusion.4), channel_id=1, source_target_pairs={{0,2},{1,3},{2,0},{3,1},{4,6},{5,7},{6,4},{7,5},{8,10},{9,11},{10,... | collective-permute-start | bytes 393224 | tf_op jit(solution)/shard_map/ppermute | solution.py:325
  4.1 12.9 %collective-permute-start.1 = (f32[1,256,128]{2,1,0:T(8,128)S(1)}, f32[1,256,128]{2,1,0:T(8,128)S(1)}, u32[]{:S(2)}, u32[]{:S(2)}) collective-permute-start(f32[1,256,128]{2,1,0:T(8,128)S(1)} %slice_bitcast_fusion.4), channel_id=1, source_target_pairs={{0,4},{1,5},{2,6},{3,7},{4,0},{5,1},{6,2},{7,3},{8,12},{9,13},{10,... | collective-permute-start | bytes 393224 | tf_op jit(solution)/shard_map/ppermute | solution.py:325
  6.7 10.4 %collective-permute-start.2 = (f32[1,256,128]{2,1,0:T(8,128)S(1)}, f32[1,256,128]{2,1,0:T(8,128)S(1)}, u32[]{:S(2)}, u32[]{:S(2)}) collective-permute-start(f32[1,256,128]{2,1,0:T(8,128)S(1)} %slice_bitcast_fusion.4), channel_id=1, source_target_pairs={{0,6},{1,7},{2,4},{3,5},{4,2},{5,3},{6,0},{7,1},{8,14},{9,15},{10,... | collective-permute-start | bytes 393224 | tf_op jit(solution)/shard_map/ppermute | solution.py:325
  7.8 29.6 %collective-permute-start.14 = (f32[5,256,128]{2,1,0:T(8,128)S(1)}, f32[5,256,128]{2,1,0:T(8,128)S(1)}, u32[]{:S(2)}, u32[]{:S(2)}) collective-permute-start(f32[5,256,128]{2,1,0:T(8,128)S(1)} %slice_bitcast_fusion.1), channel_id=1, source_target_pairs={{0,1},{1,0},{2,3},{3,2},{4,5},{5,4},{6,7},{7,6},{8,9},{9,8},{10,11... | collective-permute-start | bytes 1966088 | tf_op jit(solution)/shard_map/ppermute | solution.py:325
  9.7 29.3 %collective-permute-start.5 = (f32[9,256,128]{2,1,0:T(8,128)S(1)}, f32[9,256,128]{2,1,0:T(8,128)S(1)}, u32[]{:S(2)}, u32[]{:S(2)}) collective-permute-start(f32[9,256,128]{2,1,0:T(8,128)S(1)} %slice_bitcast_fusion.refs_0_), channel_id=1, source_target_pairs={{2,4},{3,5},{4,2},{5,3},{10,12},{11,13},{12,10},{13,11},{18,20},{1... | collective-permute-start | bytes 3538952 | tf_op jit(solution)/shard_map/ppermute | solution.py:328
  10.5 30.9 %collective-permute-start.6 = (f32[9,256,128]{2,1,0:T(8,128)S(1)}, f32[9,256,128]{2,1,0:T(8,128)}, u32[]{:S(2)}, u32[]{:S(2)}) collective-permute-start(f32[9,256,128]{2,1,0:T(8,128)S(1)} %slice_bitcast_fusion.refs_0_), channel_id=1, source_target_pairs={{0,2},{1,3},{2,0},{3,1},{4,6},{5,7},{6,4},{7,5},{8,10},{9,11},{10,... | collective-permute-start | bytes 3538952 | tf_op jit(solution)/shard_map/ppermute | solution.py:325
  17.1 17.9 %collective-permute-start.3 = (f32[4,256,128]{2,1,0:T(8,128)S(1)}, f32[4,256,128]{2,1,0:T(8,128)S(1)}, u32[]{:S(2)}, u32[]{:S(2)}) collective-permute-start(f32[4,256,128]{2,1,0:T(8,128)S(1)} %pad_maximum_fusion), channel_id=1, source_target_pairs={{0,1},{1,0},{2,3},{3,2},{4,5},{5,4},{6,7},{7,6},{8,9},{9,8},{10,11... | collective-permute-start | bytes 1572872 | tf_op jit(solution)/shard_map/ppermute | solution.py:325
  20.6 15.3 %collective-permute-start.4 = (f32[256,512]{1,0:T(8,128)}, f32[256,512]{1,0:T(8,128)}, u32[]{:S(2)}, u32[]{:S(2)}) collective-permute-start(f32[256,512]{1,0:T(8,128)} %slice_bitcast_fusion.3.refs_4_), channel_id=1, source_target_pairs={{0,16},{8,24},{16,0},{24,8},{1,17},{9,25},{17,1},{25,9},{2,18},{10... | collective-permute-start | bytes 1572872 | tf_op jit(solution)/shard_map/ppermute | solution.py:289
  35.9 23.8 %collective-permute-start.9 = (f32[8,256,128]{2,1,0:T(8,128)}, f32[8,256,128]{2,1,0:T(8,128)}, u32[]{:S(2)}, u32[]{:S(2)}) collective-permute-start(f32[8,256,128]{2,1,0:T(8,128)} %constant_dynamic-update-slice_fusion.refs_0_), channel_id=1, source_target_pairs={{0,16},{8,24},{16,0},{24,8},{1,17},{9,25},{17,1},{25,9},{2,18},{10... | collective-permute-start | bytes 3145736 | tf_op jit(solution)/shard_map/ppermute | solution.py:289
  37.4 11.9 %collective-permute-start.15 = (f32[4,256,128]{2,1,0:T(8,128)S(1)}, f32[4,256,128]{2,1,0:T(8,128)S(1)}, u32[]{:S(2)}, u32[]{:S(2)}) collective-permute-start(f32[4,256,128]{2,1,0:T(8,128)S(1)} %slice_bitcast_fusion.2), channel_id=1, source_target_pairs={{0,1},{1,0},{2,3},{3,2},{4,5},{5,4},{6,7},{7,6},{8,9},{9,8},{10,11... | collective-permute-start | bytes 1572872 | tf_op jit(solution)/shard_map/ppermute | solution.py:325
  41.4 29.2 %collective-permute-start.7 = (f32[9,256,128]{2,1,0:T(8,128)S(1)}, f32[9,256,128]{2,1,0:T(8,128)S(1)}, u32[]{:S(2)}, u32[]{:S(2)}) collective-permute-start(f32[9,256,128]{2,1,0:T(8,128)S(1)} %collective-permute-done.5.refs_3_), channel_id=1, source_target_pairs={{2,0},{3,1},{4,6},{5,7},{10,8},{11,9},{12,14},{13,15},{18,16},{19,... | collective-permute-start | bytes 3538952 | tf_op jit(solution)/shard_map/ppermute | solution.py:328
  42.7 28.0 %collective-permute-start.8 = (f32[9,256,128]{2,1,0:T(8,128)}, f32[9,256,128]{2,1,0:T(8,128)S(1)}, u32[]{:S(2)}, u32[]{:S(2)}) collective-permute-start(f32[9,256,128]{2,1,0:T(8,128)} %collective-permute-done.6.refs_1_), channel_id=1, source_target_pairs={{2,4},{3,5},{4,2},{5,3},{10,12},{11,13},{12,10},{13,11},{18,20},{1... | collective-permute-start | bytes 3538952 | tf_op jit(solution)/shard_map/ppermute | solution.py:328
  49.3 25.4 %collective-permute-start.16 = (f32[9,256,128]{2,1,0:T(8,128)}, f32[9,256,128]{2,1,0:T(8,128)}, u32[]{:S(2)}, u32[]{:S(2)}) collective-permute-start(f32[9,256,128]{2,1,0:T(8,128)} %collective-permute-done.6.refs_1_), channel_id=1, source_target_pairs={{0,1},{1,0},{2,3},{3,2},{4,5},{5,4},{6,7},{7,6},{8,9},{9,8},{10,11... | collective-permute-start | bytes 3538952 | tf_op jit(solution)/shard_map/ppermute | solution.py:325
  50.9 28.4 %collective-permute-start.10 = (f32[8,256,128]{2,1,0:T(8,128)}, f32[8,256,128]{2,1,0:T(8,128)}, u32[]{:S(2)}, u32[]{:S(2)}) collective-permute-start(f32[8,256,128]{2,1,0:T(8,128)} %constant_dynamic-update-slice_fusion.refs_0_), channel_id=1, source_target_pairs={{0,8},{8,0},{16,24},{24,16},{1,9},{9,1},{17,25},{25,17},{2,10},{10... | collective-permute-start | bytes 3145736 | tf_op jit(solution)/shard_map/ppermute | solution.py:289
  59.7 19.6 %collective-permute-start.11 = (f32[8,256,128]{2,1,0:T(8,128)}, f32[8,256,128]{2,1,0:T(8,128)}, u32[]{:S(2)}, u32[]{:S(2)}) collective-permute-start(f32[8,256,128]{2,1,0:T(8,128)} %collective-permute-done.9.refs_1_), channel_id=1, source_target_pairs={{0,8},{8,0},{16,24},{24,16},{1,9},{9,1},{17,25},{25,17},{2,10},{10... | collective-permute-start | bytes 3145736 | tf_op jit(solution)/shard_map/ppermute | solution.py:289
  70.6 5.5 %collective-permute-start.12 = (f32[256,512]{1,0:T(8,128)}, f32[256,512]{1,0:T(8,128)}, u32[]{:S(2)}, u32[]{:S(2)}) collective-permute-start(f32[256,512]{1,0:T(8,128)} %slice_bitcast_fusion.3.refs_4_), channel_id=1, source_target_pairs={{0,8},{8,0},{16,24},{24,16},{1,9},{9,1},{17,25},{25,17},{2,10},{10... | collective-permute-start | bytes 1572872 | tf_op jit(solution)/shard_map/ppermute | solution.py:289
  71.7 6.0 %collective-permute-start.13 = (f32[256,512]{1,0:T(8,128)}, f32[256,512]{1,0:T(8,128)}, u32[]{:S(2)}, u32[]{:S(2)}) collective-permute-start(f32[256,512]{1,0:T(8,128)} %collective-permute-done.4.refs_5_), channel_id=1, source_target_pairs={{0,8},{8,0},{16,24},{24,16},{1,9},{9,1},{17,25},{25,17},{2,10},{10... | collective-permute-start | bytes 1572872 | tf_op jit(solution)/shard_map/ppermute | solution.py:289
  74.7 40.3 %collective-permute-start.17 = (f32[5,256,128]{2,1,0:T(8,128)S(1)}, f32[5,256,128]{2,1,0:T(8,128)S(1)}, u32[]{:S(2)}, u32[]{:S(2)}) collective-permute-start(f32[5,256,128]{2,1,0:T(8,128)S(1)} %slice.61), channel_id=1, source_target_pairs={{2,0},{3,1},{4,6},{5,7},{10,8},{11,9},{12,14},{13,15},{18,16},{19,... | collective-permute-start | bytes 1966088 | tf_op jit(solution)/shard_map/ppermute | solution.py:328
  76.1 27.7 %copy-start.1 = (f32[9,256,128]{2,1,0:T(8,128)S(1)}, f32[9,256,128]{2,1,0:T(8,128)}, u32[]{:S(2)}) copy-start(f32[9,256,128]{2,1,0:T(8,128)} %copy-done) | copy-start | bytes 3538948
  76.1 27.6 %collective-permute-start.18 = (f32[4,256,128]{2,1,0:T(8,128)S(1)}, f32[4,256,128]{2,1,0:T(8,128)S(1)}, u32[]{:S(2)}, u32[]{:S(2)}) collective-permute-start(f32[4,256,128]{2,1,0:T(8,128)S(1)} %slice.62), channel_id=1, source_target_pairs={{2,0},{3,1},{4,6},{5,7},{10,8},{11,9},{12,14},{13,15},{18,16},{19,... | collective-permute-start | bytes 1572872 | tf_op jit(solution)/shard_map/ppermute | solution.py:328
  77.7 26.0 %collective-permute-start.19 = (f32[5,256,128]{2,1,0:T(8,128)S(1)}, f32[5,256,128]{2,1,0:T(8,128)S(1)}, u32[]{:S(2)}, u32[]{:S(2)}) collective-permute-start(f32[5,256,128]{2,1,0:T(8,128)S(1)} %slice.63), channel_id=1, source_target_pairs={{0,1},{1,0},{2,3},{3,2},{4,5},{5,4},{6,7},{7,6},{8,9},{9,8},{10,11... | collective-permute-start | bytes 1966088 | tf_op jit(solution)/shard_map/ppermute | solution.py:325
  92.4 22.7 %collective-permute-start.20 = (f32[4,256,128]{2,1,0:T(8,128)S(1)}, f32[4,256,128]{2,1,0:T(8,128)S(1)}, u32[]{:S(2)}, u32[]{:S(2)}) collective-permute-start(f32[4,256,128]{2,1,0:T(8,128)S(1)} %slice.64), channel_id=1, source_target_pairs={{0,1},{1,0},{2,3},{3,2},{4,5},{5,4},{6,7},{7,6},{8,9},{9,8},{10,11... | collective-permute-start | bytes 1572872 | tf_op jit(solution)/shard_map/ppermute | solution.py:325
  103.7 14.9 %collective-permute-start.21 = (f32[5,256,128]{2,1,0:T(8,128)S(1)}, f32[5,256,128]{2,1,0:T(8,128)S(1)}, u32[]{:S(2)}, u32[]{:S(2)}) collective-permute-start(f32[5,256,128]{2,1,0:T(8,128)S(1)} %collective-permute-done.19.refs_3_), channel_id=1, source_target_pairs={{0,2},{1,3},{2,0},{3,1},{4,6},{5,7},{6,4},{7,5},{8,10},{9,11},{10,... | collective-permute-start | bytes 1966088 | tf_op jit(solution)/shard_map/ppermute | solution.py:325
  103.8 12.5 %collective-permute-start.22 = (f32[4,256,128]{2,1,0:T(8,128)S(1)}, f32[4,256,128]{2,1,0:T(8,128)S(1)}, u32[]{:S(2)}, u32[]{:S(2)}) collective-permute-start(f32[4,256,128]{2,1,0:T(8,128)S(1)} %slice_select_fusion), channel_id=1, source_target_pairs={{0,1},{1,0},{2,3},{3,2},{4,5},{5,4},{6,7},{7,6},{8,9},{9,8},{10,11... | collective-permute-start | bytes 1572872 | tf_op jit(solution)/shard_map/ppermute | solution.py:325
  (3 other events, 21.0 us)

commit v6 on v5

--- a/solution.py
+++ b/solution.py
@@ -339,7 +339,7 @@
 
     h_own = mine[0:1]
     h_line = [h_own] + [hop(h_own, bits) for bits in (2, 4, 6)]
-    middle_row = (trailing + 1) // 2
+    middle_row = trailing // 2
     s1 = [lane(own[:middle_row]), None]
     start = after(own, h_line[1])
     e1, m1 = ends(start), middle(start)

time: 125 us -> 124 us (level)
  waiting for transfers between devices: 57 us -> 55 us
    ppermute x6, waiting for transfers between devices: 8.81 us -> 4.99 us  [over_row(): held = held + [lax.ppermute(value, 'row', pairs) for value in held]]
    ppermute x5, waiting for transfers between devices: 21.7 us -> 23.6 us  [move(): lax.ppermute(value, 'real', [(a * lanes + n, b * lanes + n) for a, b in p...]
where the time goes in v6:
time: 124 us
  waiting for transfers between devices  55 us (44%)
  Pallas kernels  28.4 us (23%)
  starting transfers between devices  28 us (23%)
  local copies, waits for them, and re-layouts  10.1 us (8%)
  other arithmetic  1.57 us (1%)
    ppermute x12, waiting for transfers between devices, hop(): lax.ppermute(value, 'real', [(n, n ^ bits) for n in range(real_count)])  26.4 us
    ppermute x5, waiting for transfers between devices, move(): lax.ppermute(value, 'real', [(a * lanes + n, b * lanes + n) for a, b in p...  23.6 us
    ppermute x12, starting transfers between devices, hop(): lax.ppermute(value, 'real', [(n, n ^ bits) for n in range(real_count)])  19.5 us
    pallas_call x1, Pallas kernels, solve(): pl.pallas_call(kernel, out_shape=[jax.ShapeDtypeStruct((window, columns),...  13 us
    pallas_call x1, Pallas kernels, update_first(): pl.pallas_call(kernel, out_shape=pltpu.VMEM((blocks, rows, columns), F32)...  9.67 us
    pallas_call x1, Pallas kernels, update_last(): pl.pallas_call(kernel, out_shape=jax.ShapeDtypeStruct(target.shape, F32),...  5.7 us
    ppermute x5, starting transfers between devices, move(): lax.ppermute(value, 'real', [(a * lanes + n, b * lanes + n) for a, b in p...  5.51 us
    ppermute x6, waiting for transfers between devices, over_row(): held = held + [lax.ppermute(value, 'row', pairs) for value in held]  4.99 us
  transfers between devices with their start and end apart: 23, of which 10 were waited for; matrix products, arithmetic and copies ran while one was open for 7% of the time, Pallas kernels for 18%

profile of v6, /device:TPU:0, one launch (start us, length us, event | category | flops | bytes accessed | tf_op | source)
XLA Modules:
  0.0 123.6 jit_solution(238013913363998527)
XLA Ops:
  1.0 3.1 %collective-permute-start = (f32[1,256,128]{2,1,0:T(8,128)S(1)}, f32[1,256,128]{2,1,0:T(8,128)S(1)}, u32[]{:S(2)}, u32[]{:S(2)}) collective-permute-start(f32[1,256,128]{2,1,0:T(8,128)S(1)} %slice_bitcast_fusion.4), channel_id=1, source_target_pairs={{0,2},{1,3},{2,0},{3,1},{4,6},{5,7},{6,4},{7,5},{8,10},{9,11},{10,... | collective-permute-start | bytes 393224 | tf_op jit(solution)/shard_map/ppermute | solution.py:325
  4.1 2.6 %collective-permute-start.1 = (f32[1,256,128]{2,1,0:T(8,128)S(1)}, f32[1,256,128]{2,1,0:T(8,128)S(1)}, u32[]{:S(2)}, u32[]{:S(2)}) collective-permute-start(f32[1,256,128]{2,1,0:T(8,128)S(1)} %slice_bitcast_fusion.4), channel_id=1, source_target_pairs={{0,4},{1,5},{2,6},{3,7},{4,0},{5,1},{6,2},{7,3},{8,12},{9,13},{10,... | collective-permute-start | bytes 393224 | tf_op jit(solution)/shard_map/ppermute | solution.py:325
  7.8 1.8 %collective-permute-start.14 = (f32[4,256,128]{2,1,0:T(8,128)S(1)}, f32[4,256,128]{2,1,0:T(8,128)S(1)}, u32[]{:S(2)}, u32[]{:S(2)}) collective-permute-start(f32[4,256,128]{2,1,0:T(8,128)S(1)} %slice_bitcast_fusion.2), channel_id=1, source_target_pairs={{0,1},{1,0},{2,3},{3,2},{4,5},{5,4},{6,7},{7,6},{8,9},{9,8},{10,11... | collective-permute-start | bytes 1572872 | tf_op jit(solution)/shard_map/ppermute | solution.py:325
  10.4 3.6 %collective-permute-start.6 = (f32[9,256,128]{2,1,0:T(8,128)S(1)}, f32[9,256,128]{2,1,0:T(8,128)}, u32[]{:S(2)}, u32[]{:S(2)}) collective-permute-start(f32[9,256,128]{2,1,0:T(8,128)S(1)} %slice_bitcast_fusion.refs_0_), channel_id=1, source_target_pairs={{0,2},{1,3},{2,0},{3,1},{4,6},{5,7},{6,4},{7,5},{8,10},{9,11},{10,... | collective-permute-start | bytes 3538952 | tf_op jit(solution)/shard_map/ppermute | solution.py:325
  14.0 3.0 %collective-permute-done.1 = f32[1,256,128]{2,1,0:T(8,128)S(1)} collective-permute-done((f32[1,256,128]{2,1,0:T(8,128)S(1)}, f32[1,256,128]{2,1,0:T(8,128)S(1)}, u32[]{:S(2)}, u32[]{:S(2)}) %collective-permute-start.1) | collective-permute-done | bytes 131104 | tf_op jit(solution)/shard_map/ppermute | solution.py:325
  17.1 1.6 %collective-permute-start.3 = (f32[4,256,128]{2,1,0:T(8,128)S(1)}, f32[4,256,128]{2,1,0:T(8,128)S(1)}, u32[]{:S(2)}, u32[]{:S(2)}) collective-permute-start(f32[4,256,128]{2,1,0:T(8,128)S(1)} %pad_maximum_fusion), channel_id=1, source_target_pairs={{0,1},{1,0},{2,3},{3,2},{4,5},{5,4},{6,7},{7,6},{8,9},{9,8},{10,11... | collective-permute-start | bytes 1572872 | tf_op jit(solution)/shard_map/ppermute | solution.py:325
  18.7 1.9 %slice_bitcast_fusion.3.refs_4_ = f32[256,512]{1,0:T(8,128)} fusion(f32[10,1,256,512]{3,2,1,0:T(8,128)} %base_ref.1), kind=kLoop, calls=%fused_computation.6 | loop fusion | bytes 1048576 | tf_op jit(solution)/shard_map/squeeze | solution.py:352
  20.6 1.5 %collective-permute-start.4 = (f32[256,512]{1,0:T(8,128)}, f32[256,512]{1,0:T(8,128)}, u32[]{:S(2)}, u32[]{:S(2)}) collective-permute-start(f32[256,512]{1,0:T(8,128)} %slice_bitcast_fusion.3.refs_4_), channel_id=1, source_target_pairs={{0,16},{8,24},{16,0},{24,8},{1,17},{9,25},{17,1},{25,9},{2,18},{10... | collective-permute-start | bytes 1572872 | tf_op jit(solution)/shard_map/ppermute | solution.py:289
  24.7 7.5 %collective-permute-done.3 = f32[4,256,128]{2,1,0:T(8,128)S(1)} collective-permute-done((f32[4,256,128]{2,1,0:T(8,128)S(1)}, f32[4,256,128]{2,1,0:T(8,128)S(1)}, u32[]{:S(2)}, u32[]{:S(2)}) %collective-permute-start.3) | collective-permute-done | bytes 524320 | tf_op jit(solution)/shard_map/ppermute | solution.py:325
  33.0 1.5 %collective-permute-start.9 = (f32[8,256,128]{2,1,0:T(8,128)}, f32[8,256,128]{2,1,0:T(8,128)}, u32[]{:S(2)}, u32[]{:S(2)}) collective-permute-start(f32[8,256,128]{2,1,0:T(8,128)} %constant_dynamic-update-slice_fusion.refs_0_), channel_id=1, source_target_pairs={{0,16},{8,24},{16,0},{24,8},{1,17},{9,25},{17,1},{25,9},{2,18},{10... | collective-permute-start | bytes 3145736 | tf_op jit(solution)/shard_map/ppermute | solution.py:289
  34.6 1.6 %collective-permute-start.15 = (f32[5,256,128]{2,1,0:T(8,128)S(1)}, f32[5,256,128]{2,1,0:T(8,128)S(1)}, u32[]{:S(2)}, u32[]{:S(2)}) collective-permute-start(f32[5,256,128]{2,1,0:T(8,128)S(1)} %slice_bitcast_fusion.1), channel_id=1, source_target_pairs={{0,1},{1,0},{2,3},{3,2},{4,5},{5,4},{6,7},{7,6},{8,9},{9,8},{10,11... | collective-permute-start | bytes 1966088 | tf_op jit(solution)/shard_map/ppermute | solution.py:325
  36.2 5.2 %collective-permute-done.6.refs_1_ = f32[9,256,128]{2,1,0:T(8,128)} collective-permute-done((f32[9,256,128]{2,1,0:T(8,128)S(1)}, f32[9,256,128]{2,1,0:T(8,128)}, u32[]{:S(2)}, u32[]{:S(2)}) %collective-permute-start.6) | collective-permute-done | bytes 1179680 | tf_op jit(solution)/shard_map/ppermute | solution.py:325
  43.4 5.8 %collective-permute-done.15 = f32[5,256,128]{2,1,0:T(8,128)S(1)} collective-permute-done((f32[5,256,128]{2,1,0:T(8,128)S(1)}, f32[5,256,128]{2,1,0:T(8,128)S(1)}, u32[]{:S(2)}, u32[]{:S(2)}) %collective-permute-start.15) | collective-permute-done | bytes 655392 | tf_op jit(solution)/shard_map/ppermute | solution.py:325
  50.4 1.5 %collective-permute-start.16 = (f32[9,256,128]{2,1,0:T(8,128)}, f32[9,256,128]{2,1,0:T(8,128)}, u32[]{:S(2)}, u32[]{:S(2)}) collective-permute-start(f32[9,256,128]{2,1,0:T(8,128)} %collective-permute-done.6.refs_1_), channel_id=1, source_target_pairs={{0,1},{1,0},{2,3},{3,2},{4,5},{5,4},{6,7},{7,6},{8,9},{9,8},{10,11... | collective-permute-start | bytes 3538952 | tf_op jit(solution)/shard_map/ppermute | solution.py:325
  51.9 5.0 %collective-permute-done.9.refs_1_ = f32[8,256,128]{2,1,0:T(8,128)} collective-permute-done((f32[8,256,128]{2,1,0:T(8,128)}, f32[8,256,128]{2,1,0:T(8,128)}, u32[]{:S(2)}, u32[]{:S(2)}) %collective-permute-start.9) | collective-permute-done | bytes 1048608 | tf_op jit(solution)/shard_map/ppermute | solution.py:289
  56.9 13.7 %collective-permute-done.7.refs_4_ = f32[9,256,128]{2,1,0:T(8,128)S(1)} collective-permute-done((f32[9,256,128]{2,1,0:T(8,128)S(1)}, f32[9,256,128]{2,1,0:T(8,128)S(1)}, u32[]{:S(2)}, u32[]{:S(2)}) %collective-permute-start.7) | collective-permute-done | bytes 1179680 | tf_op jit(solution)/shard_map/ppermute | solution.py:328
  73.4 2.3 %collective-permute-done.16.refs_5_ = f32[9,256,128]{2,1,0:T(8,128)} collective-permute-done((f32[9,256,128]{2,1,0:T(8,128)}, f32[9,256,128]{2,1,0:T(8,128)}, u32[]{:S(2)}, u32[]{:S(2)}) %collective-permute-start.16) | collective-permute-done | bytes 1179680 | tf_op jit(solution)/shard_map/ppermute | solution.py:325
  78.5 1.6 %collective-permute-start.19 = (f32[5,256,128]{2,1,0:T(8,128)S(1)}, f32[5,256,128]{2,1,0:T(8,128)S(1)}, u32[]{:S(2)}, u32[]{:S(2)}) collective-permute-start(f32[5,256,128]{2,1,0:T(8,128)S(1)} %slice.63), channel_id=1, source_target_pairs={{0,1},{1,0},{2,3},{3,2},{4,5},{5,4},{6,7},{7,6},{8,9},{9,8},{10,11... | collective-permute-start | bytes 1966088 | tf_op jit(solution)/shard_map/ppermute | solution.py:325
  80.1 13.0 %solve.1 = (f32[1024,512]{1,0:T(8,128)}, f32[10,1,256,512]{3,2,1,0:T(8,128)}) custom-call(s32[33]{0:T(128)S(1)} %concatenate.14.place, f32[8,256,128]{2,1,0:T(8,128)} %constant_dynamic-update-slice_fusion.refs_0_, f32[8,256,128]{2,1,0:T(8,128)} %collective-permute-done.9.refs_1_, f32[8,256,128]{2,1,0:T(8,128)} %collective-permute-done.10.refs_2_, ...), custom_call_target="tpu_custom_call" | custom-call | flops 16106127360 | bytes 8388608 | tf_op jit(solution)/shard_map/solve/pallas_call | solution.py:148
  93.8 9.9 %collective-permute-done.18.refs_2_ = f32[4,256,128]{2,1,0:T(8,128)S(1)} collective-permute-done((f32[4,256,128]{2,1,0:T(8,128)S(1)}, f32[4,256,128]{2,1,0:T(8,128)S(1)}, u32[]{:S(2)}, u32[]{:S(2)}) %collective-permute-start.18) | collective-permute-done | bytes 524320 | tf_op jit(solution)/shard_map/ppermute | solution.py:328
  103.8 1.6 %collective-permute-start.22 = (f32[4,256,128]{2,1,0:T(8,128)S(1)}, f32[4,256,128]{2,1,0:T(8,128)S(1)}, u32[]{:S(2)}, u32[]{:S(2)}) collective-permute-start(f32[4,256,128]{2,1,0:T(8,128)S(1)} %slice_select_fusion), channel_id=1, source_target_pairs={{0,1},{1,0},{2,3},{3,2},{4,5},{5,4},{6,7},{7,6},{8,9},{9,8},{10,11... | collective-permute-start | bytes 1572872 | tf_op jit(solution)/shard_map/ppermute | solution.py:325
  105.4 9.7 %update_first.1.acc_ref = f32[9,256,512]{2,1,0:T(8,128)S(1)} custom-call(s32[5]{0:T(128)S(1)} %stack.69.place, f32[1024,512]{1,0:T(8,128)} %get-tuple-element.22.y_ref, f32[10,1,256,512]{3,2,1,0:T(8,128)} %base_ref.1, f32[9,256,128]{2,1,0:T(8,128)S(1)} %slice_bitcast_fusion.refs_0_, f32[9,256,128]{2,1,0:T(8,128)} %collective-permute-done.6.refs_1_, ...), custom_call_target="tpu_custom_call" | custom-call | flops 4529848320 | bytes 15335424 | tf_op jit(solution)/shard_map/update_first/pallas_call | solution.py:210
  116.2 1.5 %collective-permute-done.21.refs_5_ = f32[5,256,128]{2,1,0:T(8,128)S(1)} collective-permute-done((f32[5,256,128]{2,1,0:T(8,128)S(1)}, f32[5,256,128]{2,1,0:T(8,128)S(1)}, u32[]{:S(2)}, u32[]{:S(2)}) %collective-permute-start.21) | collective-permute-done | bytes 655392 | tf_op jit(solution)/shard_map/ppermute | solution.py:325
  117.7 5.7 %update_last.1 = f32[10,1,256,512]{3,2,1,0:T(8,128)} custom-call(s32[3]{0:T(128)S(1)} %pad_add_fusion.place, f32[1024,512]{1,0:T(8,128)} %get-tuple-element.22.y_ref, f32[9,256,512]{2,1,0:T(8,128)S(1)} %update_first.1.acc_ref, f32[9,256,128]{2,1,0:T(8,128)S(1)} %collective-permute-done.8.refs_0_, ...), custom_call_target="tpu_custom_call", output_to_operand_aliasing={{}: (10, {})} | custom-call | flops 2717908992 | bytes 12976128 | tf_op jit(solution)/shard_map/update_last/pallas_call | solution.py:262
  (55 shorter events, 17.0 us)
Async XLA Ops:
  1.0 8.7 %collective-permute-start = (f32[1,256,128]{2,1,0:T(8,128)S(1)}, f32[1,256,128]{2,1,0:T(8,128)S(1)}, u32[]{:S(2)}, u32[]{:S(2)}) collective-permute-start(f32[1,256,128]{2,1,0:T(8,128)S(1)} %slice_bitcast_fusion.4), channel_id=1, source_target_pairs={{0,2},{1,3},{2,0},{3,1},{4,6},{5,7},{6,4},{7,5},{8,10},{9,11},{10,... | collective-permute-start | bytes 393224 | tf_op jit(solution)/shard_map/ppermute | solution.py:325
  4.1 12.9 %collective-permute-start.1 = (f32[1,256,128]{2,1,0:T(8,128)S(1)}, f32[1,256,128]{2,1,0:T(8,128)S(1)}, u32[]{:S(2)}, u32[]{:S(2)}) collective-permute-start(f32[1,256,128]{2,1,0:T(8,128)S(1)} %slice_bitcast_fusion.4), channel_id=1, source_target_pairs={{0,4},{1,5},{2,6},{3,7},{4,0},{5,1},{6,2},{7,3},{8,12},{9,13},{10,... | collective-permute-start | bytes 393224 | tf_op jit(solution)/shard_map/ppermute | solution.py:325
  6.7 10.4 %collective-permute-start.2 = (f32[1,256,128]{2,1,0:T(8,128)S(1)}, f32[1,256,128]{2,1,0:T(8,128)S(1)}, u32[]{:S(2)}, u32[]{:S(2)}) collective-permute-start(f32[1,256,128]{2,1,0:T(8,128)S(1)} %slice_bitcast_fusion.4), channel_id=1, source_target_pairs={{0,6},{1,7},{2,4},{3,5},{4,2},{5,3},{6,0},{7,1},{8,14},{9,15},{10,... | collective-permute-start | bytes 393224 | tf_op jit(solution)/shard_map/ppermute | solution.py:325
  7.8 26.8 %collective-permute-start.14 = (f32[4,256,128]{2,1,0:T(8,128)S(1)}, f32[4,256,128]{2,1,0:T(8,128)S(1)}, u32[]{:S(2)}, u32[]{:S(2)}) collective-permute-start(f32[4,256,128]{2,1,0:T(8,128)S(1)} %slice_bitcast_fusion.2), channel_id=1, source_target_pairs={{0,1},{1,0},{2,3},{3,2},{4,5},{5,4},{6,7},{7,6},{8,9},{9,8},{10,11... | collective-permute-start | bytes 1572872 | tf_op jit(solution)/shard_map/ppermute | solution.py:325
  9.7 26.5 %collective-permute-start.5 = (f32[9,256,128]{2,1,0:T(8,128)S(1)}, f32[9,256,128]{2,1,0:T(8,128)S(1)}, u32[]{:S(2)}, u32[]{:S(2)}) collective-permute-start(f32[9,256,128]{2,1,0:T(8,128)S(1)} %slice_bitcast_fusion.refs_0_), channel_id=1, source_target_pairs={{2,4},{3,5},{4,2},{5,3},{10,12},{11,13},{12,10},{13,11},{18,20},{1... | collective-permute-start | bytes 3538952 | tf_op jit(solution)/shard_map/ppermute | solution.py:328
  10.4 30.9 %collective-permute-start.6 = (f32[9,256,128]{2,1,0:T(8,128)S(1)}, f32[9,256,128]{2,1,0:T(8,128)}, u32[]{:S(2)}, u32[]{:S(2)}) collective-permute-start(f32[9,256,128]{2,1,0:T(8,128)S(1)} %slice_bitcast_fusion.refs_0_), channel_id=1, source_target_pairs={{0,2},{1,3},{2,0},{3,1},{4,6},{5,7},{6,4},{7,5},{8,10},{9,11},{10,... | collective-permute-start | bytes 3538952 | tf_op jit(solution)/shard_map/ppermute | solution.py:325
  17.1 15.1 %collective-permute-start.3 = (f32[4,256,128]{2,1,0:T(8,128)S(1)}, f32[4,256,128]{2,1,0:T(8,128)S(1)}, u32[]{:S(2)}, u32[]{:S(2)}) collective-permute-start(f32[4,256,128]{2,1,0:T(8,128)S(1)} %pad_maximum_fusion), channel_id=1, source_target_pairs={{0,1},{1,0},{2,3},{3,2},{4,5},{5,4},{6,7},{7,6},{8,9},{9,8},{10,11... | collective-permute-start | bytes 1572872 | tf_op jit(solution)/shard_map/ppermute | solution.py:325
  20.6 12.5 %collective-permute-start.4 = (f32[256,512]{1,0:T(8,128)}, f32[256,512]{1,0:T(8,128)}, u32[]{:S(2)}, u32[]{:S(2)}) collective-permute-start(f32[256,512]{1,0:T(8,128)} %slice_bitcast_fusion.3.refs_4_), channel_id=1, source_target_pairs={{0,16},{8,24},{16,0},{24,8},{1,17},{9,25},{17,1},{25,9},{2,18},{10... | collective-permute-start | bytes 1572872 | tf_op jit(solution)/shard_map/ppermute | solution.py:289
  33.0 23.8 %collective-permute-start.9 = (f32[8,256,128]{2,1,0:T(8,128)}, f32[8,256,128]{2,1,0:T(8,128)}, u32[]{:S(2)}, u32[]{:S(2)}) collective-permute-start(f32[8,256,128]{2,1,0:T(8,128)} %constant_dynamic-update-slice_fusion.refs_0_), channel_id=1, source_target_pairs={{0,16},{8,24},{16,0},{24,8},{1,17},{9,25},{17,1},{25,9},{2,18},{10... | collective-permute-start | bytes 3145736 | tf_op jit(solution)/shard_map/ppermute | solution.py:289
  34.6 14.7 %collective-permute-start.15 = (f32[5,256,128]{2,1,0:T(8,128)S(1)}, f32[5,256,128]{2,1,0:T(8,128)S(1)}, u32[]{:S(2)}, u32[]{:S(2)}) collective-permute-start(f32[5,256,128]{2,1,0:T(8,128)S(1)} %slice_bitcast_fusion.1), channel_id=1, source_target_pairs={{0,1},{1,0},{2,3},{3,2},{4,5},{5,4},{6,7},{7,6},{8,9},{9,8},{10,11... | collective-permute-start | bytes 1966088 | tf_op jit(solution)/shard_map/ppermute | solution.py:325
  41.3 29.2 %collective-permute-start.7 = (f32[9,256,128]{2,1,0:T(8,128)S(1)}, f32[9,256,128]{2,1,0:T(8,128)S(1)}, u32[]{:S(2)}, u32[]{:S(2)}) collective-permute-start(f32[9,256,128]{2,1,0:T(8,128)S(1)} %collective-permute-done.5.refs_3_), channel_id=1, source_target_pairs={{2,0},{3,1},{4,6},{5,7},{10,8},{11,9},{12,14},{13,15},{18,16},{19,... | collective-permute-start | bytes 3538952 | tf_op jit(solution)/shard_map/ppermute | solution.py:328
  42.6 27.9 %collective-permute-start.8 = (f32[9,256,128]{2,1,0:T(8,128)}, f32[9,256,128]{2,1,0:T(8,128)S(1)}, u32[]{:S(2)}, u32[]{:S(2)}) collective-permute-start(f32[9,256,128]{2,1,0:T(8,128)} %collective-permute-done.6.refs_1_), channel_id=1, source_target_pairs={{2,4},{3,5},{4,2},{5,3},{10,12},{11,13},{12,10},{13,11},{18,20},{1... | collective-permute-start | bytes 3538952 | tf_op jit(solution)/shard_map/ppermute | solution.py:328
  50.4 25.3 %collective-permute-start.16 = (f32[9,256,128]{2,1,0:T(8,128)}, f32[9,256,128]{2,1,0:T(8,128)}, u32[]{:S(2)}, u32[]{:S(2)}) collective-permute-start(f32[9,256,128]{2,1,0:T(8,128)} %collective-permute-done.6.refs_1_), channel_id=1, source_target_pairs={{0,1},{1,0},{2,3},{3,2},{4,5},{5,4},{6,7},{7,6},{8,9},{9,8},{10,11... | collective-permute-start | bytes 3538952 | tf_op jit(solution)/shard_map/ppermute | solution.py:325
  51.9 28.2 %collective-permute-start.10 = (f32[8,256,128]{2,1,0:T(8,128)}, f32[8,256,128]{2,1,0:T(8,128)}, u32[]{:S(2)}, u32[]{:S(2)}) collective-permute-start(f32[8,256,128]{2,1,0:T(8,128)} %constant_dynamic-update-slice_fusion.refs_0_), channel_id=1, source_target_pairs={{0,8},{8,0},{16,24},{24,16},{1,9},{9,1},{17,25},{25,17},{2,10},{10... | collective-permute-start | bytes 3145736 | tf_op jit(solution)/shard_map/ppermute | solution.py:289
  56.9 23.3 %collective-permute-start.11 = (f32[8,256,128]{2,1,0:T(8,128)}, f32[8,256,128]{2,1,0:T(8,128)}, u32[]{:S(2)}, u32[]{:S(2)}) collective-permute-start(f32[8,256,128]{2,1,0:T(8,128)} %collective-permute-done.9.refs_1_), channel_id=1, source_target_pairs={{0,8},{8,0},{16,24},{24,16},{1,9},{9,1},{17,25},{25,17},{2,10},{10... | collective-permute-start | bytes 3145736 | tf_op jit(solution)/shard_map/ppermute | solution.py:289
  70.5 6.5 %collective-permute-start.12 = (f32[256,512]{1,0:T(8,128)}, f32[256,512]{1,0:T(8,128)}, u32[]{:S(2)}, u32[]{:S(2)}) collective-permute-start(f32[256,512]{1,0:T(8,128)} %slice_bitcast_fusion.3.refs_4_), channel_id=1, source_target_pairs={{0,8},{8,0},{16,24},{24,16},{1,9},{9,1},{17,25},{25,17},{2,10},{10... | collective-permute-start | bytes 1572872 | tf_op jit(solution)/shard_map/ppermute | solution.py:289
  71.6 6.9 %collective-permute-start.13 = (f32[256,512]{1,0:T(8,128)}, f32[256,512]{1,0:T(8,128)}, u32[]{:S(2)}, u32[]{:S(2)}) collective-permute-start(f32[256,512]{1,0:T(8,128)} %collective-permute-done.4.refs_5_), channel_id=1, source_target_pairs={{0,8},{8,0},{16,24},{24,16},{1,9},{9,1},{17,25},{25,17},{2,10},{10... | collective-permute-start | bytes 1572872 | tf_op jit(solution)/shard_map/ppermute | solution.py:289
  75.7 39.4 %collective-permute-start.17 = (f32[5,256,128]{2,1,0:T(8,128)S(1)}, f32[5,256,128]{2,1,0:T(8,128)S(1)}, u32[]{:S(2)}, u32[]{:S(2)}) collective-permute-start(f32[5,256,128]{2,1,0:T(8,128)S(1)} %slice.61), channel_id=1, source_target_pairs={{2,0},{3,1},{4,6},{5,7},{10,8},{11,9},{12,14},{13,15},{18,16},{19,... | collective-permute-start | bytes 1966088 | tf_op jit(solution)/shard_map/ppermute | solution.py:328
  77.0 26.7 %collective-permute-start.18 = (f32[4,256,128]{2,1,0:T(8,128)S(1)}, f32[4,256,128]{2,1,0:T(8,128)S(1)}, u32[]{:S(2)}, u32[]{:S(2)}) collective-permute-start(f32[4,256,128]{2,1,0:T(8,128)S(1)} %slice.62), channel_id=1, source_target_pairs={{2,0},{3,1},{4,6},{5,7},{10,8},{11,9},{12,14},{13,15},{18,16},{19,... | collective-permute-start | bytes 1572872 | tf_op jit(solution)/shard_map/ppermute | solution.py:328
  78.5 25.2 %collective-permute-start.19 = (f32[5,256,128]{2,1,0:T(8,128)S(1)}, f32[5,256,128]{2,1,0:T(8,128)S(1)}, u32[]{:S(2)}, u32[]{:S(2)}) collective-permute-start(f32[5,256,128]{2,1,0:T(8,128)S(1)} %slice.63), channel_id=1, source_target_pairs={{0,1},{1,0},{2,3},{3,2},{4,5},{5,4},{6,7},{7,6},{8,9},{9,8},{10,11... | collective-permute-start | bytes 1966088 | tf_op jit(solution)/shard_map/ppermute | solution.py:325
  93.2 12.3 %copy-start.1 = (f32[9,256,128]{2,1,0:T(8,128)S(1)}, f32[9,256,128]{2,1,0:T(8,128)}, u32[]{:S(2)}) copy-start(f32[9,256,128]{2,1,0:T(8,128)} %copy-done) | copy-start | bytes 3538948
  93.2 21.9 %collective-permute-start.20 = (f32[4,256,128]{2,1,0:T(8,128)S(1)}, f32[4,256,128]{2,1,0:T(8,128)S(1)}, u32[]{:S(2)}, u32[]{:S(2)}) collective-permute-start(f32[4,256,128]{2,1,0:T(8,128)S(1)} %slice.64), channel_id=1, source_target_pairs={{0,1},{1,0},{2,3},{3,2},{4,5},{5,4},{6,7},{7,6},{8,9},{9,8},{10,11... | collective-permute-start | bytes 1572872 | tf_op jit(solution)/shard_map/ppermute | solution.py:325
  103.7 14.0 %collective-permute-start.21 = (f32[5,256,128]{2,1,0:T(8,128)S(1)}, f32[5,256,128]{2,1,0:T(8,128)S(1)}, u32[]{:S(2)}, u32[]{:S(2)}) collective-permute-start(f32[5,256,128]{2,1,0:T(8,128)S(1)} %collective-permute-done.19.refs_3_), channel_id=1, source_target_pairs={{0,2},{1,3},{2,0},{3,1},{4,6},{5,7},{6,4},{7,5},{8,10},{9,11},{10,... | collective-permute-start | bytes 1966088 | tf_op jit(solution)/shard_map/ppermute | solution.py:325
  103.8 12.4 %collective-permute-start.22 = (f32[4,256,128]{2,1,0:T(8,128)S(1)}, f32[4,256,128]{2,1,0:T(8,128)S(1)}, u32[]{:S(2)}, u32[]{:S(2)}) collective-permute-start(f32[4,256,128]{2,1,0:T(8,128)S(1)} %slice_select_fusion), channel_id=1, source_target_pairs={{0,1},{1,0},{2,3},{3,2},{4,5},{5,4},{6,7},{7,6},{8,9},{9,8},{10,11... | collective-permute-start | bytes 1572872 | tf_op jit(solution)/shard_map/ppermute | solution.py:325
  (3 other events, 11.7 us)

commit v7 on v6

--- a/solution.py
+++ b/solution.py
@@ -353,7 +353,7 @@
     codes, heads = over_row(after(h_all, sides[1]), row_count)
 
     first, second = halves
-    o2 = out(after(m1, e1))
+    o2 = out(m1)
     m2 = middle(e1)
     s2 = lane(after(e1, s1))
     o3 = [out(m2[rows]) for rows in halves]

time: 124 us -> 124 us (level)
  no operation moved by 1% of the time
where the time goes in v7:
time: 124 us; the launch traced here: 123 us
  waiting for transfers between devices  55 us (44%)
  Pallas kernels  28.4 us (23%)
  starting transfers between devices  28 us (23%)
  local copies, waits for them, and re-layouts  10.1 us (8%)
  other arithmetic  1.57 us (1%)
    ppermute x12, waiting for transfers between devices, hop(): lax.ppermute(value, 'real', [(n, n ^ bits) for n in range(real_count)])  26.4 us
    ppermute x5, waiting for transfers between devices, move(): lax.ppermute(value, 'real', [(a * lanes + n, b * lanes + n) for a, b in p...  23.6 us
    ppermute x12, starting transfers between devices, hop(): lax.ppermute(value, 'real', [(n, n ^ bits) for n in range(real_count)])  19.5 us
    pallas_call x1, Pallas kernels, solve(): pl.pallas_call(kernel, out_shape=[jax.ShapeDtypeStruct((window, columns),...  13 us
    pallas_call x1, Pallas kernels, update_first(): pl.pallas_call(kernel, out_shape=pltpu.VMEM((blocks, rows, columns), F32)...  9.67 us
    pallas_call x1, Pallas kernels, update_last(): pl.pallas_call(kernel, out_shape=jax.ShapeDtypeStruct(target.shape, F32),...  5.7 us
    ppermute x5, starting transfers between devices, move(): lax.ppermute(value, 'real', [(a * lanes + n, b * lanes + n) for a, b in p...  5.5 us
    ppermute x6, waiting for transfers between devices, over_row(): held = held + [lax.ppermute(value, 'row', pairs) for value in held]  4.99 us
  transfers between devices with their start and end apart: 23, of which 10 were waited for; matrix products, arithmetic and copies ran while one was open for 7% of the time, Pallas kernels for 18%

profile of v7, /device:TPU:0, one launch (start us, length us, event | category | flops | bytes accessed | tf_op | source)
XLA Modules:
  0.0 123.5 jit_solution(16191916692986274195)
XLA Ops:
  1.0 3.1 %collective-permute-start = (f32[1,256,128]{2,1,0:T(8,128)S(1)}, f32[1,256,128]{2,1,0:T(8,128)S(1)}, u32[]{:S(2)}, u32[]{:S(2)}) collective-permute-start(f32[1,256,128]{2,1,0:T(8,128)S(1)} %slice_bitcast_fusion.4), channel_id=1, source_target_pairs={{0,2},{1,3},{2,0},{3,1},{4,6},{5,7},{6,4},{7,5},{8,10},{9,11},{10,... | collective-permute-start | bytes 393224 | tf_op jit(solution)/shard_map/ppermute | solution.py:325
  4.1 2.6 %collective-permute-start.1 = (f32[1,256,128]{2,1,0:T(8,128)S(1)}, f32[1,256,128]{2,1,0:T(8,128)S(1)}, u32[]{:S(2)}, u32[]{:S(2)}) collective-permute-start(f32[1,256,128]{2,1,0:T(8,128)S(1)} %slice_bitcast_fusion.4), channel_id=1, source_target_pairs={{0,4},{1,5},{2,6},{3,7},{4,0},{5,1},{6,2},{7,3},{8,12},{9,13},{10,... | collective-permute-start | bytes 393224 | tf_op jit(solution)/shard_map/ppermute | solution.py:325
  7.8 1.8 %collective-permute-start.14 = (f32[4,256,128]{2,1,0:T(8,128)S(1)}, f32[4,256,128]{2,1,0:T(8,128)S(1)}, u32[]{:S(2)}, u32[]{:S(2)}) collective-permute-start(f32[4,256,128]{2,1,0:T(8,128)S(1)} %slice_bitcast_fusion.2), channel_id=1, source_target_pairs={{0,1},{1,0},{2,3},{3,2},{4,5},{5,4},{6,7},{7,6},{8,9},{9,8},{10,11... | collective-permute-start | bytes 1572872 | tf_op jit(solution)/shard_map/ppermute | solution.py:325
  10.4 3.6 %collective-permute-start.7 = (f32[9,256,128]{2,1,0:T(8,128)S(1)}, f32[9,256,128]{2,1,0:T(8,128)}, u32[]{:S(2)}, u32[]{:S(2)}) collective-permute-start(f32[9,256,128]{2,1,0:T(8,128)S(1)} %slice_bitcast_fusion.refs_0_), channel_id=1, source_target_pairs={{0,2},{1,3},{2,0},{3,1},{4,6},{5,7},{6,4},{7,5},{8,10},{9,11},{10,... | collective-permute-start | bytes 3538952 | tf_op jit(solution)/shard_map/ppermute | solution.py:325
  14.0 3.0 %collective-permute-done.1 = f32[1,256,128]{2,1,0:T(8,128)S(1)} collective-permute-done((f32[1,256,128]{2,1,0:T(8,128)S(1)}, f32[1,256,128]{2,1,0:T(8,128)S(1)}, u32[]{:S(2)}, u32[]{:S(2)}) %collective-permute-start.1) | collective-permute-done | bytes 131104 | tf_op jit(solution)/shard_map/ppermute | solution.py:325
  17.1 1.6 %collective-permute-start.3 = (f32[4,256,128]{2,1,0:T(8,128)S(1)}, f32[4,256,128]{2,1,0:T(8,128)S(1)}, u32[]{:S(2)}, u32[]{:S(2)}) collective-permute-start(f32[4,256,128]{2,1,0:T(8,128)S(1)} %pad_maximum_fusion), channel_id=1, source_target_pairs={{0,1},{1,0},{2,3},{3,2},{4,5},{5,4},{6,7},{7,6},{8,9},{9,8},{10,11... | collective-permute-start | bytes 1572872 | tf_op jit(solution)/shard_map/ppermute | solution.py:325
  18.7 1.9 %slice_bitcast_fusion.3.refs_4_ = f32[256,512]{1,0:T(8,128)} fusion(f32[10,1,256,512]{3,2,1,0:T(8,128)} %base_ref.1), kind=kLoop, calls=%fused_computation.6 | loop fusion | bytes 1048576 | tf_op jit(solution)/shard_map/squeeze | solution.py:352
  20.6 1.5 %collective-permute-start.4 = (f32[256,512]{1,0:T(8,128)}, f32[256,512]{1,0:T(8,128)}, u32[]{:S(2)}, u32[]{:S(2)}) collective-permute-start(f32[256,512]{1,0:T(8,128)} %slice_bitcast_fusion.3.refs_4_), channel_id=1, source_target_pairs={{0,16},{8,24},{16,0},{24,8},{1,17},{9,25},{17,1},{25,9},{2,18},{10... | collective-permute-start | bytes 1572872 | tf_op jit(solution)/shard_map/ppermute | solution.py:289
  24.7 7.5 %collective-permute-done.3 = f32[4,256,128]{2,1,0:T(8,128)S(1)} collective-permute-done((f32[4,256,128]{2,1,0:T(8,128)S(1)}, f32[4,256,128]{2,1,0:T(8,128)S(1)}, u32[]{:S(2)}, u32[]{:S(2)}) %collective-permute-start.3) | collective-permute-done | bytes 524320 | tf_op jit(solution)/shard_map/ppermute | solution.py:325
  33.0 1.5 %collective-permute-start.9 = (f32[8,256,128]{2,1,0:T(8,128)}, f32[8,256,128]{2,1,0:T(8,128)}, u32[]{:S(2)}, u32[]{:S(2)}) collective-permute-start(f32[8,256,128]{2,1,0:T(8,128)} %constant_dynamic-update-slice_fusion.refs_0_), channel_id=1, source_target_pairs={{0,16},{8,24},{16,0},{24,8},{1,17},{9,25},{17,1},{25,9},{2,18},{10... | collective-permute-start | bytes 3145736 | tf_op jit(solution)/shard_map/ppermute | solution.py:289
  34.6 1.6 %collective-permute-start.15 = (f32[5,256,128]{2,1,0:T(8,128)S(1)}, f32[5,256,128]{2,1,0:T(8,128)S(1)}, u32[]{:S(2)}, u32[]{:S(2)}) collective-permute-start(f32[5,256,128]{2,1,0:T(8,128)S(1)} %slice_bitcast_fusion.1), channel_id=1, source_target_pairs={{0,1},{1,0},{2,3},{3,2},{4,5},{5,4},{6,7},{7,6},{8,9},{9,8},{10,11... | collective-permute-start | bytes 1966088 | tf_op jit(solution)/shard_map/ppermute | solution.py:325
  37.5 3.9 %collective-permute-done.7.refs_1_ = f32[9,256,128]{2,1,0:T(8,128)} collective-permute-done((f32[9,256,128]{2,1,0:T(8,128)S(1)}, f32[9,256,128]{2,1,0:T(8,128)}, u32[]{:S(2)}, u32[]{:S(2)}) %collective-permute-start.7) | collective-permute-done | bytes 1179680 | tf_op jit(solution)/shard_map/ppermute | solution.py:325
  42.1 7.1 %collective-permute-done.15 = f32[5,256,128]{2,1,0:T(8,128)S(1)} collective-permute-done((f32[5,256,128]{2,1,0:T(8,128)S(1)}, f32[5,256,128]{2,1,0:T(8,128)S(1)}, u32[]{:S(2)}, u32[]{:S(2)}) %collective-permute-start.15) | collective-permute-done | bytes 655392 | tf_op jit(solution)/shard_map/ppermute | solution.py:325
  50.4 1.5 %collective-permute-start.16 = (f32[9,256,128]{2,1,0:T(8,128)}, f32[9,256,128]{2,1,0:T(8,128)}, u32[]{:S(2)}, u32[]{:S(2)}) collective-permute-start(f32[9,256,128]{2,1,0:T(8,128)} %collective-permute-done.7.refs_1_), channel_id=1, source_target_pairs={{0,1},{1,0},{2,3},{3,2},{4,5},{5,4},{6,7},{7,6},{8,9},{9,8},{10,11... | collective-permute-start | bytes 3538952 | tf_op jit(solution)/shard_map/ppermute | solution.py:325
  51.9 5.0 %collective-permute-done.9.refs_1_ = f32[8,256,128]{2,1,0:T(8,128)} collective-permute-done((f32[8,256,128]{2,1,0:T(8,128)}, f32[8,256,128]{2,1,0:T(8,128)}, u32[]{:S(2)}, u32[]{:S(2)}) %collective-permute-start.9) | collective-permute-done | bytes 1048608 | tf_op jit(solution)/shard_map/ppermute | solution.py:289
  56.9 13.6 %collective-permute-done.6.refs_4_ = f32[9,256,128]{2,1,0:T(8,128)S(1)} collective-permute-done((f32[9,256,128]{2,1,0:T(8,128)S(1)}, f32[9,256,128]{2,1,0:T(8,128)S(1)}, u32[]{:S(2)}, u32[]{:S(2)}) %collective-permute-start.6) | collective-permute-done | bytes 1179680 | tf_op jit(solution)/shard_map/ppermute | solution.py:328
  73.3 2.4 %collective-permute-done.16.refs_5_ = f32[9,256,128]{2,1,0:T(8,128)} collective-permute-done((f32[9,256,128]{2,1,0:T(8,128)}, f32[9,256,128]{2,1,0:T(8,128)}, u32[]{:S(2)}, u32[]{:S(2)}) %collective-permute-start.16) | collective-permute-done | bytes 1179680 | tf_op jit(solution)/shard_map/ppermute | solution.py:325
  77.0 1.5 %collective-permute-start.18 = (f32[4,256,128]{2,1,0:T(8,128)S(1)}, f32[4,256,128]{2,1,0:T(8,128)S(1)}, u32[]{:S(2)}, u32[]{:S(2)}) collective-permute-start(f32[4,256,128]{2,1,0:T(8,128)S(1)} %slice.62), channel_id=1, source_target_pairs={{2,0},{3,1},{4,6},{5,7},{10,8},{11,9},{12,14},{13,15},{18,16},{19,... | collective-permute-start | bytes 1572872 | tf_op jit(solution)/shard_map/ppermute | solution.py:328
  78.5 1.6 %collective-permute-start.19 = (f32[5,256,128]{2,1,0:T(8,128)S(1)}, f32[5,256,128]{2,1,0:T(8,128)S(1)}, u32[]{:S(2)}, u32[]{:S(2)}) collective-permute-start(f32[5,256,128]{2,1,0:T(8,128)S(1)} %slice.63), channel_id=1, source_target_pairs={{0,1},{1,0},{2,3},{3,2},{4,5},{5,4},{6,7},{7,6},{8,9},{9,8},{10,11... | collective-permute-start | bytes 1966088 | tf_op jit(solution)/shard_map/ppermute | solution.py:325
  80.1 13.0 %solve.1 = (f32[1024,512]{1,0:T(8,128)}, f32[10,1,256,512]{3,2,1,0:T(8,128)}) custom-call(s32[33]{0:T(128)S(1)} %concatenate.14.place, f32[8,256,128]{2,1,0:T(8,128)} %constant_dynamic-update-slice_fusion.refs_0_, f32[8,256,128]{2,1,0:T(8,128)} %collective-permute-done.9.refs_1_, f32[8,256,128]{2,1,0:T(8,128)} %collective-permute-done.10.refs_2_, ...), custom_call_target="tpu_custom_call" | custom-call | flops 16106127360 | bytes 8388608 | tf_op jit(solution)/shard_map/solve/pallas_call | solution.py:148
  93.8 9.9 %collective-permute-done.18.refs_2_ = f32[4,256,128]{2,1,0:T(8,128)S(1)} collective-permute-done((f32[4,256,128]{2,1,0:T(8,128)S(1)}, f32[4,256,128]{2,1,0:T(8,128)S(1)}, u32[]{:S(2)}, u32[]{:S(2)}) %collective-permute-start.18) | collective-permute-done | bytes 524320 | tf_op jit(solution)/shard_map/ppermute | solution.py:328
  103.8 1.6 %collective-permute-start.22 = (f32[4,256,128]{2,1,0:T(8,128)S(1)}, f32[4,256,128]{2,1,0:T(8,128)S(1)}, u32[]{:S(2)}, u32[]{:S(2)}) collective-permute-start(f32[4,256,128]{2,1,0:T(8,128)S(1)} %slice_select_fusion), channel_id=1, source_target_pairs={{0,1},{1,0},{2,3},{3,2},{4,5},{5,4},{6,7},{7,6},{8,9},{9,8},{10,11... | collective-permute-start | bytes 1572872 | tf_op jit(solution)/shard_map/ppermute | solution.py:325
  105.4 9.7 %update_first.1.acc_ref = f32[9,256,512]{2,1,0:T(8,128)S(1)} custom-call(s32[5]{0:T(128)S(1)} %stack.69.place, f32[1024,512]{1,0:T(8,128)} %get-tuple-element.20.y_ref, f32[10,1,256,512]{3,2,1,0:T(8,128)} %base_ref.1, f32[9,256,128]{2,1,0:T(8,128)S(1)} %slice_bitcast_fusion.refs_0_, f32[9,256,128]{2,1,0:T(8,128)} %collective-permute-done.7.refs_1_, ...), custom_call_target="tpu_custom_call" | custom-call | flops 4529848320 | bytes 15335424 | tf_op jit(solution)/shard_map/update_first/pallas_call | solution.py:210
  117.6 5.7 %update_last.1 = f32[10,1,256,512]{3,2,1,0:T(8,128)} custom-call(s32[3]{0:T(128)S(1)} %pad_add_fusion.place, f32[1024,512]{1,0:T(8,128)} %get-tuple-element.20.y_ref, f32[9,256,512]{2,1,0:T(8,128)S(1)} %update_first.1.acc_ref, f32[9,256,128]{2,1,0:T(8,128)S(1)} %collective-permute-done.8.refs_0_, ...), custom_call_target="tpu_custom_call", output_to_operand_aliasing={{}: (10, {})} | custom-call | flops 2717908992 | bytes 12976128 | tf_op jit(solution)/shard_map/update_last/pallas_call | solution.py:262
  (55 shorter events, 16.9 us)
Async XLA Ops:
  1.0 8.7 %collective-permute-start = (f32[1,256,128]{2,1,0:T(8,128)S(1)}, f32[1,256,128]{2,1,0:T(8,128)S(1)}, u32[]{:S(2)}, u32[]{:S(2)}) collective-permute-start(f32[1,256,128]{2,1,0:T(8,128)S(1)} %slice_bitcast_fusion.4), channel_id=1, source_target_pairs={{0,2},{1,3},{2,0},{3,1},{4,6},{5,7},{6,4},{7,5},{8,10},{9,11},{10,... | collective-permute-start | bytes 393224 | tf_op jit(solution)/shard_map/ppermute | solution.py:325
  4.1 12.9 %collective-permute-start.1 = (f32[1,256,128]{2,1,0:T(8,128)S(1)}, f32[1,256,128]{2,1,0:T(8,128)S(1)}, u32[]{:S(2)}, u32[]{:S(2)}) collective-permute-start(f32[1,256,128]{2,1,0:T(8,128)S(1)} %slice_bitcast_fusion.4), channel_id=1, source_target_pairs={{0,4},{1,5},{2,6},{3,7},{4,0},{5,1},{6,2},{7,3},{8,12},{9,13},{10,... | collective-permute-start | bytes 393224 | tf_op jit(solution)/shard_map/ppermute | solution.py:325
  6.7 10.4 %collective-permute-start.2 = (f32[1,256,128]{2,1,0:T(8,128)S(1)}, f32[1,256,128]{2,1,0:T(8,128)S(1)}, u32[]{:S(2)}, u32[]{:S(2)}) collective-permute-start(f32[1,256,128]{2,1,0:T(8,128)S(1)} %slice_bitcast_fusion.4), channel_id=1, source_target_pairs={{0,6},{1,7},{2,4},{3,5},{4,2},{5,3},{6,0},{7,1},{8,14},{9,15},{10,... | collective-permute-start | bytes 393224 | tf_op jit(solution)/shard_map/ppermute | solution.py:325
  7.8 26.8 %collective-permute-start.14 = (f32[4,256,128]{2,1,0:T(8,128)S(1)}, f32[4,256,128]{2,1,0:T(8,128)S(1)}, u32[]{:S(2)}, u32[]{:S(2)}) collective-permute-start(f32[4,256,128]{2,1,0:T(8,128)S(1)} %slice_bitcast_fusion.2), channel_id=1, source_target_pairs={{0,1},{1,0},{2,3},{3,2},{4,5},{5,4},{6,7},{7,6},{8,9},{9,8},{10,11... | collective-permute-start | bytes 1572872 | tf_op jit(solution)/shard_map/ppermute | solution.py:325
  9.7 26.5 %collective-permute-start.5 = (f32[9,256,128]{2,1,0:T(8,128)S(1)}, f32[9,256,128]{2,1,0:T(8,128)S(1)}, u32[]{:S(2)}, u32[]{:S(2)}) collective-permute-start(f32[9,256,128]{2,1,0:T(8,128)S(1)} %slice_bitcast_fusion.refs_0_), channel_id=1, source_target_pairs={{2,4},{3,5},{4,2},{5,3},{10,12},{11,13},{12,10},{13,11},{18,20},{1... | collective-permute-start | bytes 3538952 | tf_op jit(solution)/shard_map/ppermute | solution.py:328
  10.4 30.9 %collective-permute-start.7 = (f32[9,256,128]{2,1,0:T(8,128)S(1)}, f32[9,256,128]{2,1,0:T(8,128)}, u32[]{:S(2)}, u32[]{:S(2)}) collective-permute-start(f32[9,256,128]{2,1,0:T(8,128)S(1)} %slice_bitcast_fusion.refs_0_), channel_id=1, source_target_pairs={{0,2},{1,3},{2,0},{3,1},{4,6},{5,7},{6,4},{7,5},{8,10},{9,11},{10,... | collective-permute-start | bytes 3538952 | tf_op jit(solution)/shard_map/ppermute | solution.py:325
  17.1 15.1 %collective-permute-start.3 = (f32[4,256,128]{2,1,0:T(8,128)S(1)}, f32[4,256,128]{2,1,0:T(8,128)S(1)}, u32[]{:S(2)}, u32[]{:S(2)}) collective-permute-start(f32[4,256,128]{2,1,0:T(8,128)S(1)} %pad_maximum_fusion), channel_id=1, source_target_pairs={{0,1},{1,0},{2,3},{3,2},{4,5},{5,4},{6,7},{7,6},{8,9},{9,8},{10,11... | collective-permute-start | bytes 1572872 | tf_op jit(solution)/shard_map/ppermute | solution.py:325
  20.6 12.5 %collective-permute-start.4 = (f32[256,512]{1,0:T(8,128)}, f32[256,512]{1,0:T(8,128)}, u32[]{:S(2)}, u32[]{:S(2)}) collective-permute-start(f32[256,512]{1,0:T(8,128)} %slice_bitcast_fusion.3.refs_4_), channel_id=1, source_target_pairs={{0,16},{8,24},{16,0},{24,8},{1,17},{9,25},{17,1},{25,9},{2,18},{10... | collective-permute-start | bytes 1572872 | tf_op jit(solution)/shard_map/ppermute | solution.py:289
  33.0 23.8 %collective-permute-start.9 = (f32[8,256,128]{2,1,0:T(8,128)}, f32[8,256,128]{2,1,0:T(8,128)}, u32[]{:S(2)}, u32[]{:S(2)}) collective-permute-start(f32[8,256,128]{2,1,0:T(8,128)} %constant_dynamic-update-slice_fusion.refs_0_), channel_id=1, source_target_pairs={{0,16},{8,24},{16,0},{24,8},{1,17},{9,25},{17,1},{25,9},{2,18},{10... | collective-permute-start | bytes 3145736 | tf_op jit(solution)/shard_map/ppermute | solution.py:289
  34.6 14.7 %collective-permute-start.15 = (f32[5,256,128]{2,1,0:T(8,128)S(1)}, f32[5,256,128]{2,1,0:T(8,128)S(1)}, u32[]{:S(2)}, u32[]{:S(2)}) collective-permute-start(f32[5,256,128]{2,1,0:T(8,128)S(1)} %slice_bitcast_fusion.1), channel_id=1, source_target_pairs={{0,1},{1,0},{2,3},{3,2},{4,5},{5,4},{6,7},{7,6},{8,9},{9,8},{10,11... | collective-permute-start | bytes 1966088 | tf_op jit(solution)/shard_map/ppermute | solution.py:325
  36.2 34.3 %collective-permute-start.6 = (f32[9,256,128]{2,1,0:T(8,128)S(1)}, f32[9,256,128]{2,1,0:T(8,128)S(1)}, u32[]{:S(2)}, u32[]{:S(2)}) collective-permute-start(f32[9,256,128]{2,1,0:T(8,128)S(1)} %collective-permute-done.5.refs_3_), channel_id=1, source_target_pairs={{2,0},{3,1},{4,6},{5,7},{10,8},{11,9},{12,14},{13,15},{18,16},{19,... | collective-permute-start | bytes 3538952 | tf_op jit(solution)/shard_map/ppermute | solution.py:328
  41.3 29.1 %collective-permute-start.8 = (f32[9,256,128]{2,1,0:T(8,128)}, f32[9,256,128]{2,1,0:T(8,128)S(1)}, u32[]{:S(2)}, u32[]{:S(2)}) collective-permute-start(f32[9,256,128]{2,1,0:T(8,128)} %collective-permute-done.7.refs_1_), channel_id=1, source_target_pairs={{2,4},{3,5},{4,2},{5,3},{10,12},{11,13},{12,10},{13,11},{18,20},{1... | collective-permute-start | bytes 3538952 | tf_op jit(solution)/shard_map/ppermute | solution.py:328
  50.4 25.3 %collective-permute-start.16 = (f32[9,256,128]{2,1,0:T(8,128)}, f32[9,256,128]{2,1,0:T(8,128)}, u32[]{:S(2)}, u32[]{:S(2)}) collective-permute-start(f32[9,256,128]{2,1,0:T(8,128)} %collective-permute-done.7.refs_1_), channel_id=1, source_target_pairs={{0,1},{1,0},{2,3},{3,2},{4,5},{5,4},{6,7},{7,6},{8,9},{9,8},{10,11... | collective-permute-start | bytes 3538952 | tf_op jit(solution)/shard_map/ppermute | solution.py:325
  51.9 28.2 %collective-permute-start.10 = (f32[8,256,128]{2,1,0:T(8,128)}, f32[8,256,128]{2,1,0:T(8,128)}, u32[]{:S(2)}, u32[]{:S(2)}) collective-permute-start(f32[8,256,128]{2,1,0:T(8,128)} %constant_dynamic-update-slice_fusion.refs_0_), channel_id=1, source_target_pairs={{0,8},{8,0},{16,24},{24,16},{1,9},{9,1},{17,25},{25,17},{2,10},{10... | collective-permute-start | bytes 3145736 | tf_op jit(solution)/shard_map/ppermute | solution.py:289
  56.9 23.3 %collective-permute-start.11 = (f32[8,256,128]{2,1,0:T(8,128)}, f32[8,256,128]{2,1,0:T(8,128)}, u32[]{:S(2)}, u32[]{:S(2)}) collective-permute-start(f32[8,256,128]{2,1,0:T(8,128)} %collective-permute-done.9.refs_1_), channel_id=1, source_target_pairs={{0,8},{8,0},{16,24},{24,16},{1,9},{9,1},{17,25},{25,17},{2,10},{10... | collective-permute-start | bytes 3145736 | tf_op jit(solution)/shard_map/ppermute | solution.py:289
  70.5 6.6 %collective-permute-start.12 = (f32[256,512]{1,0:T(8,128)}, f32[256,512]{1,0:T(8,128)}, u32[]{:S(2)}, u32[]{:S(2)}) collective-permute-start(f32[256,512]{1,0:T(8,128)} %slice_bitcast_fusion.3.refs_4_), channel_id=1, source_target_pairs={{0,8},{8,0},{16,24},{24,16},{1,9},{9,1},{17,25},{25,17},{2,10},{10... | collective-permute-start | bytes 1572872 | tf_op jit(solution)/shard_map/ppermute | solution.py:289
  71.5 7.0 %collective-permute-start.13 = (f32[256,512]{1,0:T(8,128)}, f32[256,512]{1,0:T(8,128)}, u32[]{:S(2)}, u32[]{:S(2)}) collective-permute-start(f32[256,512]{1,0:T(8,128)} %collective-permute-done.4.refs_5_), channel_id=1, source_target_pairs={{0,8},{8,0},{16,24},{24,16},{1,9},{9,1},{17,25},{25,17},{2,10},{10... | collective-permute-start | bytes 1572872 | tf_op jit(solution)/shard_map/ppermute | solution.py:289
  75.7 39.4 %collective-permute-start.17 = (f32[5,256,128]{2,1,0:T(8,128)S(1)}, f32[5,256,128]{2,1,0:T(8,128)S(1)}, u32[]{:S(2)}, u32[]{:S(2)}) collective-permute-start(f32[5,256,128]{2,1,0:T(8,128)S(1)} %slice.61), channel_id=1, source_target_pairs={{2,0},{3,1},{4,6},{5,7},{10,8},{11,9},{12,14},{13,15},{18,16},{19,... | collective-permute-start | bytes 1966088 | tf_op jit(solution)/shard_map/ppermute | solution.py:328
  77.0 26.7 %collective-permute-start.18 = (f32[4,256,128]{2,1,0:T(8,128)S(1)}, f32[4,256,128]{2,1,0:T(8,128)S(1)}, u32[]{:S(2)}, u32[]{:S(2)}) collective-permute-start(f32[4,256,128]{2,1,0:T(8,128)S(1)} %slice.62), channel_id=1, source_target_pairs={{2,0},{3,1},{4,6},{5,7},{10,8},{11,9},{12,14},{13,15},{18,16},{19,... | collective-permute-start | bytes 1572872 | tf_op jit(solution)/shard_map/ppermute | solution.py:328
  78.5 25.2 %collective-permute-start.19 = (f32[5,256,128]{2,1,0:T(8,128)S(1)}, f32[5,256,128]{2,1,0:T(8,128)S(1)}, u32[]{:S(2)}, u32[]{:S(2)}) collective-permute-start(f32[5,256,128]{2,1,0:T(8,128)S(1)} %slice.63), channel_id=1, source_target_pairs={{0,1},{1,0},{2,3},{3,2},{4,5},{5,4},{6,7},{7,6},{8,9},{9,8},{10,11... | collective-permute-start | bytes 1966088 | tf_op jit(solution)/shard_map/ppermute | solution.py:325
  93.2 12.3 %copy-start.1 = (f32[9,256,128]{2,1,0:T(8,128)S(1)}, f32[9,256,128]{2,1,0:T(8,128)}, u32[]{:S(2)}) copy-start(f32[9,256,128]{2,1,0:T(8,128)} %copy-done) | copy-start | bytes 3538948
  93.2 21.9 %collective-permute-start.20 = (f32[4,256,128]{2,1,0:T(8,128)S(1)}, f32[4,256,128]{2,1,0:T(8,128)S(1)}, u32[]{:S(2)}, u32[]{:S(2)}) collective-permute-start(f32[4,256,128]{2,1,0:T(8,128)S(1)} %slice.64), channel_id=1, source_target_pairs={{0,1},{1,0},{2,3},{3,2},{4,5},{5,4},{6,7},{7,6},{8,9},{9,8},{10,11... | collective-permute-start | bytes 1572872 | tf_op jit(solution)/shard_map/ppermute | solution.py:325
  103.7 13.9 %collective-permute-start.21 = (f32[5,256,128]{2,1,0:T(8,128)S(1)}, f32[5,256,128]{2,1,0:T(8,128)S(1)}, u32[]{:S(2)}, u32[]{:S(2)}) collective-permute-start(f32[5,256,128]{2,1,0:T(8,128)S(1)} %collective-permute-done.19.refs_3_), channel_id=1, source_target_pairs={{0,2},{1,3},{2,0},{3,1},{4,6},{5,7},{6,4},{7,5},{8,10},{9,11},{10,... | collective-permute-start | bytes 1966088 | tf_op jit(solution)/shard_map/ppermute | solution.py:325
  103.8 12.4 %collective-permute-start.22 = (f32[4,256,128]{2,1,0:T(8,128)S(1)}, f32[4,256,128]{2,1,0:T(8,128)S(1)}, u32[]{:S(2)}, u32[]{:S(2)}) collective-permute-start(f32[4,256,128]{2,1,0:T(8,128)S(1)} %slice_select_fusion), channel_id=1, source_target_pairs={{0,1},{1,0},{2,3},{3,2},{4,5},{5,4},{6,7},{7,6},{8,9},{9,8},{10,11... | collective-permute-start | bytes 1572872 | tf_op jit(solution)/shard_map/ppermute | solution.py:325
  (3 other events, 11.7 us)
